TPU v7x, 512 devices: a whole 4x8x8 slice. The times are simulated.
512 devices in a mesh: gx: 32 (over z, x), gy: 16 (over y, core).
Axes of the slice: x: 4, y: 8, z: 8, core: 2. Of those that a mesh axis runs over, the one named last changes fastest.
Arguments:
- initial: bfloat16 [32, 16, 384, 512], P('gx', 'gy'), may hold values from -500 to 500
- couplings: bfloat16 [32, 16, 5, 384, 384], P('gx', 'gy'), may hold values from -0.125 to 0.125
- frequencies: float32 [32, 16, 384], P('gx', 'gy'), may hold values from 0.5 to 2
- linked: int32 [32, 16, 4], P('gx', 'gy'), may hold values from 0 to 1, as said below
Outputs:
- orthonormal: bfloat16 [32, 16, 384, 512], P('gx', 'gy')
- diag_scale: float32 [512], replicated
Inputs may be any that keep to these rules, and one draw needn't show every extreme that they name: `linked`: 1 where the coupling block toward that neighbour is present, else 0.
All inputs are finite; a program needn't handle non-finite values.
Results may differ from a plain program's by a relative error of at most 0.0046.
The roundings to bfloat16 on the way count: a program that leaves them out, or rounds other values in their place, can miss the bound.
Values may be sent and summed in bfloat16 or wider, within the bound.
No kernel may reach another device: no remote copies, remote signals or barrier semaphores. Data moves between devices by JAX's collectives and lax.ppermute only.
A program may use at most 64 MiB of HBM per device.

v0:
```python
import math

import jax
import jax.numpy as jnp
from jax import lax
from jax.sharding import PartitionSpec as P

DEGREE = 3


spectrum_center = 1.25
spectrum_scale = 0.5


def extended(cells, sides, width):
    for axis, dim in sides:
        count = lax.axis_size(axis)
        ends = count - 1
        head = lax.slice_in_dim(cells, 0, width, axis=dim)
        tail = lax.slice_in_dim(cells, cells.shape[dim] - width, cells.shape[dim], axis=dim)
        cells = jnp.concatenate(
            [
                lax.ppermute(tail, axis, [(i, (i + 1) % count) for i in range(ends)]),
                cells,
                lax.ppermute(head, axis, [((i + 1) % count, i) for i in range(ends)]),
            ],
            axis=dim,
        )
    return cells


def operate(field, couplings, frequencies, linked):
    padded = extended(field, (("gx", 0), ("gy", 1)), 1)
    middle = padded[1, 1:-1]
    sources = (padded[0, 1:-1], padded[2, 1:-1], padded[1, :-2], padded[1, 2:])
    blocks = couplings[0]
    present = linked[0].astype(jnp.float32)
    summed = frequencies[0][..., None] * middle.astype(jnp.float32)
    summed = summed + jnp.einsum(
        "bij,bjk->bik", blocks[:, 0], middle, preferred_element_type=jnp.float32
    )
    for direction in range(4):
        product = jnp.einsum(
            "bij,bjk->bik",
            blocks[:, direction + 1],
            sources[direction],
            preferred_element_type=jnp.float32,
        )
        summed = summed + present[:, direction, None, None] * product
    return summed[None]


def local(initial, couplings, frequencies, linked):
    previous = initial.astype(jnp.float32)
    current = spectrum_scale * (
        operate(initial, couplings, frequencies, linked) - spectrum_center * previous
    )
    for degree_step in range(DEGREE - 1):
        rounded = current.astype(jnp.bfloat16)
        following = (
            2.0
            * spectrum_scale
            * (
                operate(rounded, couplings, frequencies, linked)
                - spectrum_center * rounded.astype(jnp.float32)
            )
            - previous
        )
        previous, current = (current, following)
    width = current.shape[3]
    matrix_rows = current.reshape(-1, width)
    local_correlation = jnp.dot(
        matrix_rows.T,
        matrix_rows,
        precision=lax.Precision.HIGHEST,
        preferred_element_type=jnp.float32,
    )
    correlation = lax.psum(local_correlation, ("gx", "gy"))
    factor = jnp.linalg.cholesky(correlation)
    inverse = jax.scipy.linalg.solve_triangular(
        factor, jnp.eye(width, dtype=jnp.float32), lower=True
    )
    total_rows = matrix_rows.shape[0] * lax.axis_size("gx") * lax.axis_size("gy")
    root = math.sqrt(total_rows)
    orthonormal = (
        jnp.dot(
            matrix_rows,
            inverse.T,
            precision=lax.Precision.HIGHEST,
            preferred_element_type=jnp.float32,
        )
        * root
    ).astype(jnp.bfloat16)
    diag_scale = jnp.diagonal(factor) / root
    return (orthonormal.reshape(current.shape), diag_scale)


def solution(mesh):
    in_specs = (
        P("gx", "gy", None, None),
        P("gx", "gy", None, None, None),
        P("gx", "gy", None),
        P("gx", "gy", None),
    )
    out_specs = (P("gx", "gy", None, None), P())
    return jax.shard_map(local, mesh=mesh, in_specs=in_specs, out_specs=out_specs, check_vma=False)
```

profile of v0, /device:TPU:1, one launch (start us, length us, event | category | flops | bytes accessed | tf_op | source)
XLA Modules:
  0.0 574.4 jit_solution(8953993733090544318)
XLA Ops:
  7.3 4.1 collective-permute-start
  11.4 1.3 collective-permute-start.1
  12.7 3.7 collective-permute-done
  16.4 0.8 constant_dynamic-update-slice_fusion.2
  17.1 1.8 constant_dynamic-update-slice_fusion.1
  18.9 1.2 collective-permute-done.1
  20.1 0.8 constant_dynamic-update-slice_fusion
  20.9 7.3 %collective-permute-start.3 = (bf16[3,1,384,512]{3,2,1,0:T(8,128)(2,1)}, bf16[3,1,384,512]{3,2,1,0:T(8,128)(2,1)}, u32[]{:S(2)}, u32[]{:S(2)}) collective-permute-start(bf16[3,1,384,512]{3,2,1,0:T(8,128)(2,1)} %constant_dynamic-update-slice_fusion), channel_id=1, source_target_pairs={{1,0},{2,1},{3,2},{4,3},{5,4},{6,5},{7,6},{8,7},{9,8},{10,9},{11,1... | collective-permute-start | bytes 3538952 | tf_op jit(solution)/shard_map/ppermute | solution.py:25
  28.1 2.6 collective-permute-start.2
  31.9 0.9 convolution_multiply_fusion.11
  32.8 10.2 %collective-permute-done.3 = bf16[3,1,384,512]{3,2,1,0:T(8,128)(2,1)} collective-permute-done((bf16[3,1,384,512]{3,2,1,0:T(8,128)(2,1)}, bf16[3,1,384,512]{3,2,1,0:T(8,128)(2,1)}, u32[]{:S(2)}, u32[]{:S(2)}) %collective-permute-start.3) | collective-permute-done | bytes 1179680 | tf_op jit(solution)/shard_map/ppermute | solution.py:25
  43.0 2.0 fusion.8
  45.1 2.0 fusion.9
  47.1 1.2 fusion.88
  48.3 3.1 collective-permute-start.4
  51.4 1.3 collective-permute-start.5
  52.7 3.4 collective-permute-done.4
  56.1 3.8 collective-permute-done.5
  60.1 8.3 %collective-permute-start.6 = (bf16[3,1,384,512]{3,2,1,0:T(8,128)(2,1)S(1)}, bf16[3,1,384,512]{3,2,1,0:T(8,128)(2,1)S(1)}, u32[]{:S(2)}, u32[]{:S(2)}) collective-permute-start(bf16[3,1,384,512]{3,2,1,0:T(8,128)(2,1)S(1)} %pad_maximum_fusion), channel_id=1, source_target_pairs={{0,1},{1,2},{2,3},{3,4},{4,5},{5,6},{6,7},{7,8},{8,9},{9,10},{10,1... | collective-permute-start | bytes 3538952 | tf_op jit(solution)/shard_map/ppermute | solution.py:23
  68.4 1.9 collective-permute-start.7
  70.7 0.9 fusion.6
  71.6 9.9 %collective-permute-done.6 = bf16[3,1,384,512]{3,2,1,0:T(8,128)(2,1)S(1)} collective-permute-done((bf16[3,1,384,512]{3,2,1,0:T(8,128)(2,1)S(1)}, bf16[3,1,384,512]{3,2,1,0:T(8,128)(2,1)S(1)}, u32[]{:S(2)}, u32[]{:S(2)}) %collective-permute-start.6) | collective-permute-done | bytes 1179680 | tf_op jit(solution)/shard_map/ppermute | solution.py:23
  81.5 1.0 fusion.5
  82.5 3.4 collective-permute-done.7
  85.9 1.0 fusion.4
  86.9 1.2 fusion.34
  88.1 5.8 %collective-permute-start.8 = (bf16[1,1,384,512]{3,2,1,0:T(8,128)(2,1)S(1)}, bf16[1,1,384,512]{3,2,1,0:T(8,128)(2,1)S(1)}, u32[]{:S(2)}, u32[]{:S(2)}) collective-permute-start(bf16[1,1,384,512]{3,2,1,0:T(8,128)(2,1)S(1)} %fusion.34), channel_id=1, source_target_pairs={{0,16},{16,32},{32,48},{48,64},{64,80},{80,96},{96,112},{112,128},... | collective-permute-start | bytes 1179656 | tf_op jit(solution)/shard_map/ppermute | solution.py:23
  93.9 1.3 collective-permute-start.9
  95.2 3.4 collective-permute-done.8
  98.6 3.8 collective-permute-done.9
  102.6 6.6 %collective-permute-start.10 = (bf16[3,1,384,512]{3,2,1,0:T(8,128)(2,1)S(1)}, bf16[3,1,384,512]{3,2,1,0:T(8,128)(2,1)S(1)}, u32[]{:S(2)}, u32[]{:S(2)}) collective-permute-start(bf16[3,1,384,512]{3,2,1,0:T(8,128)(2,1)S(1)} %pad_maximum_fusion.1), channel_id=1, source_target_pairs={{0,1},{1,2},{2,3},{3,4},{4,5},{5,6},{6,7},{7,8},{8,9},{9,10},{10,1... | collective-permute-start | bytes 3538952 | tf_op jit(solution)/shard_map/ppermute | solution.py:23
  109.1 2.4 collective-permute-start.11
  111.9 0.9 fusion.2
  112.8 9.4 %collective-permute-done.10 = bf16[3,1,384,512]{3,2,1,0:T(8,128)(2,1)S(1)} collective-permute-done((bf16[3,1,384,512]{3,2,1,0:T(8,128)(2,1)S(1)}, bf16[3,1,384,512]{3,2,1,0:T(8,128)(2,1)S(1)}, u32[]{:S(2)}, u32[]{:S(2)}) %collective-permute-start.10) | collective-permute-done | bytes 1179680 | tf_op jit(solution)/shard_map/ppermute | solution.py:23
  122.3 1.0 fusion.1
  123.3 3.4 collective-permute-done.11
  126.7 1.0 fusion
  127.7 1.2 fusion.29
  128.9 2.9 fusion.89
  131.9 1.1 fusion.63
  133.0 279.7 %all-reduce.3.cloned.1.call-done = f32[512,512]{0,1:T(8,128)} async-done(((f32[512,512]{0,1:T(8,128)}), f32[512,512]{0,1:T(8,128)}) %all-reduce.3.cloned.1.call-update) | async-done | bytes 1048592 | tf_op jit(solution)/shard_map/psum | solution.py:78
  412.6 1.6 copy.33
  414.5 1.0 copy-done.4
  415.6 11.7 %cholesky.104 = f32[128,128]{1,0:T(8,128)S(1)} custom-call(f32[128,128]{1,0:T(8,128)S(1)} %cholesky.266), custom_call_target="Cholesky" | custom-call | tf_op jit(solution)/shard_map/jit(cholesky)/cholesky | solution.py:79
  427.4 9.8 %custom-call.31 = f32[1,128,128]{1,2,0:T(8,128)S(1)} custom-call(f32[1,128,128]{2,1,0:T(8,128)S(1)} %get-tuple-element.31), custom_call_target="InvertDiagBlocksLowerTriangular" | custom-call | tf_op jit(solution)/shard_map/jit(cholesky)/cholesky | solution.py:79
  437.9 11.9 %cholesky.217 = f32[128,128]{1,0:T(8,128)S(1)} custom-call(f32[128,128]{1,0:T(8,128)S(1)} %cholesky.270), custom_call_target="Cholesky" | custom-call | tf_op jit(solution)/shard_map/jit(cholesky)/cholesky | solution.py:79
  449.8 9.8 %custom-call.32 = f32[1,128,128]{1,2,0:T(8,128)S(1)} custom-call(f32[1,128,128]{2,1,0:T(8,128)S(1)} %get-tuple-element.28), custom_call_target="InvertDiagBlocksLowerTriangular" | custom-call | tf_op jit(solution)/shard_map/jit(cholesky)/cholesky | solution.py:79
  460.3 11.7 %cholesky.238 = f32[128,128]{1,0:T(8,128)S(1)} custom-call(f32[128,128]{1,0:T(8,128)S(1)} %cholesky.275), custom_call_target="Cholesky" | custom-call | tf_op jit(solution)/shard_map/jit(cholesky)/cholesky | solution.py:79
  472.1 0.7 compare_reduce_fusion.1
  472.8 9.8 %custom-call.33 = f32[1,128,128]{1,2,0:T(8,128)S(1)} custom-call(f32[1,128,128]{2,1,0:T(8,128)S(1)} %get-tuple-element.25), custom_call_target="InvertDiagBlocksLowerTriangular" | custom-call | tf_op jit(solution)/shard_map/jit(cholesky)/cholesky | solution.py:79
  483.2 11.9 %cholesky.255 = f32[128,128]{1,0:T(8,128)S(1)} custom-call(f32[128,128]{1,0:T(8,128)S(1)} %convolution_subtract_fusion.5), custom_call_target="Cholesky" | custom-call | tf_op jit(solution)/shard_map/jit(cholesky)/cholesky | solution.py:79
  495.2 0.7 compare_reduce_fusion
  499.1 1.3 fusion.45
  500.4 13.6 %while.1 = (s32[]{:T(128)}, f32[512,512]{1,0:T(8,128)}, s32[4,2]{0,1:T(2,128)S(1)}, f32[4,128,128]{2,1,0:T(8,128)}, s32[]{:T(128)}) while((s32[]{:T(128)}, f32[512,512]{1,0:T(8,128)}, s32[4,2]{0,1:T(2,128)S(1)}, f32[4,128,128]{2,1,0:T(8,128)}, s32[]{:T(128)}) %tuple.36), condition=%wide.while_cond, body=%wide.while_body.sunk | while | flops 2 | bytes 132705 | solution.py:80
  501.0 2.8 bitcast_dynamic-update-slice_fusion.2
  504.4 2.8 bitcast_dynamic-update-slice_fusion.2
  507.8 2.8 bitcast_dynamic-update-slice_fusion.2
  511.3 2.8 bitcast_dynamic-update-slice_fusion.2
  514.0 40.1 %custom-call.34 = f32[4,128,128]{1,2,0:T(8,128)S(1)} custom-call(f32[4,128,128]{2,1,0:T(8,128)} %get-tuple-element.9), custom_call_target="InvertDiagBlocksLowerTriangular" | custom-call | tf_op jit(solution)/shard_map/jit(_solve_triangular)/triangular_solve | solution.py:80
  554.5 1.4 convolution_subtract_fusion.1
  556.3 1.3 convolution_subtract_fusion
  558.0 1.6 convolution_subtract_fusion.2
  560.0 2.2 fusion.36
  562.2 4.5 gather_fusion
  (60 shorter events, 9.9 us)
Async XLA Ops:
  7.2 24.3 %copy-start.1 = (bf16[1,1,384,512]{3,2,1,0:T(8,128)(2,1)S(1)}, bf16[1,1,384,512]{3,2,1,0:T(8,128)(2,1)}, u32[]{:S(2)}) copy-start(bf16[1,1,384,512]{3,2,1,0:T(8,128)(2,1)} %param.4) | copy-start | bytes 1179652
  7.2 23.6 %copy-start.6 = (f32[1,1,384]{2,1,0:T(1,128)S(1)}, f32[1,1,384]{2,1,0:T(1,128)}, u32[]{:S(2)}) copy-start(f32[1,1,384]{2,1,0:T(1,128)} %param.6) | copy-start | bytes 4612
  7.2 23.6 %copy-start.7 = (s32[1,1,4]{2,1,0:T(1,128)S(1)}, s32[1,1,4]{2,1,0:T(1,128)}, u32[]{:S(2)}) copy-start(s32[1,1,4]{2,1,0:T(1,128)} %param.7) | copy-start | bytes 52
  7.2 24.3 %copy-start = (bf16[1,1,5,384,384]{4,3,2,1,0:T(8,128)(2,1)S(1)}, bf16[1,1,5,384,384]{4,3,2,1,0:T(8,128)(2,1)}, u32[]{:S(2)}) copy-start(bf16[1,1,5,384,384]{4,3,2,1,0:T(8,128)(2,1)} %param.5) | copy-start | bytes 4423684
  7.2 405.4 %all-reduce.3.cloned.1.call-start = ((), (), s32[]{:S(2)}) async-start(), calls=%async_computation | async-start | bytes 2097152 | tf_op jit(solution)/shard_map/psum | solution.py:78
  7.3 9.1 %collective-permute-start = (bf16[1,1,384,512]{3,2,1,0:T(8,128)(2,1)}, bf16[1,1,384,512]{3,2,1,0:T(8,128)(2,1)S(1)}, u32[]{:S(2)}, u32[]{:S(2)}) collective-permute-start(bf16[1,1,384,512]{3,2,1,0:T(8,128)(2,1)} %param.4), channel_id=1, source_target_pairs={{0,16},{16,32},{32,48},{48,64},{64,80},{80,96},{96,112},{112,128},... | collective-permute-start | bytes 1179656 | tf_op jit(solution)/shard_map/ppermute | solution.py:23
  11.4 8.7 %collective-permute-start.1 = (bf16[1,1,384,512]{3,2,1,0:T(8,128)(2,1)}, bf16[1,1,384,512]{3,2,1,0:T(8,128)(2,1)S(1)}, u32[]{:S(2)}, u32[]{:S(2)}) collective-permute-start(bf16[1,1,384,512]{3,2,1,0:T(8,128)(2,1)} %param.4), channel_id=1, source_target_pairs={{16,0},{32,16},{48,32},{64,48},{80,64},{96,80},{112,96},{128,112},... | collective-permute-start | bytes 1179656 | tf_op jit(solution)/shard_map/ppermute | solution.py:25
  20.9 22.2 %collective-permute-start.3 = (bf16[3,1,384,512]{3,2,1,0:T(8,128)(2,1)}, bf16[3,1,384,512]{3,2,1,0:T(8,128)(2,1)}, u32[]{:S(2)}, u32[]{:S(2)}) collective-permute-start(bf16[3,1,384,512]{3,2,1,0:T(8,128)(2,1)} %constant_dynamic-update-slice_fusion), channel_id=1, source_target_pairs={{1,0},{2,1},{3,2},{4,3},{5,4},{6,5},{7,6},{8,7},{9,8},{10,9},{11,1... | collective-permute-start | bytes 3538952 | tf_op jit(solution)/shard_map/ppermute | solution.py:25
  28.1 16.9 %collective-permute-start.2 = (bf16[3,1,384,512]{3,2,1,0:T(8,128)(2,1)}, bf16[3,1,384,512]{3,2,1,0:T(8,128)(2,1)}, u32[]{:S(2)}, u32[]{:S(2)}) collective-permute-start(bf16[3,1,384,512]{3,2,1,0:T(8,128)(2,1)} %constant_dynamic-update-slice_fusion), channel_id=1, source_target_pairs={{0,1},{1,2},{2,3},{3,4},{4,5},{5,6},{6,7},{7,8},{8,9},{9,10},{10,1... | collective-permute-start | bytes 3538952 | tf_op jit(solution)/shard_map/ppermute | solution.py:23
  48.3 7.8 %collective-permute-start.4 = (bf16[1,1,384,512]{3,2,1,0:T(8,128)(2,1)S(1)}, bf16[1,1,384,512]{3,2,1,0:T(8,128)(2,1)S(1)}, u32[]{:S(2)}, u32[]{:S(2)}) collective-permute-start(bf16[1,1,384,512]{3,2,1,0:T(8,128)(2,1)S(1)} %get-tuple-element.36), channel_id=1, source_target_pairs={{0,16},{16,32},{32,48},{48,64},{64,80},{80,96},{96,112},{112,128},... | collective-permute-start | bytes 1179656 | tf_op jit(solution)/shard_map/ppermute | solution.py:23
  51.4 8.5 %collective-permute-start.5 = (bf16[1,1,384,512]{3,2,1,0:T(8,128)(2,1)S(1)}, bf16[1,1,384,512]{3,2,1,0:T(8,128)(2,1)S(1)}, u32[]{:S(2)}, u32[]{:S(2)}) collective-permute-start(bf16[1,1,384,512]{3,2,1,0:T(8,128)(2,1)S(1)} %get-tuple-element.36), channel_id=1, source_target_pairs={{16,0},{32,16},{48,32},{64,48},{80,64},{96,80},{112,96},{128,112},... | collective-permute-start | bytes 1179656 | tf_op jit(solution)/shard_map/ppermute | solution.py:25
  60.1 21.4 %collective-permute-start.6 = (bf16[3,1,384,512]{3,2,1,0:T(8,128)(2,1)S(1)}, bf16[3,1,384,512]{3,2,1,0:T(8,128)(2,1)S(1)}, u32[]{:S(2)}, u32[]{:S(2)}) collective-permute-start(bf16[3,1,384,512]{3,2,1,0:T(8,128)(2,1)S(1)} %pad_maximum_fusion), channel_id=1, source_target_pairs={{0,1},{1,2},{2,3},{3,4},{4,5},{5,6},{6,7},{7,8},{8,9},{9,10},{10,1... | collective-permute-start | bytes 3538952 | tf_op jit(solution)/shard_map/ppermute | solution.py:23
  68.4 17.5 %collective-permute-start.7 = (bf16[3,1,384,512]{3,2,1,0:T(8,128)(2,1)S(1)}, bf16[3,1,384,512]{3,2,1,0:T(8,128)(2,1)S(1)}, u32[]{:S(2)}, u32[]{:S(2)}) collective-permute-start(bf16[3,1,384,512]{3,2,1,0:T(8,128)(2,1)S(1)} %pad_maximum_fusion), channel_id=1, source_target_pairs={{1,0},{2,1},{3,2},{4,3},{5,4},{6,5},{7,6},{8,7},{9,8},{10,9},{11,1... | collective-permute-start | bytes 3538952 | tf_op jit(solution)/shard_map/ppermute | solution.py:25
  88.1 10.5 %collective-permute-start.8 = (bf16[1,1,384,512]{3,2,1,0:T(8,128)(2,1)S(1)}, bf16[1,1,384,512]{3,2,1,0:T(8,128)(2,1)S(1)}, u32[]{:S(2)}, u32[]{:S(2)}) collective-permute-start(bf16[1,1,384,512]{3,2,1,0:T(8,128)(2,1)S(1)} %fusion.34), channel_id=1, source_target_pairs={{0,16},{16,32},{32,48},{48,64},{64,80},{80,96},{96,112},{112,128},... | collective-permute-start | bytes 1179656 | tf_op jit(solution)/shard_map/ppermute | solution.py:23
  93.9 8.5 %collective-permute-start.9 = (bf16[1,1,384,512]{3,2,1,0:T(8,128)(2,1)S(1)}, bf16[1,1,384,512]{3,2,1,0:T(8,128)(2,1)S(1)}, u32[]{:S(2)}, u32[]{:S(2)}) collective-permute-start(bf16[1,1,384,512]{3,2,1,0:T(8,128)(2,1)S(1)} %fusion.34), channel_id=1, source_target_pairs={{16,0},{32,16},{48,32},{64,48},{80,64},{96,80},{112,96},{128,112},... | collective-permute-start | bytes 1179656 | tf_op jit(solution)/shard_map/ppermute | solution.py:25
  102.6 19.7 %collective-permute-start.10 = (bf16[3,1,384,512]{3,2,1,0:T(8,128)(2,1)S(1)}, bf16[3,1,384,512]{3,2,1,0:T(8,128)(2,1)S(1)}, u32[]{:S(2)}, u32[]{:S(2)}) collective-permute-start(bf16[3,1,384,512]{3,2,1,0:T(8,128)(2,1)S(1)} %pad_maximum_fusion.1), channel_id=1, source_target_pairs={{0,1},{1,2},{2,3},{3,4},{4,5},{5,6},{6,7},{7,8},{8,9},{9,10},{10,1... | collective-permute-start | bytes 3538952 | tf_op jit(solution)/shard_map/ppermute | solution.py:23
  109.1 17.5 %collective-permute-start.11 = (bf16[3,1,384,512]{3,2,1,0:T(8,128)(2,1)S(1)}, bf16[3,1,384,512]{3,2,1,0:T(8,128)(2,1)S(1)}, u32[]{:S(2)}, u32[]{:S(2)}) collective-permute-start(bf16[3,1,384,512]{3,2,1,0:T(8,128)(2,1)S(1)} %pad_maximum_fusion.1), channel_id=1, source_target_pairs={{1,0},{2,1},{3,2},{4,3},{5,4},{6,5},{7,6},{8,7},{9,8},{10,9},{11,1... | collective-permute-start | bytes 3538952 | tf_op jit(solution)/shard_map/ppermute | solution.py:25
  412.6 1.7 copy-start.2
  414.5 1.0 copy-start.4
  415.5 21.7 %copy-start.5 = (f32[512,512]{1,0:T(8,128)S(1)}, f32[512,512]{1,0:T(8,128)}, u32[]{:S(2)}) copy-start(f32[512,512]{1,0:T(8,128)} %copy-done.4) | copy-start | bytes 3145732
  500.4 55.9 %copy-start.3 = (f32[512,512]{1,0:T(8,128)S(1)}, f32[512,512]{1,0:T(8,128)}, u32[]{:S(2)}) copy-start(f32[512,512]{1,0:T(8,128)} %fusion.63) | copy-start | bytes 3145732
Sparse Core Ops, SparseCore 0:
  131.9 280.6 all-reduce.2
where the time goes:
time: 579 us; the launch traced here: 574 us
  waiting for transfers between devices  335 us (58%)
  other arithmetic  123 us (21%)
  starting transfers between devices  46 us (8%)
  matrix products  28.3 us (5%)
  local copies, waits for them, and re-layouts  24.9 us (4%)
  between operations  17.3 us (3%)
    psum x1, waiting for transfers between devices, local(): correlation = lax.psum(local_correlation, ('gx', 'gy'))  280 us
    another operation x14, other arithmetic, local(): factor = jnp.linalg.cholesky(correlation)  78.9 us
    another operation x3, other arithmetic, local(): jax.scipy.linalg.solve_triangular(factor, jnp.eye(width, dtype=jnp.float3...  41.4 us
    ppermute x6, starting transfers between devices, extended(): lax.ppermute(tail, axis, [(i, (i + 1) % count) for i in range(ends)])  30.5 us
    ppermute x6, waiting for transfers between devices, extended(): lax.ppermute(tail, axis, [(i, (i + 1) % count) for i in range(ends)])  29.7 us
    ppermute x6, waiting for transfers between devices, extended(): lax.ppermute(head, axis, [((i + 1) % count, i) for i in range(ends)])  25.9 us
    ppermute x6, starting transfers between devices, extended(): lax.ppermute(head, axis, [((i + 1) % count, i) for i in range(ends)])  15.5 us
    dot_general x12, matrix products, operate(): jnp.einsum('bij,bjk->bik', blocks[:, direction + 1], sources[direction],...  14.4 us
  transfers between devices with their start and end apart: 13, of which 12 were waited for; matrix products, arithmetic and copies ran while one was open for 2% of the time, Pallas kernels for 0%

commit v1 on v0

v1 whole, which is shorter than its diff:
```python
import functools
import math

import jax
import jax.numpy as jnp
from jax import lax
from jax.experimental import pallas as pl
from jax.experimental.pallas import tpu as pltpu
from jax.sharding import Mesh
from jax.sharding import PartitionSpec as P

CENTER = 1.25
SCALE = 0.5
NB = 128
HIGHEST = lax.Precision.HIGHEST
F32 = jnp.float32
VMEM = pl.BlockSpec(memory_space=pltpu.VMEM)
SMEM = pl.BlockSpec(memory_space=pltpu.SMEM)
GX = ("z", "x")
GY = ("y", "c")
CHIPS = ("z", "x", "y")
N_CHIPS = 256
LIMIT = 40 * 2**20


def dot(a, b, dims, precision=None):
    return lax.dot_general(
        a, b, (dims, ((), ())), precision=precision, preferred_element_type=F32
    )


def self_kernel(v_ref, c_ref, w_ref, o_ref):
    v = v_ref[...]
    o_ref[...] = (w_ref[...] - CENTER) * v.astype(F32) + dot(c_ref[0], v, ((1,), (0,)))


def halo_sum(part_ref, c_ref, l_ref, halos):
    total = part_ref[...]
    for d, h in enumerate(halos):
        total = total + l_ref[d] * dot(c_ref[d + 1], h[...], ((1,), (0,)))
    return total


def first_kernel(part_ref, c_ref, l_ref, h0, h1, h2, h3, o_ref, r_ref):
    out = SCALE * halo_sum(part_ref, c_ref, l_ref, (h0, h1, h2, h3))
    o_ref[...] = out
    r_ref[...] = out.astype(jnp.bfloat16)


def middle_kernel(part_ref, c_ref, l_ref, h0, h1, h2, h3, p_ref, r_ref):
    out = 2.0 * SCALE * halo_sum(part_ref, c_ref, l_ref, (h0, h1, h2, h3)) - p_ref[...].astype(F32)
    r_ref[...] = out.astype(jnp.bfloat16)


def last_kernel(part_ref, c_ref, l_ref, h0, h1, h2, h3, p_ref, core_ref, o_ref, keep_ref, send_ref):
    o_ref[...] = 2.0 * SCALE * halo_sum(part_ref, c_ref, l_ref, (h0, h1, h2, h3)) - p_ref[...]
    n = 0
    for i in range(4):
        left = o_ref[:, i * NB : (i + 1) * NB]
        g = dot(left, o_ref[:, : (i + 1) * NB], ((0,), (0,)), HIGHEST)
        for l in range(i + 1):
            block = g[:, l * NB : (l + 1) * NB]
            rows = slice((n % 5) * NB, (n % 5 + 1) * NB)
            mine = core_ref[0] == n // 5

            @pl.when(mine)
            def _():
                keep_ref[rows, :] = block

            @pl.when(jnp.logical_not(mine))
            def _():
                send_ref[rows, :] = block

            n += 1


def shape(*dims, dtype=F32):
    return jax.ShapeDtypeStruct(dims, dtype)


def call(kernel, outs, specs, name, flops, scratch=()):
    return pl.pallas_call(
        kernel,
        out_shape=outs,
        in_specs=specs,
        out_specs=jax.tree.map(lambda _: VMEM, outs),
        scratch_shapes=scratch,
        compiler_params=pltpu.CompilerParams(vmem_limit_bytes=LIMIT),
        cost_estimate=pl.CostEstimate(flops=flops, bytes_accessed=2**21, transcendentals=0),
        name=name,
    )


def lanes(v, k):
    return jnp.broadcast_to(v[:, k : k + 1], (8, NB))


def row(v, i):
    return jnp.broadcast_to(v[i : i + 1, :], (8, NB))


def leaf(a, z_ref, d_ref):
    lane = lax.broadcasted_iota(jnp.int32, (8, NB), 1)
    sub = lax.broadcasted_iota(jnp.int32, (8, NB), 0)
    z = [(lane == sub + 8 * r).astype(F32) for r in range(16)]
    diag = jnp.zeros((8, NB), F32)
    for m in range(16):
        k0 = 8 * m
        cols = [lanes(a[m], k0 + j) for j in range(8)]
        s = {(i, j): row(cols[j], i) for i in range(8) for j in range(i, 8)}
        rb = [row(a[m], j) for j in range(8)]
        zb = [row(z[m], j) for j in range(8)]
        cr = {r: [lanes(a[r], k0 + j) for j in range(8)] for r in range(m + 1, 16)}
        for j in range(8):
            inv = 1.0 / s[j, j]
            for jj in range(j + 1, 8):
                f = s[j, jj] * inv
                for k in range(jj, 8):
                    s[jj, k] = s[jj, k] - f * s[j, k]
                rb[jj] = rb[jj] - f * rb[j]
                zb[jj] = zb[jj] - f * zb[j]
            for r in range(m + 1, 16):
                low = cr[r][j] * inv
                for jj in range(j + 1, 8):
                    cr[r][jj] = cr[r][jj] - low * s[j, jj]
                a[r] = a[r] - low * rb[j]
                z[r] = z[r] - low * zb[j]
            rs = lax.rsqrt(s[j, j])
            z_ref[k0 + j : k0 + j + 1, :] = (zb[j] * rs)[0:1]
            diag = jnp.where(lane == k0 + j, s[j, j] * rs, diag)
    d_ref[...] = diag[0:1]


def finish_kernel(root, mine_ref, other_ref, f_ref, core_ref, o_ref, d_ref, w_ref, z_ref, e_ref):
    n = 0
    for i in range(4):
        for l in range(i + 1):
            rows = slice((n % 5) * NB, (n % 5 + 1) * NB)
            mine = core_ref[0] == n // 5

            @pl.when(mine)
            def _():
                w_ref[l, i * NB : (i + 1) * NB, :] = mine_ref[rows, :]

            @pl.when(jnp.logical_not(mine))
            def _():
                w_ref[l, i * NB : (i + 1) * NB, :] = other_ref[rows, :]

            n += 1
    for l in range(4):
        w_ref[l, 512:, :] = f_ref[:, l * NB : (l + 1) * NB]

    def step(j, carry):
        start = pl.multiple_of(j * NB, NB)
        tiles = [w_ref[j, pl.ds(start + 8 * r, 8), :] for r in range(16)]
        leaf(tiles, z_ref, e_ref)
        d_ref[pl.ds(j, 1), :] = e_ref[...] * (1.0 / root)
        for l in range(4):

            @pl.when(l == j)
            def _():
                lo = l * NB
                w_ref[l, lo:, :] = dot(w_ref[l, lo:, :], z_ref[...], ((1,), (1,)), HIGHEST)

        for l in range(1, 4):

            @pl.when(l > j)
            def _():
                lo = l * NB
                w_ref[l, lo:, :] = w_ref[l, lo:, :] - dot(
                    w_ref[j, lo:, :], w_ref[j, lo : lo + NB, :], ((1,), (1,)), HIGHEST
                )

        return carry

    lax.fori_loop(0, 4, step, 0)
    for l in range(4):
        o_ref[:, l * NB : (l + 1) * NB] = (w_ref[l, 512:, :] * root).astype(jnp.bfloat16)


def shift(v, axes, count, step):
    pairs = [(i, i + step) for i in range(count) if 0 <= i + step < count]
    return lax.ppermute(v, axes, pairs)


def neighbours(v):
    return (
        shift(v, GX, 32, 1),
        shift(v, GX, 32, -1),
        shift(v, GY, 16, 1),
        shift(v, GY, 16, -1),
    )


def swap(v):
    return lax.ppermute(v, "c", [(0, 1), (1, 0)])


def local(initial, couplings, frequencies, linked):
    rows, width = initial.shape[2:]
    v0 = initial[0, 0]
    blocks = couplings[0, 0]
    weights = frequencies[0, 0][:, None]
    present = linked[0, 0].astype(F32)
    core = lax.axis_index("c").astype(jnp.int32)[None]
    full = shape(rows, width)
    half = shape(rows, width, dtype=jnp.bfloat16)
    flops = 2 * rows * rows * width
    own = call(self_kernel, full, [VMEM] * 3, "own_block", flops)
    specs = [VMEM, VMEM, SMEM] + [VMEM] * 4

    part, halos = own(v0, blocks, weights), neighbours(v0)
    x1, r1 = call(first_kernel, (full, half), specs, "first", 4 * flops)(
        part, blocks, present, *halos
    )
    part, halos = own(r1, blocks, weights), neighbours(r1)
    r2 = call(middle_kernel, half, specs + [VMEM], "middle", 4 * flops)(
        part, blocks, present, *halos, v0
    )
    part, halos = own(r2, blocks, weights), neighbours(r2)
    piece = shape(5 * NB, NB)
    filtered, keep, send = call(
        last_kernel, (full, piece, piece), specs + [VMEM, SMEM], "last_and_correlation", 8 * flops
    )(part, blocks, present, *halos, x1, core)

    summed = keep + swap(send)
    share = 5 * NB * NB // N_CHIPS
    got = lax.all_to_all(summed.reshape(N_CHIPS, share), CHIPS, 0, 0, tiled=True)
    total = got.reshape(N_CHIPS, share).sum(0)
    spread = jnp.broadcast_to(total[None], (N_CHIPS, share))
    mine = lax.all_to_all(spread, CHIPS, 0, 0, tiled=True).reshape(5 * NB, NB)
    other = swap(mine)

    root = math.sqrt(rows * 512)
    out, diag = call(
        functools.partial(finish_kernel, root),
        (half, shape(4, NB)),
        [VMEM] * 3 + [SMEM],
        "finish",
        8 * flops,
        (
            pltpu.VMEM((4, width + rows, NB), F32),
            pltpu.VMEM((NB, NB), F32),
            pltpu.VMEM((1, NB), F32),
        ),
    )(mine, other, filtered, core)
    return out[None, None], diag.reshape(width)


def solution(mesh):
    fine = Mesh(mesh.devices.reshape(8, 4, 8, 2), GX + GY)
    in_specs = (
        P(GX, GY, None, None),
        P(GX, GY, None, None, None),
        P(GX, GY, None),
        P(GX, GY, None),
    )
    out_specs = (P(GX, GY, None, None), P())
    return jax.shard_map(local, mesh=fine, in_specs=in_specs, out_specs=out_specs, check_vma=False)
```

time: 579 us -> 181 us (0.31)
  waiting for transfers between devices: 335 us -> 20 us
  other arithmetic: 123 us -> 1.29 us
  blocking collectives: 0 us -> 70.3 us
  Pallas kernels: 0 us -> 30.4 us
  matrix products: 28.3 us -> 0 us
  local copies, waits for them, and re-layouts: 24.9 us -> 8.49 us
  between operations: 17.3 us -> 0.92 us
    psum x1 -> x0, waiting for transfers between devices: 280 us -> none  [local(): correlation = lax.psum(local_correlation, ('gx', 'gy'))]
    another operation x17 -> x0, other arithmetic: 120 us -> none  [the longest x14 78.9 us: local(): factor = jnp.linalg.cholesky(correlation)]
    all_to_all x0 -> x2, blocking collectives: none -> 70.3 us  [the longest x1 45.5 us: local(): lax.all_to_all(summed.reshape(N_CHIPS, share), CHIPS, 0, 0, tiled=True)]
    ppermute x12 -> x14, waiting for transfers between devices: 55.6 us -> 20 us  [the longest x12 17.6 us: shift(): return lax.ppermute(v, axes, pairs)]
    pallas_call x0 -> x7, Pallas kernels: none -> 30.4 us  [the longest x1 21.5 us: local(): call(functools.partial(finish_kernel, root), (half, shape(4, NB)), [VMEM]...]
    dot_general x17 -> x0, matrix products: 20.6 us -> none  [the longest x12 14.4 us: operate(): jnp.einsum('bij,bjk->bik', blocks[:, direction + 1], sources[direction],...]
    another operation x17 -> x1, local copies, waits for them, and re-layouts: 13.8 us -> 0.81 us  [local(): weights = frequencies[0, 0][:, None]]
    another operation x13 -> x0, matrix products: 7.7 us -> none  [the longest x7 5.82 us: local(): jax.scipy.linalg.solve_triangular(factor, jnp.eye(width, dtype=jnp.float3...]
  transfers between devices with their start and end apart: 13 -> 14, of which waited for: 12 -> 8; matrix products, arithmetic and copies ran while one was open for 2% -> 0% of each run, Pallas kernels for 0% -> 1%
where the time goes in v1:
time: 181 us
  blocking collectives  70.3 us (39%)
  starting transfers between devices  49.3 us (27%)
  Pallas kernels  30.4 us (17%)
  waiting for transfers between devices  20 us (11%)
  local copies, waits for them, and re-layouts  8.49 us (5%)
    all_to_all x1, blocking collectives, local(): lax.all_to_all(summed.reshape(N_CHIPS, share), CHIPS, 0, 0, tiled=True)  45.5 us
    ppermute x12, starting transfers between devices, shift(): return lax.ppermute(v, axes, pairs)  39.9 us
    all_to_all x1, blocking collectives, local(): mine = lax.all_to_all(spread, CHIPS, 0, 0, tiled=True).reshape(5 * NB, NB)  24.8 us
    pallas_call x1, Pallas kernels, local(): call(functools.partial(finish_kernel, root), (half, shape(4, NB)), [VMEM]...  21.5 us
    ppermute x12, waiting for transfers between devices, shift(): return lax.ppermute(v, axes, pairs)  17.6 us
    ppermute x2, starting transfers between devices, swap(): return lax.ppermute(v, 'c', [(0, 1), (1, 0)])  9.4 us
    unnamed x20, local copies, waits for them, and re-layouts  6.74 us
    pallas_call x1, Pallas kernels, local(): call(last_kernel, (full, piece, piece), specs + [VMEM, SMEM], 'last_and_c...  4.66 us
  transfers between devices with their start and end apart: 14, of which 8 were waited for; matrix products, arithmetic and copies ran while one was open for 0% of the time, Pallas kernels for 1%

profile of v1, /device:TPU:1, one launch (start us, length us, event | category | flops | bytes accessed | tf_op | source)
XLA Modules:
  0.0 180.7 jit_solution(11799630227166920019)
XLA Ops:
  0.6 8.8 %collective-permute-start.3 = (bf16[384,512]{1,0:T(8,128)(2,1)}, bf16[384,512]{1,0:T(8,128)(2,1)S(1)}, u32[]{:S(2)}, u32[]{:S(2)}) collective-permute-start(bf16[384,512]{1,0:T(8,128)(2,1)} %bitcast.14), channel_id=1, source_target_pairs={{1,0},{2,1},{3,2},{4,3},{5,4},{6,5},{7,6},{8,7},{9,8},{10,9},{11,1... | collective-permute-start | bytes 1179656 | tf_op jit(solution)/shard_map/ppermute | solution.py:183
  9.4 1.9 %collective-permute-start.2 = (bf16[384,512]{1,0:T(8,128)(2,1)}, bf16[384,512]{1,0:T(8,128)(2,1)S(1)}, u32[]{:S(2)}, u32[]{:S(2)}) collective-permute-start(bf16[384,512]{1,0:T(8,128)(2,1)} %bitcast.15), channel_id=1, source_target_pairs={{0,1},{1,2},{2,3},{3,4},{4,5},{5,6},{6,7},{7,8},{8,9},{9,10},{10,1... | collective-permute-start | bytes 1179656 | tf_op jit(solution)/shard_map/ppermute | solution.py:183
  11.4 1.3 collective-permute-start.1
  12.7 4.0 %collective-permute-start = (bf16[384,512]{1,0:T(8,128)(2,1)}, bf16[384,512]{1,0:T(8,128)(2,1)S(1)}, u32[]{:S(2)}, u32[]{:S(2)}) collective-permute-start(bf16[384,512]{1,0:T(8,128)(2,1)} %bitcast.17), channel_id=1, source_target_pairs={{0,16},{16,32},{32,48},{48,64},{64,80},{80,96},{96,112},{112,128},... | collective-permute-start | bytes 1179656 | tf_op jit(solution)/shard_map/ppermute | solution.py:183
  16.7 0.8 copy.9.w_ref
  17.5 0.0 copy-start.9
  17.5 0.0 copy-start
  17.5 1.4 copy-done
  18.9 0.0 copy-start.2
  18.9 1.0 copy-done.2
  19.9 0.0 copy-start.1
  19.9 0.4 own_block.3.part_ref
  20.3 0.0 copy-done.9
  20.3 0.0 collective-permute-done.3.h3
  20.3 0.0 collective-permute-done.2.h2
  20.3 3.3 %collective-permute-done.1.h1 = bf16[384,512]{1,0:T(8,128)(2,1)S(1)} collective-permute-done((bf16[384,512]{1,0:T(8,128)(2,1)}, bf16[384,512]{1,0:T(8,128)(2,1)S(1)}, u32[]{:S(2)}, u32[]{:S(2)}) %collective-permute-start.1) | collective-permute-done | bytes 393248 | tf_op jit(solution)/shard_map/ppermute | solution.py:183
  23.6 0.0 copy-start.3
  23.6 0.7 copy-done.3
  24.4 0.2 collective-permute-done.h0
  24.6 0.0 copy-start.5
  24.6 0.7 copy-done.5
  25.3 0.0 copy-done.1
  25.3 0.0 copy-start.4
  25.3 1.0 copy-done.4
  26.3 0.0 copy-start.6
  26.3 1.0 copy-done.6
  27.3 1.5 first.1
  28.9 3.6 %collective-permute-start.7 = (bf16[384,512]{1,0:T(8,128)(2,1)S(1)}, bf16[384,512]{1,0:T(8,128)(2,1)S(1)}, u32[]{:S(2)}, u32[]{:S(2)}) collective-permute-start(bf16[384,512]{1,0:T(8,128)(2,1)S(1)} %get-tuple-element.9.v_ref), channel_id=1, source_target_pairs={{1,0},{2,1},{3,2},{4,3},{5,4},{6,5},{7,6},{8,7},{9,8},{10,9},{11,1... | collective-permute-start | bytes 1179656 | tf_op jit(solution)/shard_map/ppermute | solution.py:183
  32.5 2.0 %collective-permute-start.6 = (bf16[384,512]{1,0:T(8,128)(2,1)S(1)}, bf16[384,512]{1,0:T(8,128)(2,1)S(1)}, u32[]{:S(2)}, u32[]{:S(2)}) collective-permute-start(bf16[384,512]{1,0:T(8,128)(2,1)S(1)} %get-tuple-element.9.v_ref), channel_id=1, source_target_pairs={{0,1},{1,2},{2,3},{3,4},{4,5},{5,6},{6,7},{7,8},{8,9},{9,10},{10,1... | collective-permute-start | bytes 1179656 | tf_op jit(solution)/shard_map/ppermute | solution.py:183
  34.5 1.3 collective-permute-start.5
  35.8 4.6 %collective-permute-start.4 = (bf16[384,512]{1,0:T(8,128)(2,1)S(1)}, bf16[384,512]{1,0:T(8,128)(2,1)S(1)}, u32[]{:S(2)}, u32[]{:S(2)}) collective-permute-start(bf16[384,512]{1,0:T(8,128)(2,1)S(1)} %get-tuple-element.9.v_ref), channel_id=1, source_target_pairs={{0,16},{16,32},{32,48},{48,64},{64,80},{80,96},{96,112},{112,128},... | collective-permute-start | bytes 1179656 | tf_op jit(solution)/shard_map/ppermute | solution.py:183
  40.4 0.4 own_block.4.part_ref
  40.8 0.0 collective-permute-done.7.h3
  40.8 0.0 collective-permute-done.6.h2
  40.8 6.7 %collective-permute-done.5.h1 = bf16[384,512]{1,0:T(8,128)(2,1)S(1)} collective-permute-done((bf16[384,512]{1,0:T(8,128)(2,1)S(1)}, bf16[384,512]{1,0:T(8,128)(2,1)S(1)}, u32[]{:S(2)}, u32[]{:S(2)}) %collective-permute-start.5) | collective-permute-done | bytes 393248 | tf_op jit(solution)/shard_map/ppermute | solution.py:183
  47.5 0.9 collective-permute-done.4.h0
  48.4 1.5 middle.1.v_ref
  49.9 3.2 %collective-permute-start.11 = (bf16[384,512]{1,0:T(8,128)(2,1)S(1)}, bf16[384,512]{1,0:T(8,128)(2,1)S(1)}, u32[]{:S(2)}, u32[]{:S(2)}) collective-permute-start(bf16[384,512]{1,0:T(8,128)(2,1)S(1)} %middle.1.v_ref), channel_id=1, source_target_pairs={{1,0},{2,1},{3,2},{4,3},{5,4},{6,5},{7,6},{8,7},{9,8},{10,9},{11,1... | collective-permute-start | bytes 1179656 | tf_op jit(solution)/shard_map/ppermute | solution.py:183
  53.2 2.3 %collective-permute-start.10 = (bf16[384,512]{1,0:T(8,128)(2,1)S(1)}, bf16[384,512]{1,0:T(8,128)(2,1)}, u32[]{:S(2)}, u32[]{:S(2)}) collective-permute-start(bf16[384,512]{1,0:T(8,128)(2,1)S(1)} %middle.1.v_ref), channel_id=1, source_target_pairs={{0,1},{1,2},{2,3},{3,4},{4,5},{5,6},{6,7},{7,8},{8,9},{9,10},{10,1... | collective-permute-start | bytes 1179656 | tf_op jit(solution)/shard_map/ppermute | solution.py:183
  55.5 1.3 collective-permute-start.9
  56.8 5.5 %collective-permute-start.8 = (bf16[384,512]{1,0:T(8,128)(2,1)S(1)}, bf16[384,512]{1,0:T(8,128)(2,1)}, u32[]{:S(2)}, u32[]{:S(2)}) collective-permute-start(bf16[384,512]{1,0:T(8,128)(2,1)S(1)} %middle.1.v_ref), channel_id=1, source_target_pairs={{0,16},{16,32},{32,48},{48,64},{64,80},{80,96},{96,112},{112,128},... | collective-permute-start | bytes 1179656 | tf_op jit(solution)/shard_map/ppermute | solution.py:183
  62.3 0.4 own_block.5.part_ref
  62.7 0.0 collective-permute-done.11.h3
  62.7 0.0 collective-permute-done.10.h2
  62.7 5.7 %collective-permute-done.9.h1 = bf16[384,512]{1,0:T(8,128)(2,1)} collective-permute-done((bf16[384,512]{1,0:T(8,128)(2,1)S(1)}, bf16[384,512]{1,0:T(8,128)(2,1)}, u32[]{:S(2)}, u32[]{:S(2)}) %collective-permute-start.9) | collective-permute-done | bytes 393248 | tf_op jit(solution)/shard_map/ppermute | solution.py:183
  68.4 0.8 collective-permute-done.8.h0
  69.1 4.7 %last_and_correlation.1 = (f32[384,512]{1,0:T(8,128)S(1)}, f32[640,128]{1,0:T(8,128)S(1)}, f32[640,128]{1,0:T(8,128)S(1)}) custom-call(f32[384,512]{1,0:T(8,128)S(1)} %own_block.5.part_ref, bf16[5,384,384]{2,1,0:T(8,128)(2,1)S(1)} %bitcast.13, f32[4]{0:T(128)S(1)} %convert_bitcast_fusion.l_ref, bf16[384,512]{1,0:T(8,128)(2,1)} %collective-permute-done.8.h0, ...), custom_call_target="tpu_custom_call" | custom-call | flops 1207959552 | bytes 2097152 | tf_op jit(solution)/shard_map/last_and_correlation/pallas_call | solution.py:222
  73.8 0.0 copy-start.7
  73.8 0.9 copy-done.7
  74.7 3.6 %collective-permute-start.12 = (f32[640,128]{1,0:T(8,128)S(1)}, f32[640,128]{1,0:T(8,128)S(1)}, u32[]{:S(2)}, u32[]{:S(2)}) collective-permute-start(f32[640,128]{1,0:T(8,128)S(1)} %get-tuple-element.12), channel_id=1, source_target_pairs={{0,1},{1,0},{2,3},{3,2},{4,5},{5,4},{6,7},{7,6},{8,9},{9,8},{10,11... | collective-permute-start | bytes 983048 | tf_op jit(solution)/shard_map/ppermute | solution.py:196
  78.3 1.2 collective-permute-done.12
  79.6 0.5 all_to_all.13
  80.1 45.5 %all_to_all.16 = f32[256,1,320]{2,1,0:T(1,128)S(1)} all-to-all(f32[256,1,320]{2,1,0:T(1,128)S(1)} %all_to_all.13), channel_id=1, replica_groups=mesh['z'=8,'x'=4,'y'=8,'c'=2] {'z','x','y'}, dimensions={0} | all-to-all | bytes 655360 | tf_op jit(solution)/shard_map/all_to_all | solution.py:228
  125.6 0.0 copy-start.8
  125.6 0.3 reduce_sum.9
  125.9 0.2 broadcast_in_dim.13
  126.2 24.8 %all_to_all.17 = f32[256,1,320]{2,1,0:T(1,128)S(1)} all-to-all(f32[256,1,320]{2,1,0:T(1,128)S(1)} %broadcast_in_dim.13), channel_id=1, replica_groups=mesh['z'=8,'x'=4,'y'=8,'c'=2] {'z','x','y'}, dimensions={0} | all-to-all | bytes 655360 | tf_op jit(solution)/shard_map/all_to_all | solution.py:231
  151.0 0.9 reduce.1
  151.9 0.2 reshape.22.mine_ref
  152.1 5.8 %collective-permute-start.13 = (f32[640,128]{1,0:T(8,128)S(1)}, f32[640,128]{1,0:T(8,128)S(1)}, u32[]{:S(2)}, u32[]{:S(2)}) collective-permute-start(f32[640,128]{1,0:T(8,128)S(1)} %reshape.22.mine_ref), channel_id=1, source_target_pairs={{0,1},{1,0},{2,3},{3,2},{4,5},{5,4},{6,7},{7,6},{8,9},{9,8},{10,11... | collective-permute-start | bytes 983048 | tf_op jit(solution)/shard_map/ppermute | solution.py:196
  157.9 1.2 collective-permute-done.13.other_ref
  159.2 0.0 copy-done.8
  159.2 21.5 %finish.1 = (bf16[384,512]{1,0:T(8,128)(2,1)}, f32[4,128]{1,0:T(4,128)}) custom-call(f32[640,128]{1,0:T(8,128)S(1)} %reshape.22.mine_ref, f32[640,128]{1,0:T(8,128)S(1)} %collective-permute-done.13.other_ref, f32[384,512]{1,0:T(8,128)S(1)} %copy-done.8, s32[1]{0:T(128)} %bitcast.4.core_ref), custom_call_target="tpu_custom_call" | custom-call | flops 1207959552 | bytes 2097152 | tf_op jit(solution)/shard_map/finish/pallas_call | solution.py:235
  (2 shorter events, 0.0 us)
Async XLA Ops:
  0.6 19.7 %collective-permute-start.3 = (bf16[384,512]{1,0:T(8,128)(2,1)}, bf16[384,512]{1,0:T(8,128)(2,1)S(1)}, u32[]{:S(2)}, u32[]{:S(2)}) collective-permute-start(bf16[384,512]{1,0:T(8,128)(2,1)} %bitcast.14), channel_id=1, source_target_pairs={{1,0},{2,1},{3,2},{4,3},{5,4},{6,5},{7,6},{8,7},{9,8},{10,9},{11,1... | collective-permute-start | bytes 1179656 | tf_op jit(solution)/shard_map/ppermute | solution.py:183
  9.4 10.9 %collective-permute-start.2 = (bf16[384,512]{1,0:T(8,128)(2,1)}, bf16[384,512]{1,0:T(8,128)(2,1)S(1)}, u32[]{:S(2)}, u32[]{:S(2)}) collective-permute-start(bf16[384,512]{1,0:T(8,128)(2,1)} %bitcast.15), channel_id=1, source_target_pairs={{0,1},{1,2},{2,3},{3,4},{4,5},{5,6},{6,7},{7,8},{8,9},{9,10},{10,1... | collective-permute-start | bytes 1179656 | tf_op jit(solution)/shard_map/ppermute | solution.py:183
  11.4 12.3 %collective-permute-start.1 = (bf16[384,512]{1,0:T(8,128)(2,1)}, bf16[384,512]{1,0:T(8,128)(2,1)S(1)}, u32[]{:S(2)}, u32[]{:S(2)}) collective-permute-start(bf16[384,512]{1,0:T(8,128)(2,1)} %bitcast.16), channel_id=1, source_target_pairs={{16,0},{32,16},{48,32},{64,48},{80,64},{96,80},{112,96},{128,112},... | collective-permute-start | bytes 1179656 | tf_op jit(solution)/shard_map/ppermute | solution.py:183
  12.7 11.9 %collective-permute-start = (bf16[384,512]{1,0:T(8,128)(2,1)}, bf16[384,512]{1,0:T(8,128)(2,1)S(1)}, u32[]{:S(2)}, u32[]{:S(2)}) collective-permute-start(bf16[384,512]{1,0:T(8,128)(2,1)} %bitcast.17), channel_id=1, source_target_pairs={{0,16},{16,32},{32,48},{48,64},{64,80},{80,96},{96,112},{112,128},... | collective-permute-start | bytes 1179656 | tf_op jit(solution)/shard_map/ppermute | solution.py:183
  17.5 2.8 %copy-start.9 = (s32[1,1,4]{2,1,0:T(1,128)S(1)}, s32[1,1,4]{2,1,0:T(1,128)}, u32[]{:S(2)}) copy-start(s32[1,1,4]{2,1,0:T(1,128)} %param.7) | copy-start | bytes 52
  17.5 1.4 copy-start
  18.9 1.0 copy-start.2
  19.9 5.5 %copy-start.1 = (bf16[1,1,5,384,384]{4,3,2,1,0:T(8,128)(2,1)S(1)}, bf16[1,1,5,384,384]{4,3,2,1,0:T(8,128)(2,1)}, u32[]{:S(2)}) copy-start(bf16[1,1,5,384,384]{4,3,2,1,0:T(8,128)(2,1)} %param.5) | copy-start | bytes 4423684
  23.6 0.8 copy-start.3
  24.6 0.7 copy-start.5
  25.3 1.0 copy-start.4
  26.3 1.0 copy-start.6
  28.9 11.9 %collective-permute-start.7 = (bf16[384,512]{1,0:T(8,128)(2,1)S(1)}, bf16[384,512]{1,0:T(8,128)(2,1)S(1)}, u32[]{:S(2)}, u32[]{:S(2)}) collective-permute-start(bf16[384,512]{1,0:T(8,128)(2,1)S(1)} %get-tuple-element.9.v_ref), channel_id=1, source_target_pairs={{1,0},{2,1},{3,2},{4,3},{5,4},{6,5},{7,6},{8,7},{9,8},{10,9},{11,1... | collective-permute-start | bytes 1179656 | tf_op jit(solution)/shard_map/ppermute | solution.py:183
  32.5 8.3 %collective-permute-start.6 = (bf16[384,512]{1,0:T(8,128)(2,1)S(1)}, bf16[384,512]{1,0:T(8,128)(2,1)S(1)}, u32[]{:S(2)}, u32[]{:S(2)}) collective-permute-start(bf16[384,512]{1,0:T(8,128)(2,1)S(1)} %get-tuple-element.9.v_ref), channel_id=1, source_target_pairs={{0,1},{1,2},{2,3},{3,4},{4,5},{5,6},{6,7},{7,8},{8,9},{9,10},{10,1... | collective-permute-start | bytes 1179656 | tf_op jit(solution)/shard_map/ppermute | solution.py:183
  34.5 13.1 %collective-permute-start.5 = (bf16[384,512]{1,0:T(8,128)(2,1)S(1)}, bf16[384,512]{1,0:T(8,128)(2,1)S(1)}, u32[]{:S(2)}, u32[]{:S(2)}) collective-permute-start(bf16[384,512]{1,0:T(8,128)(2,1)S(1)} %get-tuple-element.9.v_ref), channel_id=1, source_target_pairs={{16,0},{32,16},{48,32},{64,48},{80,64},{96,80},{112,96},{128,112},... | collective-permute-start | bytes 1179656 | tf_op jit(solution)/shard_map/ppermute | solution.py:183
  35.8 12.6 %collective-permute-start.4 = (bf16[384,512]{1,0:T(8,128)(2,1)S(1)}, bf16[384,512]{1,0:T(8,128)(2,1)S(1)}, u32[]{:S(2)}, u32[]{:S(2)}) collective-permute-start(bf16[384,512]{1,0:T(8,128)(2,1)S(1)} %get-tuple-element.9.v_ref), channel_id=1, source_target_pairs={{0,16},{16,32},{32,48},{48,64},{64,80},{80,96},{96,112},{112,128},... | collective-permute-start | bytes 1179656 | tf_op jit(solution)/shard_map/ppermute | solution.py:183
  49.9 12.7 %collective-permute-start.11 = (bf16[384,512]{1,0:T(8,128)(2,1)S(1)}, bf16[384,512]{1,0:T(8,128)(2,1)S(1)}, u32[]{:S(2)}, u32[]{:S(2)}) collective-permute-start(bf16[384,512]{1,0:T(8,128)(2,1)S(1)} %middle.1.v_ref), channel_id=1, source_target_pairs={{1,0},{2,1},{3,2},{4,3},{5,4},{6,5},{7,6},{8,7},{9,8},{10,9},{11,1... | collective-permute-start | bytes 1179656 | tf_op jit(solution)/shard_map/ppermute | solution.py:183
  53.2 9.5 %collective-permute-start.10 = (bf16[384,512]{1,0:T(8,128)(2,1)S(1)}, bf16[384,512]{1,0:T(8,128)(2,1)}, u32[]{:S(2)}, u32[]{:S(2)}) collective-permute-start(bf16[384,512]{1,0:T(8,128)(2,1)S(1)} %middle.1.v_ref), channel_id=1, source_target_pairs={{0,1},{1,2},{2,3},{3,4},{4,5},{5,6},{6,7},{7,8},{8,9},{9,10},{10,1... | collective-permute-start | bytes 1179656 | tf_op jit(solution)/shard_map/ppermute | solution.py:183
  55.5 12.9 %collective-permute-start.9 = (bf16[384,512]{1,0:T(8,128)(2,1)S(1)}, bf16[384,512]{1,0:T(8,128)(2,1)}, u32[]{:S(2)}, u32[]{:S(2)}) collective-permute-start(bf16[384,512]{1,0:T(8,128)(2,1)S(1)} %middle.1.v_ref), channel_id=1, source_target_pairs={{16,0},{32,16},{48,32},{64,48},{80,64},{96,80},{112,96},{128,112},... | collective-permute-start | bytes 1179656 | tf_op jit(solution)/shard_map/ppermute | solution.py:183
  56.8 12.3 %collective-permute-start.8 = (bf16[384,512]{1,0:T(8,128)(2,1)S(1)}, bf16[384,512]{1,0:T(8,128)(2,1)}, u32[]{:S(2)}, u32[]{:S(2)}) collective-permute-start(bf16[384,512]{1,0:T(8,128)(2,1)S(1)} %middle.1.v_ref), channel_id=1, source_target_pairs={{0,16},{16,32},{32,48},{48,64},{64,80},{80,96},{96,112},{112,128},... | collective-permute-start | bytes 1179656 | tf_op jit(solution)/shard_map/ppermute | solution.py:183
  73.8 0.9 copy-start.7
  74.7 4.9 %collective-permute-start.12 = (f32[640,128]{1,0:T(8,128)S(1)}, f32[640,128]{1,0:T(8,128)S(1)}, u32[]{:S(2)}, u32[]{:S(2)}) collective-permute-start(f32[640,128]{1,0:T(8,128)S(1)} %get-tuple-element.12), channel_id=1, source_target_pairs={{0,1},{1,0},{2,3},{3,2},{4,5},{5,4},{6,7},{7,6},{8,9},{9,8},{10,11... | collective-permute-start | bytes 983048 | tf_op jit(solution)/shard_map/ppermute | solution.py:196
  125.6 33.5 %copy-start.8 = (f32[384,512]{1,0:T(8,128)S(1)}, f32[384,512]{1,0:T(8,128)}, u32[]{:S(2)}) copy-start(f32[384,512]{1,0:T(8,128)} %copy-done.7) | copy-start | bytes 2359300
  152.1 7.0 %collective-permute-start.13 = (f32[640,128]{1,0:T(8,128)S(1)}, f32[640,128]{1,0:T(8,128)S(1)}, u32[]{:S(2)}, u32[]{:S(2)}) collective-permute-start(f32[640,128]{1,0:T(8,128)S(1)} %reshape.22.mine_ref), channel_id=1, source_target_pairs={{0,1},{1,0},{2,3},{3,2},{4,5},{5,4},{6,7},{7,6},{8,9},{9,8},{10,11... | collective-permute-start | bytes 983048 | tf_op jit(solution)/shard_map/ppermute | solution.py:196

commit v2 on v1

--- a/solution.py
+++ b/solution.py
@@ -20,7 +20,7 @@
 GY = ("y", "c")
 CHIPS = ("z", "x", "y")
 N_CHIPS = 256
-LIMIT = 40 * 2**20
+LIMIT = 12 * 2**20
 
 
 def dot(a, b, dims, precision=None):
@@ -29,35 +29,55 @@
     )
 
 
-def self_kernel(v_ref, c_ref, w_ref, o_ref):
+def halo_product(c_ref, l_ref, index, h_ref):
+    return l_ref[index - 1].astype(F32) * dot(c_ref[index], h_ref[...], ((1,), (0,)))
+
+
+def own_kernel(v_ref, c_ref, w_ref, o_ref):
     v = v_ref[...]
     o_ref[...] = (w_ref[...] - CENTER) * v.astype(F32) + dot(c_ref[0], v, ((1,), (0,)))
 
 
-def halo_sum(part_ref, c_ref, l_ref, halos):
+def halo_sum(part_ref, c_ref, l_ref, i_ref, halos):
     total = part_ref[...]
     for d, h in enumerate(halos):
-        total = total + l_ref[d] * dot(c_ref[d + 1], h[...], ((1,), (0,)))
+        total = total + halo_product(c_ref, l_ref, i_ref[d], h)
     return total
 
 
-def first_kernel(part_ref, c_ref, l_ref, h0, h1, h2, h3, o_ref, r_ref):
-    out = SCALE * halo_sum(part_ref, c_ref, l_ref, (h0, h1, h2, h3))
+def first_kernel(part_ref, c_ref, l_ref, i_ref, h0, h1, h2, h3, o_ref, r_ref):
+    out = SCALE * halo_sum(part_ref, c_ref, l_ref, i_ref, (h0, h1, h2, h3))
     o_ref[...] = out
     r_ref[...] = out.astype(jnp.bfloat16)
 
 
-def middle_kernel(part_ref, c_ref, l_ref, h0, h1, h2, h3, p_ref, r_ref):
-    out = 2.0 * SCALE * halo_sum(part_ref, c_ref, l_ref, (h0, h1, h2, h3)) - p_ref[...].astype(F32)
+def middle_kernel(part_ref, c_ref, l_ref, i_ref, h0, h1, h2, h3, p_ref, r_ref):
+    out = 2.0 * SCALE * halo_sum(part_ref, c_ref, l_ref, i_ref, (h0, h1, h2, h3)) - p_ref[...].astype(F32)
     r_ref[...] = out.astype(jnp.bfloat16)
 
 
-def last_kernel(part_ref, c_ref, l_ref, h0, h1, h2, h3, p_ref, core_ref, o_ref, keep_ref, send_ref):
-    o_ref[...] = 2.0 * SCALE * halo_sum(part_ref, c_ref, l_ref, (h0, h1, h2, h3)) - p_ref[...]
+def pieces(v):
+    high = v.astype(jnp.bfloat16)
+    rest = v - high.astype(F32)
+    middle = rest.astype(jnp.bfloat16)
+    return high, middle, (rest - middle.astype(F32)).astype(jnp.bfloat16)
+
+
+def product(a, b, dims):
+    total = dot(a[1], b[1], dims)
+    for i, k in ((0, 2), (2, 0), (0, 1), (1, 0), (0, 0)):
+        total = total + dot(a[i], b[k], dims)
+    return total
+
+
+def last_kernel(part_ref, c_ref, l_ref, i_ref, h0, h1, h2, h3, p_ref, core_ref, o_ref, keep_ref, send_ref):
+    out = 2.0 * SCALE * halo_sum(part_ref, c_ref, l_ref, i_ref, (h0, h1, h2, h3)) - p_ref[...]
+    o_ref[...] = out
+    right = pieces(out)
     n = 0
     for i in range(4):
-        left = o_ref[:, i * NB : (i + 1) * NB]
-        g = dot(left, o_ref[:, : (i + 1) * NB], ((0,), (0,)), HIGHEST)
+        left = pieces(out[:, i * NB : (i + 1) * NB].T)
+        g = product(left, [p[:, : (i + 1) * NB] for p in right], ((1,), (0,)))
         for l in range(i + 1):
             block = g[:, l * NB : (l + 1) * NB]
             rows = slice((n % 5) * NB, (n % 5 + 1) * NB)
@@ -178,17 +198,19 @@
         o_ref[:, l * NB : (l + 1) * NB] = (w_ref[l, 512:, :] * root).astype(jnp.bfloat16)
 
 
-def shift(v, axes, count, step):
-    pairs = [(i, i + step) for i in range(count) if 0 <= i + step < count]
+def exchange(v, axes, count, first):
+    pairs = []
+    for i in range(first, count - 1, 2):
+        pairs += [(i, i + 1), (i + 1, i)]
     return lax.ppermute(v, axes, pairs)
 
 
 def neighbours(v):
     return (
-        shift(v, GX, 32, 1),
-        shift(v, GX, 32, -1),
-        shift(v, GY, 16, 1),
-        shift(v, GY, 16, -1),
+        exchange(v, GY, 16, 0),
+        exchange(v, GY, 16, 1),
+        exchange(v, GX, 32, 0),
+        exchange(v, GX, 32, 1),
     )
 
 
@@ -201,27 +223,28 @@
     v0 = initial[0, 0]
     blocks = couplings[0, 0]
     weights = frequencies[0, 0][:, None]
-    present = linked[0, 0].astype(F32)
-    core = lax.axis_index("c").astype(jnp.int32)[None]
+    present = linked[0, 0]
+    core = lax.axis_index("c").astype(jnp.int32)
+    odd = lax.rem(lax.axis_index("x"), 2).astype(jnp.int32)
+    index = jnp.stack([4 - core, 3 + core, 2 - odd, 1 + odd])
+    core = core[None]
     full = shape(rows, width)
     half = shape(rows, width, dtype=jnp.bfloat16)
     flops = 2 * rows * rows * width
-    own = call(self_kernel, full, [VMEM] * 3, "own_block", flops)
-    specs = [VMEM, VMEM, SMEM] + [VMEM] * 4
-
-    part, halos = own(v0, blocks, weights), neighbours(v0)
-    x1, r1 = call(first_kernel, (full, half), specs, "first", 4 * flops)(
-        part, blocks, present, *halos
-    )
-    part, halos = own(r1, blocks, weights), neighbours(r1)
-    r2 = call(middle_kernel, half, specs + [VMEM], "middle", 4 * flops)(
-        part, blocks, present, *halos, v0
-    )
-    part, halos = own(r2, blocks, weights), neighbours(r2)
+
+    own = call(own_kernel, full, [VMEM] * 3, "own_block", flops)
+
+    def operands(v):
+        halos = neighbours(v)
+        return (own(v, blocks, weights), blocks, present, index, *halos)
+
+    specs = [VMEM, VMEM, SMEM, SMEM] + [VMEM] * 4
+    x1, r1 = call(first_kernel, (full, half), specs, "first", 4 * flops)(*operands(v0))
+    r2 = call(middle_kernel, half, specs + [VMEM], "middle", 4 * flops)(*operands(r1), v0)
     piece = shape(5 * NB, NB)
     filtered, keep, send = call(
         last_kernel, (full, piece, piece), specs + [VMEM, SMEM], "last_and_correlation", 8 * flops
-    )(part, blocks, present, *halos, x1, core)
+    )(*operands(r2), x1, core)
 
     summed = keep + swap(send)
     share = 5 * NB * NB // N_CHIPS

time: 181 us -> 159 us (0.88)
  waiting for transfers between devices: 20 us -> 8.91 us
  blocking collectives: 70.3 us -> 65.4 us
  local copies, waits for them, and re-layouts: 8.49 us -> 4.98 us
  starting transfers between devices: 49.3 us -> 46.5 us
    ppermute x12, waiting for transfers between devices: 17.6 us -> 6.44 us  [exchange(): return lax.ppermute(v, axes, pairs)]
    all_to_all x1, blocking collectives: 45.5 us -> 40.6 us  [local(): lax.all_to_all(summed.reshape(N_CHIPS, share), CHIPS, 0, 0, tiled=True)]
    unnamed x20 -> x8, local copies, waits for them, and re-layouts: 6.74 us -> 3.24 us
  transfers between devices with their start and end apart: 14 -> 14, of which waited for: 8 -> 6; matrix products, arithmetic and copies ran while one was open for 0% -> 1% of each run, Pallas kernels for 1% -> 1%
where the time goes in v2:
time: 159 us; the launch traced here: 158 us
  blocking collectives  65.4 us (41%)
  starting transfers between devices  46.5 us (29%)
  Pallas kernels  30.4 us (19%)
  waiting for transfers between devices  8.91 us (6%)
  local copies, waits for them, and re-layouts  4.98 us (3%)
    all_to_all x1, blocking collectives, local(): lax.all_to_all(summed.reshape(N_CHIPS, share), CHIPS, 0, 0, tiled=True)  40.6 us
    ppermute x12, starting transfers between devices, exchange(): return lax.ppermute(v, axes, pairs)  38.4 us
    all_to_all x1, blocking collectives, local(): mine = lax.all_to_all(spread, CHIPS, 0, 0, tiled=True).reshape(5 * NB, NB)  24.8 us
    pallas_call x1, Pallas kernels, local(): call(functools.partial(finish_kernel, root), (half, shape(4, NB)), [VMEM]...  21.5 us
    ppermute x2, starting transfers between devices, swap(): return lax.ppermute(v, 'c', [(0, 1), (1, 0)])  8.08 us
    ppermute x12, waiting for transfers between devices, exchange(): return lax.ppermute(v, axes, pairs)  6.44 us
    pallas_call x1, Pallas kernels, local(): call(last_kernel, (full, piece, piece), specs + [VMEM, SMEM], 'last_and_c...  4.67 us
    unnamed x8, local copies, waits for them, and re-layouts  3.24 us
  transfers between devices with their start and end apart: 14, of which 6 were waited for; matrix products, arithmetic and copies ran while one was open for 1% of the time, Pallas kernels for 1%

profile of v2, /device:TPU:1, one launch (start us, length us, event | category | flops | bytes accessed | tf_op | source)
XLA Modules:
  0.0 158.5 jit_solution(15134824243438419544)
XLA Ops:
  0.6 0.7 collective-permute-start.3
  1.3 6.4 %collective-permute-start.2 = (bf16[384,512]{1,0:T(8,128)(2,1)}, bf16[384,512]{1,0:T(8,128)(2,1)S(1)}, u32[]{:S(2)}, u32[]{:S(2)}) collective-permute-start(bf16[384,512]{1,0:T(8,128)(2,1)} %bitcast.18), channel_id=1, source_target_pairs={{0,16},{16,0},{32,48},{48,32},{64,80},{80,64},{96,112},{112,96},{1... | collective-permute-start | bytes 1179656 | tf_op jit(solution)/shard_map/ppermute | solution.py:205
  7.7 4.3 %collective-permute-start.1 = (bf16[384,512]{1,0:T(8,128)(2,1)}, bf16[384,512]{1,0:T(8,128)(2,1)S(1)}, u32[]{:S(2)}, u32[]{:S(2)}) collective-permute-start(bf16[384,512]{1,0:T(8,128)(2,1)} %bitcast.19), channel_id=1, source_target_pairs={{1,2},{2,1},{3,4},{4,3},{5,6},{6,5},{7,8},{8,7},{9,10},{10,9},{11,... | collective-permute-start | bytes 1179656 | tf_op jit(solution)/shard_map/ppermute | solution.py:205
  12.1 1.9 %collective-permute-start = (bf16[384,512]{1,0:T(8,128)(2,1)}, bf16[384,512]{1,0:T(8,128)(2,1)S(1)}, u32[]{:S(2)}, u32[]{:S(2)}) collective-permute-start(bf16[384,512]{1,0:T(8,128)(2,1)} %bitcast.20), channel_id=1, source_target_pairs={{0,1},{1,0},{2,3},{3,2},{4,5},{5,4},{6,7},{7,6},{8,9},{9,8},{10,11... | collective-permute-start | bytes 1179656 | tf_op jit(solution)/shard_map/ppermute | solution.py:205
  14.0 0.8 copy.9.w_ref
  14.8 0.0 copy-start.3
  14.8 0.0 copy-start
  14.8 1.4 copy-done
  16.2 0.0 copy-start.2
  16.2 1.0 copy-done.2
  17.2 0.0 copy-start.1
  17.2 0.4 own_block.3.part_ref
  17.6 0.1 pad_add_fusion.i_ref
  17.7 0.0 collective-permute-done.3.h3
  17.7 0.0 collective-permute-done.2.h2
  17.7 0.0 collective-permute-done.1.h1
  17.7 0.0 collective-permute-done.h0
  17.7 0.0 copy-done.3
  17.7 0.9 copy-done.1
  18.6 1.5 first.1
  20.1 0.7 collective-permute-start.7
  20.8 6.1 %collective-permute-start.6 = (bf16[384,512]{1,0:T(8,128)(2,1)S(1)}, bf16[384,512]{1,0:T(8,128)(2,1)S(1)}, u32[]{:S(2)}, u32[]{:S(2)}) collective-permute-start(bf16[384,512]{1,0:T(8,128)(2,1)S(1)} %get-tuple-element.9.v_ref), channel_id=1, source_target_pairs={{0,16},{16,0},{32,48},{48,32},{64,80},{80,64},{96,112},{112,96},{1... | collective-permute-start | bytes 1179656 | tf_op jit(solution)/shard_map/ppermute | solution.py:205
  26.9 4.1 %collective-permute-start.5 = (bf16[384,512]{1,0:T(8,128)(2,1)S(1)}, bf16[384,512]{1,0:T(8,128)(2,1)S(1)}, u32[]{:S(2)}, u32[]{:S(2)}) collective-permute-start(bf16[384,512]{1,0:T(8,128)(2,1)S(1)} %get-tuple-element.9.v_ref), channel_id=1, source_target_pairs={{1,2},{2,1},{3,4},{4,3},{5,6},{6,5},{7,8},{8,7},{9,10},{10,9},{11,... | collective-permute-start | bytes 1179656 | tf_op jit(solution)/shard_map/ppermute | solution.py:205
  31.0 1.9 %collective-permute-start.4 = (bf16[384,512]{1,0:T(8,128)(2,1)S(1)}, bf16[384,512]{1,0:T(8,128)(2,1)S(1)}, u32[]{:S(2)}, u32[]{:S(2)}) collective-permute-start(bf16[384,512]{1,0:T(8,128)(2,1)S(1)} %get-tuple-element.9.v_ref), channel_id=1, source_target_pairs={{0,1},{1,0},{2,3},{3,2},{4,5},{5,4},{6,7},{7,6},{8,9},{9,8},{10,11... | collective-permute-start | bytes 1179656 | tf_op jit(solution)/shard_map/ppermute | solution.py:205
  33.0 0.4 own_block.4.part_ref
  33.3 0.0 collective-permute-done.7.h3
  33.4 2.2 %collective-permute-done.6.h2 = bf16[384,512]{1,0:T(8,128)(2,1)S(1)} collective-permute-done((bf16[384,512]{1,0:T(8,128)(2,1)S(1)}, bf16[384,512]{1,0:T(8,128)(2,1)S(1)}, u32[]{:S(2)}, u32[]{:S(2)}) %collective-permute-start.6) | collective-permute-done | bytes 393248 | tf_op jit(solution)/shard_map/ppermute | solution.py:205
  35.6 0.9 collective-permute-done.5.h1
  36.5 0.0 collective-permute-done.4.h0
  36.5 1.6 middle.1.v_ref
  38.1 0.7 collective-permute-start.11
  38.8 5.5 %collective-permute-start.10 = (bf16[384,512]{1,0:T(8,128)(2,1)S(1)}, bf16[384,512]{1,0:T(8,128)(2,1)S(1)}, u32[]{:S(2)}, u32[]{:S(2)}) collective-permute-start(bf16[384,512]{1,0:T(8,128)(2,1)S(1)} %middle.1.v_ref), channel_id=1, source_target_pairs={{0,16},{16,0},{32,48},{48,32},{64,80},{80,64},{96,112},{112,96},{1... | collective-permute-start | bytes 1179656 | tf_op jit(solution)/shard_map/ppermute | solution.py:205
  44.4 4.1 %collective-permute-start.9 = (bf16[384,512]{1,0:T(8,128)(2,1)S(1)}, bf16[384,512]{1,0:T(8,128)(2,1)S(1)}, u32[]{:S(2)}, u32[]{:S(2)}) collective-permute-start(bf16[384,512]{1,0:T(8,128)(2,1)S(1)} %middle.1.v_ref), channel_id=1, source_target_pairs={{1,2},{2,1},{3,4},{4,3},{5,6},{6,5},{7,8},{8,7},{9,10},{10,9},{11,... | collective-permute-start | bytes 1179656 | tf_op jit(solution)/shard_map/ppermute | solution.py:205
  48.5 1.9 %collective-permute-start.8 = (bf16[384,512]{1,0:T(8,128)(2,1)S(1)}, bf16[384,512]{1,0:T(8,128)(2,1)S(1)}, u32[]{:S(2)}, u32[]{:S(2)}) collective-permute-start(bf16[384,512]{1,0:T(8,128)(2,1)S(1)} %middle.1.v_ref), channel_id=1, source_target_pairs={{0,1},{1,0},{2,3},{3,2},{4,5},{5,4},{6,7},{7,6},{8,9},{9,8},{10,11... | collective-permute-start | bytes 1179656 | tf_op jit(solution)/shard_map/ppermute | solution.py:205
  50.4 0.4 own_block.5.part_ref
  50.8 0.0 collective-permute-done.11.h3
  50.8 2.4 %collective-permute-done.10.h2 = bf16[384,512]{1,0:T(8,128)(2,1)S(1)} collective-permute-done((bf16[384,512]{1,0:T(8,128)(2,1)S(1)}, bf16[384,512]{1,0:T(8,128)(2,1)S(1)}, u32[]{:S(2)}, u32[]{:S(2)}) %collective-permute-start.10) | collective-permute-done | bytes 393248 | tf_op jit(solution)/shard_map/ppermute | solution.py:205
  53.2 0.8 collective-permute-done.9.h1
  54.0 0.0 collective-permute-done.8.h0
  54.0 4.7 %last_and_correlation.1 = (f32[384,512]{1,0:T(8,128)S(1)}, f32[640,128]{1,0:T(8,128)S(1)}, f32[640,128]{1,0:T(8,128)S(1)}) custom-call(f32[384,512]{1,0:T(8,128)S(1)} %own_block.5.part_ref, bf16[5,384,384]{2,1,0:T(8,128)(2,1)S(1)} %bitcast.16, s32[4]{0:T(128)S(1)} %bitcast.25, s32[4]{0:T(128)S(1)} %pad_add_fusion.i_ref, ...), custom_call_target="tpu_custom_call" | custom-call | flops 1207959552 | bytes 2097152 | tf_op jit(solution)/shard_map/last_and_correlation/pallas_call | solution.py:245
  58.7 2.3 %collective-permute-start.12 = (f32[640,128]{1,0:T(8,128)S(1)}, f32[640,128]{1,0:T(8,128)S(1)}, u32[]{:S(2)}, u32[]{:S(2)}) collective-permute-start(f32[640,128]{1,0:T(8,128)S(1)} %get-tuple-element.12), channel_id=1, source_target_pairs={{0,1},{1,0},{2,3},{3,2},{4,5},{5,4},{6,7},{7,6},{8,9},{9,8},{10,11... | collective-permute-start | bytes 983048 | tf_op jit(solution)/shard_map/ppermute | solution.py:218
  61.0 1.2 collective-permute-done.12
  62.3 0.5 all_to_all.13
  62.8 40.6 %all_to_all.16 = f32[256,1,320]{2,1,0:T(1,128)S(1)} all-to-all(f32[256,1,320]{2,1,0:T(1,128)S(1)} %all_to_all.13), channel_id=1, replica_groups=mesh['z'=8,'x'=4,'y'=8,'c'=2] {'z','x','y'}, dimensions={0} | all-to-all | bytes 655360 | tf_op jit(solution)/shard_map/all_to_all | solution.py:251
  103.4 0.3 reduce_sum.9
  103.7 0.2 broadcast_in_dim.13
  103.9 24.8 %all_to_all.17 = f32[256,1,320]{2,1,0:T(1,128)S(1)} all-to-all(f32[256,1,320]{2,1,0:T(1,128)S(1)} %broadcast_in_dim.13), channel_id=1, replica_groups=mesh['z'=8,'x'=4,'y'=8,'c'=2] {'z','x','y'}, dimensions={0} | all-to-all | bytes 655360 | tf_op jit(solution)/shard_map/all_to_all | solution.py:254
  128.7 0.9 reduce.1
  129.7 0.2 reshape.21.mine_ref
  129.9 5.8 %collective-permute-start.13 = (f32[640,128]{1,0:T(8,128)S(1)}, f32[640,128]{1,0:T(8,128)S(1)}, u32[]{:S(2)}, u32[]{:S(2)}) collective-permute-start(f32[640,128]{1,0:T(8,128)S(1)} %reshape.21.mine_ref), channel_id=1, source_target_pairs={{0,1},{1,0},{2,3},{3,2},{4,5},{5,4},{6,7},{7,6},{8,9},{9,8},{10,11... | collective-permute-start | bytes 983048 | tf_op jit(solution)/shard_map/ppermute | solution.py:218
  135.7 1.2 collective-permute-done.13.other_ref
  136.9 21.5 %finish.1 = (bf16[384,512]{1,0:T(8,128)(2,1)}, f32[4,128]{1,0:T(4,128)}) custom-call(f32[640,128]{1,0:T(8,128)S(1)} %reshape.21.mine_ref, f32[640,128]{1,0:T(8,128)S(1)} %collective-permute-done.13.other_ref, f32[384,512]{1,0:T(8,128)S(1)} %get-tuple-element.13.f_ref, s32[1]{0:T(128)} %bitcast.8.core_ref), custom_call_target="tpu_custom_call" | custom-call | flops 1207959552 | bytes 2097152 | tf_op jit(solution)/shard_map/finish/pallas_call | solution.py:258
  (1 shorter events, 0.0 us)
Async XLA Ops:
  0.6 17.0 %collective-permute-start.3 = (bf16[384,512]{1,0:T(8,128)(2,1)}, bf16[384,512]{1,0:T(8,128)(2,1)S(1)}, u32[]{:S(2)}, u32[]{:S(2)}) collective-permute-start(bf16[384,512]{1,0:T(8,128)(2,1)} %bitcast.17), channel_id=1, source_target_pairs={{16,32},{32,16},{48,64},{64,48},{80,96},{96,80},{112,128},{128,112... | collective-permute-start | bytes 1179656 | tf_op jit(solution)/shard_map/ppermute | solution.py:205
  1.3 16.3 %collective-permute-start.2 = (bf16[384,512]{1,0:T(8,128)(2,1)}, bf16[384,512]{1,0:T(8,128)(2,1)S(1)}, u32[]{:S(2)}, u32[]{:S(2)}) collective-permute-start(bf16[384,512]{1,0:T(8,128)(2,1)} %bitcast.18), channel_id=1, source_target_pairs={{0,16},{16,0},{32,48},{48,32},{64,80},{80,64},{96,112},{112,96},{1... | collective-permute-start | bytes 1179656 | tf_op jit(solution)/shard_map/ppermute | solution.py:205
  7.7 10.0 %collective-permute-start.1 = (bf16[384,512]{1,0:T(8,128)(2,1)}, bf16[384,512]{1,0:T(8,128)(2,1)S(1)}, u32[]{:S(2)}, u32[]{:S(2)}) collective-permute-start(bf16[384,512]{1,0:T(8,128)(2,1)} %bitcast.19), channel_id=1, source_target_pairs={{1,2},{2,1},{3,4},{4,3},{5,6},{6,5},{7,8},{8,7},{9,10},{10,9},{11,... | collective-permute-start | bytes 1179656 | tf_op jit(solution)/shard_map/ppermute | solution.py:205
  12.1 5.7 %collective-permute-start = (bf16[384,512]{1,0:T(8,128)(2,1)}, bf16[384,512]{1,0:T(8,128)(2,1)S(1)}, u32[]{:S(2)}, u32[]{:S(2)}) collective-permute-start(bf16[384,512]{1,0:T(8,128)(2,1)} %bitcast.20), channel_id=1, source_target_pairs={{0,1},{1,0},{2,3},{3,2},{4,5},{5,4},{6,7},{7,6},{8,9},{9,8},{10,11... | collective-permute-start | bytes 1179656 | tf_op jit(solution)/shard_map/ppermute | solution.py:205
  14.8 2.9 %copy-start.3 = (s32[1,1,4]{2,1,0:T(1,128)S(1)}, s32[1,1,4]{2,1,0:T(1,128)}, u32[]{:S(2)}) copy-start(s32[1,1,4]{2,1,0:T(1,128)} %param.7) | copy-start | bytes 52
  14.8 1.4 copy-start
  16.2 1.0 copy-start.2
  17.2 1.4 copy-start.1
  20.1 13.2 %collective-permute-start.7 = (bf16[384,512]{1,0:T(8,128)(2,1)S(1)}, bf16[384,512]{1,0:T(8,128)(2,1)S(1)}, u32[]{:S(2)}, u32[]{:S(2)}) collective-permute-start(bf16[384,512]{1,0:T(8,128)(2,1)S(1)} %get-tuple-element.9.v_ref), channel_id=1, source_target_pairs={{16,32},{32,16},{48,64},{64,48},{80,96},{96,80},{112,128},{128,112... | collective-permute-start | bytes 1179656 | tf_op jit(solution)/shard_map/ppermute | solution.py:205
  20.8 14.8 %collective-permute-start.6 = (bf16[384,512]{1,0:T(8,128)(2,1)S(1)}, bf16[384,512]{1,0:T(8,128)(2,1)S(1)}, u32[]{:S(2)}, u32[]{:S(2)}) collective-permute-start(bf16[384,512]{1,0:T(8,128)(2,1)S(1)} %get-tuple-element.9.v_ref), channel_id=1, source_target_pairs={{0,16},{16,0},{32,48},{48,32},{64,80},{80,64},{96,112},{112,96},{1... | collective-permute-start | bytes 1179656 | tf_op jit(solution)/shard_map/ppermute | solution.py:205
  26.9 9.7 %collective-permute-start.5 = (bf16[384,512]{1,0:T(8,128)(2,1)S(1)}, bf16[384,512]{1,0:T(8,128)(2,1)S(1)}, u32[]{:S(2)}, u32[]{:S(2)}) collective-permute-start(bf16[384,512]{1,0:T(8,128)(2,1)S(1)} %get-tuple-element.9.v_ref), channel_id=1, source_target_pairs={{1,2},{2,1},{3,4},{4,3},{5,6},{6,5},{7,8},{8,7},{9,10},{10,9},{11,... | collective-permute-start | bytes 1179656 | tf_op jit(solution)/shard_map/ppermute | solution.py:205
  31.0 5.5 %collective-permute-start.4 = (bf16[384,512]{1,0:T(8,128)(2,1)S(1)}, bf16[384,512]{1,0:T(8,128)(2,1)S(1)}, u32[]{:S(2)}, u32[]{:S(2)}) collective-permute-start(bf16[384,512]{1,0:T(8,128)(2,1)S(1)} %get-tuple-element.9.v_ref), channel_id=1, source_target_pairs={{0,1},{1,0},{2,3},{3,2},{4,5},{5,4},{6,7},{7,6},{8,9},{9,8},{10,11... | collective-permute-start | bytes 1179656 | tf_op jit(solution)/shard_map/ppermute | solution.py:205
  38.1 12.7 %collective-permute-start.11 = (bf16[384,512]{1,0:T(8,128)(2,1)S(1)}, bf16[384,512]{1,0:T(8,128)(2,1)S(1)}, u32[]{:S(2)}, u32[]{:S(2)}) collective-permute-start(bf16[384,512]{1,0:T(8,128)(2,1)S(1)} %middle.1.v_ref), channel_id=1, source_target_pairs={{16,32},{32,16},{48,64},{64,48},{80,96},{96,80},{112,128},{128,112... | collective-permute-start | bytes 1179656 | tf_op jit(solution)/shard_map/ppermute | solution.py:205
  38.8 14.4 %collective-permute-start.10 = (bf16[384,512]{1,0:T(8,128)(2,1)S(1)}, bf16[384,512]{1,0:T(8,128)(2,1)S(1)}, u32[]{:S(2)}, u32[]{:S(2)}) collective-permute-start(bf16[384,512]{1,0:T(8,128)(2,1)S(1)} %middle.1.v_ref), channel_id=1, source_target_pairs={{0,16},{16,0},{32,48},{48,32},{64,80},{80,64},{96,112},{112,96},{1... | collective-permute-start | bytes 1179656 | tf_op jit(solution)/shard_map/ppermute | solution.py:205
  44.4 9.7 %collective-permute-start.9 = (bf16[384,512]{1,0:T(8,128)(2,1)S(1)}, bf16[384,512]{1,0:T(8,128)(2,1)S(1)}, u32[]{:S(2)}, u32[]{:S(2)}) collective-permute-start(bf16[384,512]{1,0:T(8,128)(2,1)S(1)} %middle.1.v_ref), channel_id=1, source_target_pairs={{1,2},{2,1},{3,4},{4,3},{5,6},{6,5},{7,8},{8,7},{9,10},{10,9},{11,... | collective-permute-start | bytes 1179656 | tf_op jit(solution)/shard_map/ppermute | solution.py:205
  48.5 5.5 %collective-permute-start.8 = (bf16[384,512]{1,0:T(8,128)(2,1)S(1)}, bf16[384,512]{1,0:T(8,128)(2,1)S(1)}, u32[]{:S(2)}, u32[]{:S(2)}) collective-permute-start(bf16[384,512]{1,0:T(8,128)(2,1)S(1)} %middle.1.v_ref), channel_id=1, source_target_pairs={{0,1},{1,0},{2,3},{3,2},{4,5},{5,4},{6,7},{7,6},{8,9},{9,8},{10,11... | collective-permute-start | bytes 1179656 | tf_op jit(solution)/shard_map/ppermute | solution.py:205
  58.7 3.5 %collective-permute-start.12 = (f32[640,128]{1,0:T(8,128)S(1)}, f32[640,128]{1,0:T(8,128)S(1)}, u32[]{:S(2)}, u32[]{:S(2)}) collective-permute-start(f32[640,128]{1,0:T(8,128)S(1)} %get-tuple-element.12), channel_id=1, source_target_pairs={{0,1},{1,0},{2,3},{3,2},{4,5},{5,4},{6,7},{7,6},{8,9},{9,8},{10,11... | collective-permute-start | bytes 983048 | tf_op jit(solution)/shard_map/ppermute | solution.py:218
  129.9 7.0 %collective-permute-start.13 = (f32[640,128]{1,0:T(8,128)S(1)}, f32[640,128]{1,0:T(8,128)S(1)}, u32[]{:S(2)}, u32[]{:S(2)}) collective-permute-start(f32[640,128]{1,0:T(8,128)S(1)} %reshape.21.mine_ref), channel_id=1, source_target_pairs={{0,1},{1,0},{2,3},{3,2},{4,5},{5,4},{6,7},{7,6},{8,9},{9,8},{10,11... | collective-permute-start | bytes 983048 | tf_op jit(solution)/shard_map/ppermute | solution.py:218

commit v3 on v2

--- a/solution.py
+++ b/solution.py
@@ -18,8 +18,7 @@
 SMEM = pl.BlockSpec(memory_space=pltpu.SMEM)
 GX = ("z", "x")
 GY = ("y", "c")
-CHIPS = ("z", "x", "y")
-N_CHIPS = 256
+PLANE = ("z", "y")
 LIMIT = 12 * 2**20
 
 
@@ -56,11 +55,15 @@
     r_ref[...] = out.astype(jnp.bfloat16)
 
 
+def split(v):
+    high = v.astype(jnp.bfloat16).astype(F32)
+    rest = v - high
+    middle = rest.astype(jnp.bfloat16).astype(F32)
+    return high, middle, rest - middle
+
+
 def pieces(v):
-    high = v.astype(jnp.bfloat16)
-    rest = v - high.astype(F32)
-    middle = rest.astype(jnp.bfloat16)
-    return high, middle, (rest - middle.astype(F32)).astype(jnp.bfloat16)
+    return [p.astype(jnp.bfloat16) for p in split(v)]
 
 
 def product(a, b, dims):
@@ -111,26 +114,33 @@
     )
 
 
+NEAR = 3
+
+
 def lanes(v, k):
     return jnp.broadcast_to(v[:, k : k + 1], (8, NB))
 
 
-def row(v, i):
-    return jnp.broadcast_to(v[i : i + 1, :], (8, NB))
-
-
-def leaf(a, z_ref, d_ref):
+def row(ref, i):
+    return jnp.broadcast_to(ref[i : i + 1, :], (8, NB))
+
+
+def leaf(a, z_ref, d_ref, col_buf, a_buf, z_buf, right_buf, left_buf, hook):
     lane = lax.broadcasted_iota(jnp.int32, (8, NB), 1)
     sub = lax.broadcasted_iota(jnp.int32, (8, NB), 0)
     z = [(lane == sub + 8 * r).astype(F32) for r in range(16)]
     diag = jnp.zeros((8, NB), F32)
     for m in range(16):
-        k0 = 8 * m
-        cols = [lanes(a[m], k0 + j) for j in range(8)]
-        s = {(i, j): row(cols[j], i) for i in range(8) for j in range(i, 8)}
-        rb = [row(a[m], j) for j in range(8)]
-        zb = [row(z[m], j) for j in range(8)]
-        cr = {r: [lanes(a[r], k0 + j) for j in range(8)] for r in range(m + 1, 16)}
+        k0, p = 8 * m, m % 2
+        near = range(m + 1, min(m + 1 + NEAR, 16))
+        for j in range(8):
+            col_buf[p, j] = lanes(a[m], k0 + j)
+        a_buf[p] = a[m]
+        z_buf[p] = z[m]
+        s = {(i, j): row(col_buf.at[p, j], i) for i in range(8) for j in range(i, 8)}
+        rb = [row(a_buf.at[p], j) for j in range(8)]
+        zb = [row(z_buf.at[p], j) for j in range(8)]
+        cr = {r: [lanes(a[r], k0 + j) for j in range(8)] for r in near}
         for j in range(8):
             inv = 1.0 / s[j, j]
             for jj in range(j + 1, 8):
@@ -139,63 +149,96 @@
                     s[jj, k] = s[jj, k] - f * s[j, k]
                 rb[jj] = rb[jj] - f * rb[j]
                 zb[jj] = zb[jj] - f * zb[j]
-            for r in range(m + 1, 16):
+            for r in near:
                 low = cr[r][j] * inv
                 for jj in range(j + 1, 8):
                     cr[r][jj] = cr[r][jj] - low * s[j, jj]
                 a[r] = a[r] - low * rb[j]
                 z[r] = z[r] - low * zb[j]
+            if m + 1 + NEAR < 16:
+                right_buf[p, j : j + 1, :NB] = rb[j][0:1]
+                right_buf[p, j : j + 1, NB:] = zb[j][0:1]
+                left_buf[p, j : j + 1, :] = (rb[j] * inv)[0:1]
             rs = lax.rsqrt(s[j, j])
             z_ref[k0 + j : k0 + j + 1, :] = (zb[j] * rs)[0:1]
             diag = jnp.where(lane == k0 + j, s[j, j] * rs, diag)
+        if m + 1 + NEAR < 16:
+            lh, lm, ll = split(left_buf[p])
+            rh, rm, rl = split(right_buf[p])
+            left = jnp.concatenate([lh, lh, lm, lm, lh, ll], 0).astype(jnp.bfloat16)
+            right = jnp.concatenate([rh, rm, rh, rm, rl, rh], 0).astype(jnp.bfloat16)
+            change = dot(left, right, ((0,), (0,)))
+            for r in range(m + 1 + NEAR, 16):
+                a[r] = a[r] - change[8 * r : 8 * r + 8, :NB]
+                z[r] = z[r] - change[8 * r : 8 * r + 8, NB:]
+        hook(m)
     d_ref[...] = diag[0:1]
 
 
-def finish_kernel(root, mine_ref, other_ref, f_ref, core_ref, o_ref, d_ref, w_ref, z_ref, e_ref):
-    n = 0
+def finish_kernel(
+    root, mine_ref, other_ref, f_ref, core_ref, o_ref, d_ref, w_ref, z_ref, e_ref, *bufs
+):
+    order = {}
     for i in range(4):
         for l in range(i + 1):
-            rows = slice((n % 5) * NB, (n % 5 + 1) * NB)
-            mine = core_ref[0] == n // 5
-
-            @pl.when(mine)
-            def _():
-                w_ref[l, i * NB : (i + 1) * NB, :] = mine_ref[rows, :]
-
-            @pl.when(jnp.logical_not(mine))
-            def _():
-                w_ref[l, i * NB : (i + 1) * NB, :] = other_ref[rows, :]
-
-            n += 1
-    for l in range(4):
-        w_ref[l, 512:, :] = f_ref[:, l * NB : (l + 1) * NB]
-
-    def step(j, carry):
-        start = pl.multiple_of(j * NB, NB)
-        tiles = [w_ref[j, pl.ds(start + 8 * r, 8), :] for r in range(16)]
-        leaf(tiles, z_ref, e_ref)
-        d_ref[pl.ds(j, 1), :] = e_ref[...] * (1.0 / root)
-        for l in range(4):
-
-            @pl.when(l == j)
-            def _():
-                lo = l * NB
-                w_ref[l, lo:, :] = dot(w_ref[l, lo:, :], z_ref[...], ((1,), (1,)), HIGHEST)
-
-        for l in range(1, 4):
-
-            @pl.when(l > j)
-            def _():
-                lo = l * NB
-                w_ref[l, lo:, :] = w_ref[l, lo:, :] - dot(
-                    w_ref[j, lo:, :], w_ref[j, lo : lo + NB, :], ((1,), (1,)), HIGHEST
-                )
-
-        return carry
-
-    lax.fori_loop(0, 4, step, 0)
-    for l in range(4):
-        o_ref[:, l * NB : (l + 1) * NB] = (w_ref[l, 512:, :] * root).astype(jnp.bfloat16)
+            order[i, l] = len(order)
+    stored = set()
+
+    def rows(i):
+        return slice(i * NB, (i + 1) * NB)
+
+    def get(i, l):
+        if (i, l) in stored:
+            return w_ref[l, rows(i), :]
+        if i >= 4:
+            return f_ref[rows(i - 4), rows(l)]
+        n = order[i, l]
+        here, there = mine_ref[rows(n % 5), :], other_ref[rows(n % 5), :]
+        return jnp.where(core_ref[0] == n // 5, here, there)
+
+    def put(i, l, v):
+        w_ref[l, rows(i), :] = v
+        stored.add((i, l))
+
+    def panel(i, j):
+        v = dot(get(i, j), z_ref[j], ((1,), (1,)), HIGHEST)
+        put(i, j, v)
+        if i >= 4:
+            o_ref[rows(i - 4), rows(j)] = (v * root).astype(jnp.bfloat16)
+
+    def update(i, l, j):
+        change = dot(w_ref[j, rows(i), :], w_ref[j, rows(l), :], ((1,), (1,)), HIGHEST)
+        put(i, l, get(i, l) - change)
+
+    queue = []
+
+    def hook(_):
+        if queue:
+            task, where = queue.pop(0)
+            task(*where)
+
+    for j in range(4):
+        block = get(j, j)
+        leaf([block[8 * r : 8 * r + 8] for r in range(16)], z_ref.at[j], e_ref, *bufs, hook)
+        d_ref[j : j + 1, :] = e_ref[...] * (1.0 / root)
+        while queue:
+            hook(j)
+        if j < 3:
+            panel(j + 1, j)
+            update(j + 1, j + 1, j)
+        for i in range(j + 2, 4):
+            queue.append((panel, (i, j)))
+        for i in range(j + 2, 4):
+            queue.append((update, (i, j + 1, j)))
+        for i in range(j + 2, 4):
+            for l in range(j + 2, i + 1):
+                queue.append((update, (i, l, j)))
+        for i in range(4, 7):
+            queue.append((panel, (i, j)))
+            for l in range(j + 1, 4):
+                queue.append((update, (i, l, j)))
+    while queue:
+        hook(4)
 
 
 def exchange(v, axes, count, first):
@@ -247,11 +290,15 @@
     )(*operands(r2), x1, core)
 
     summed = keep + swap(send)
-    share = 5 * NB * NB // N_CHIPS
-    got = lax.all_to_all(summed.reshape(N_CHIPS, share), CHIPS, 0, 0, tiled=True)
-    total = got.reshape(N_CHIPS, share).sum(0)
-    spread = jnp.broadcast_to(total[None], (N_CHIPS, share))
-    mine = lax.all_to_all(spread, CHIPS, 0, 0, tiled=True).reshape(5 * NB, NB)
+    quarter = 5 * NB // 4
+    share = quarter * NB // 64
+    part = lax.all_to_all(summed.reshape(4, quarter, NB), "x", 0, 0).sum(0)
+    part = lax.all_to_all(part.reshape(64, share), PLANE, 0, 0, tiled=True)
+    total = part.reshape(64, share).sum(0)
+    part = lax.all_to_all(jnp.broadcast_to(total[None], (64, share)), PLANE, 0, 0, tiled=True)
+    part = part.reshape(1, quarter, NB)
+    mine = lax.all_to_all(jnp.broadcast_to(part, (4, quarter, NB)), "x", 0, 0)
+    mine = mine.reshape(5 * NB, NB)
     other = swap(mine)
 
     root = math.sqrt(rows * 512)
@@ -263,8 +310,13 @@
         8 * flops,
         (
             pltpu.VMEM((4, width + rows, NB), F32),
-            pltpu.VMEM((NB, NB), F32),
+            pltpu.VMEM((4, NB, NB), F32),
             pltpu.VMEM((1, NB), F32),
+            pltpu.VMEM((2, 8, 8, NB), F32),
+            pltpu.VMEM((2, 8, NB), F32),
+            pltpu.VMEM((2, 8, NB), F32),
+            pltpu.VMEM((2, 8, 2 * NB), F32),
+            pltpu.VMEM((2, 8, NB), F32),
         ),
     )(mine, other, filtered, core)
     return out[None, None], diag.reshape(width)

time: 159 us -> 152 us (0.956)
  Pallas kernels: 30.4 us -> 26.2 us
  blocking collectives: 65.4 us -> 63 us
    pallas_call x1, Pallas kernels: 21.5 us -> 17.3 us  [local(): call(functools.partial(finish_kernel, root), (half, shape(4, NB)), [VMEM]...]
    all_to_all x2 -> x4, blocking collectives: 65.4 us -> 63 us  [the longest x1 28.3 us: local(): part = lax.all_to_all(part.reshape(64, share), PLANE, 0, 0, tiled=True)]
where the time goes in v3:
time: 152 us
  blocking collectives  63 us (41%)
  starting transfers between devices  48 us (32%)
  Pallas kernels  26.2 us (17%)
  waiting for transfers between devices  8.73 us (6%)
  local copies, waits for them, and re-layouts  4.35 us (3%)
    ppermute x12, starting transfers between devices, exchange(): return lax.ppermute(v, axes, pairs)  38.4 us
    all_to_all x1, blocking collectives, local(): part = lax.all_to_all(part.reshape(64, share), PLANE, 0, 0, tiled=True)  28.3 us
    pallas_call x1, Pallas kernels, local(): call(functools.partial(finish_kernel, root), (half, shape(4, NB)), [VMEM]...  17.3 us
    all_to_all x1, blocking collectives, local(): lax.all_to_all(jnp.broadcast_to(total[None], (64, share)), PLANE, 0, 0, t...  15.1 us
    all_to_all x1, blocking collectives, local(): part = lax.all_to_all(summed.reshape(4, quarter, NB), 'x', 0, 0).sum(0)  11.4 us
    ppermute x2, starting transfers between devices, swap(): return lax.ppermute(v, 'c', [(0, 1), (1, 0)])  9.6 us
    all_to_all x1, blocking collectives, local(): mine = lax.all_to_all(jnp.broadcast_to(part, (4, quarter, NB)), 'x', 0, 0)  8.25 us
    ppermute x12, waiting for transfers between devices, exchange(): return lax.ppermute(v, axes, pairs)  6.44 us
  transfers between devices with their start and end apart: 14, of which 6 were waited for; matrix products, arithmetic and copies ran while one was open for 1% of the time, Pallas kernels for 1%

profile of v3, /device:TPU:1, one launch (start us, length us, event | category | flops | bytes accessed | tf_op | source)
XLA Modules:
  0.0 151.7 jit_solution(347642220706264850)
XLA Ops:
  0.6 0.7 collective-permute-start.3
  1.3 6.4 %collective-permute-start.2 = (bf16[384,512]{1,0:T(8,128)(2,1)}, bf16[384,512]{1,0:T(8,128)(2,1)S(1)}, u32[]{:S(2)}, u32[]{:S(2)}) collective-permute-start(bf16[384,512]{1,0:T(8,128)(2,1)} %bitcast.20), channel_id=1, source_target_pairs={{0,16},{16,0},{32,48},{48,32},{64,80},{80,64},{96,112},{112,96},{1... | collective-permute-start | bytes 1179656 | tf_op jit(solution)/shard_map/ppermute | solution.py:248
  7.7 4.3 %collective-permute-start.1 = (bf16[384,512]{1,0:T(8,128)(2,1)}, bf16[384,512]{1,0:T(8,128)(2,1)S(1)}, u32[]{:S(2)}, u32[]{:S(2)}) collective-permute-start(bf16[384,512]{1,0:T(8,128)(2,1)} %bitcast.21), channel_id=1, source_target_pairs={{1,2},{2,1},{3,4},{4,3},{5,6},{6,5},{7,8},{8,7},{9,10},{10,9},{11,... | collective-permute-start | bytes 1179656 | tf_op jit(solution)/shard_map/ppermute | solution.py:248
  12.1 1.9 %collective-permute-start = (bf16[384,512]{1,0:T(8,128)(2,1)}, bf16[384,512]{1,0:T(8,128)(2,1)S(1)}, u32[]{:S(2)}, u32[]{:S(2)}) collective-permute-start(bf16[384,512]{1,0:T(8,128)(2,1)} %bitcast.22), channel_id=1, source_target_pairs={{0,1},{1,0},{2,3},{3,2},{4,5},{5,4},{6,7},{7,6},{8,9},{9,8},{10,11... | collective-permute-start | bytes 1179656 | tf_op jit(solution)/shard_map/ppermute | solution.py:248
  14.0 0.8 copy.9.w_ref
  14.8 0.0 copy-start.3
  14.8 0.0 copy-start
  14.8 1.4 copy-done
  16.2 0.0 copy-start.2
  16.2 1.0 copy-done.2
  17.2 0.0 copy-start.1
  17.2 0.4 own_block.3.part_ref
  17.6 0.1 pad_add_fusion.i_ref
  17.7 0.0 collective-permute-done.3.h3
  17.7 0.0 collective-permute-done.2.h2
  17.7 0.0 collective-permute-done.1.h1
  17.7 0.0 collective-permute-done.h0
  17.7 0.0 copy-done.3
  17.7 0.9 copy-done.1
  18.6 1.5 %first.1 = (f32[384,512]{1,0:T(8,128)S(1)}, bf16[384,512]{1,0:T(8,128)(2,1)S(1)}) custom-call(f32[384,512]{1,0:T(8,128)S(1)} %own_block.3.part_ref, bf16[5,384,384]{2,1,0:T(8,128)(2,1)S(1)} %bitcast.14, s32[4]{0:T(128)S(1)} %bitcast.27, s32[4]{0:T(128)S(1)} %pad_add_fusion.i_ref, bf16[384,512]{1,0:T(8,128)(2,1)S(1)} %collective-permute-done.h0, ...), custom_call_target="tpu_custom_call" | custom-call | flops 603979776 | bytes 2097152 | tf_op jit(solution)/shard_map/first/pallas_call | solution.py:285
  20.1 0.7 collective-permute-start.7
  20.8 6.1 %collective-permute-start.6 = (bf16[384,512]{1,0:T(8,128)(2,1)S(1)}, bf16[384,512]{1,0:T(8,128)(2,1)S(1)}, u32[]{:S(2)}, u32[]{:S(2)}) collective-permute-start(bf16[384,512]{1,0:T(8,128)(2,1)S(1)} %get-tuple-element.9.v_ref), channel_id=1, source_target_pairs={{0,16},{16,0},{32,48},{48,32},{64,80},{80,64},{96,112},{112,96},{1... | collective-permute-start | bytes 1179656 | tf_op jit(solution)/shard_map/ppermute | solution.py:248
  26.9 4.1 %collective-permute-start.5 = (bf16[384,512]{1,0:T(8,128)(2,1)S(1)}, bf16[384,512]{1,0:T(8,128)(2,1)S(1)}, u32[]{:S(2)}, u32[]{:S(2)}) collective-permute-start(bf16[384,512]{1,0:T(8,128)(2,1)S(1)} %get-tuple-element.9.v_ref), channel_id=1, source_target_pairs={{1,2},{2,1},{3,4},{4,3},{5,6},{6,5},{7,8},{8,7},{9,10},{10,9},{11,... | collective-permute-start | bytes 1179656 | tf_op jit(solution)/shard_map/ppermute | solution.py:248
  31.0 1.9 %collective-permute-start.4 = (bf16[384,512]{1,0:T(8,128)(2,1)S(1)}, bf16[384,512]{1,0:T(8,128)(2,1)S(1)}, u32[]{:S(2)}, u32[]{:S(2)}) collective-permute-start(bf16[384,512]{1,0:T(8,128)(2,1)S(1)} %get-tuple-element.9.v_ref), channel_id=1, source_target_pairs={{0,1},{1,0},{2,3},{3,2},{4,5},{5,4},{6,7},{7,6},{8,9},{9,8},{10,11... | collective-permute-start | bytes 1179656 | tf_op jit(solution)/shard_map/ppermute | solution.py:248
  33.0 0.4 own_block.4.part_ref
  33.3 0.0 collective-permute-done.7.h3
  33.4 2.2 %collective-permute-done.6.h2 = bf16[384,512]{1,0:T(8,128)(2,1)S(1)} collective-permute-done((bf16[384,512]{1,0:T(8,128)(2,1)S(1)}, bf16[384,512]{1,0:T(8,128)(2,1)S(1)}, u32[]{:S(2)}, u32[]{:S(2)}) %collective-permute-start.6) | collective-permute-done | bytes 393248 | tf_op jit(solution)/shard_map/ppermute | solution.py:248
  35.6 0.9 collective-permute-done.5.h1
  36.5 0.0 collective-permute-done.4.h0
  36.5 1.6 %middle.1.v_ref = bf16[384,512]{1,0:T(8,128)(2,1)S(1)} custom-call(f32[384,512]{1,0:T(8,128)S(1)} %own_block.4.part_ref, bf16[5,384,384]{2,1,0:T(8,128)(2,1)S(1)} %bitcast.16, s32[4]{0:T(128)S(1)} %bitcast.28, s32[4]{0:T(128)S(1)} %pad_add_fusion.i_ref, bf16[384,512]{1,0:T(8,128)(2,1)S(1)} %collective-permute-done.4.h0, ...), custom_call_target="tpu_custom_call" | custom-call | flops 603979776 | bytes 2097152 | tf_op jit(solution)/shard_map/middle/pallas_call | solution.py:286
  38.1 0.7 collective-permute-start.11
  38.8 5.5 %collective-permute-start.10 = (bf16[384,512]{1,0:T(8,128)(2,1)S(1)}, bf16[384,512]{1,0:T(8,128)(2,1)S(1)}, u32[]{:S(2)}, u32[]{:S(2)}) collective-permute-start(bf16[384,512]{1,0:T(8,128)(2,1)S(1)} %middle.1.v_ref), channel_id=1, source_target_pairs={{0,16},{16,0},{32,48},{48,32},{64,80},{80,64},{96,112},{112,96},{1... | collective-permute-start | bytes 1179656 | tf_op jit(solution)/shard_map/ppermute | solution.py:248
  44.4 4.1 %collective-permute-start.9 = (bf16[384,512]{1,0:T(8,128)(2,1)S(1)}, bf16[384,512]{1,0:T(8,128)(2,1)S(1)}, u32[]{:S(2)}, u32[]{:S(2)}) collective-permute-start(bf16[384,512]{1,0:T(8,128)(2,1)S(1)} %middle.1.v_ref), channel_id=1, source_target_pairs={{1,2},{2,1},{3,4},{4,3},{5,6},{6,5},{7,8},{8,7},{9,10},{10,9},{11,... | collective-permute-start | bytes 1179656 | tf_op jit(solution)/shard_map/ppermute | solution.py:248
  48.5 1.9 %collective-permute-start.8 = (bf16[384,512]{1,0:T(8,128)(2,1)S(1)}, bf16[384,512]{1,0:T(8,128)(2,1)S(1)}, u32[]{:S(2)}, u32[]{:S(2)}) collective-permute-start(bf16[384,512]{1,0:T(8,128)(2,1)S(1)} %middle.1.v_ref), channel_id=1, source_target_pairs={{0,1},{1,0},{2,3},{3,2},{4,5},{5,4},{6,7},{7,6},{8,9},{9,8},{10,11... | collective-permute-start | bytes 1179656 | tf_op jit(solution)/shard_map/ppermute | solution.py:248
  50.4 0.4 own_block.5.part_ref
  50.8 0.0 collective-permute-done.11.h3
  50.8 2.4 %collective-permute-done.10.h2 = bf16[384,512]{1,0:T(8,128)(2,1)S(1)} collective-permute-done((bf16[384,512]{1,0:T(8,128)(2,1)S(1)}, bf16[384,512]{1,0:T(8,128)(2,1)S(1)}, u32[]{:S(2)}, u32[]{:S(2)}) %collective-permute-start.10) | collective-permute-done | bytes 393248 | tf_op jit(solution)/shard_map/ppermute | solution.py:248
  53.2 0.8 collective-permute-done.9.h1
  54.0 0.0 collective-permute-done.8.h0
  54.0 4.7 %last_and_correlation.1 = (f32[384,512]{1,0:T(8,128)S(1)}, f32[640,128]{1,0:T(8,128)S(1)}, f32[640,128]{1,0:T(8,128)S(1)}) custom-call(f32[384,512]{1,0:T(8,128)S(1)} %own_block.5.part_ref, bf16[5,384,384]{2,1,0:T(8,128)(2,1)S(1)} %bitcast.18, s32[4]{0:T(128)S(1)} %bitcast.29, s32[4]{0:T(128)S(1)} %pad_add_fusion.i_ref, ...), custom_call_target="tpu_custom_call" | custom-call | flops 1207959552 | bytes 2097152 | tf_op jit(solution)/shard_map/last_and_correlation/pallas_call | solution.py:288
  58.7 2.3 %collective-permute-start.12 = (f32[640,128]{1,0:T(8,128)S(1)}, f32[640,128]{1,0:T(8,128)S(1)}, u32[]{:S(2)}, u32[]{:S(2)}) collective-permute-start(f32[640,128]{1,0:T(8,128)S(1)} %get-tuple-element.12), channel_id=1, source_target_pairs={{0,1},{1,0},{2,3},{3,2},{4,5},{5,4},{6,7},{7,6},{8,9},{9,8},{10,11... | collective-permute-start | bytes 983048 | tf_op jit(solution)/shard_map/ppermute | solution.py:261
  61.0 1.2 collective-permute-done.12
  62.3 11.4 %all_to_all.25 = f32[4,160,128]{2,1,0:T(8,128)S(1)} all-to-all(f32[4,160,128]{2,1,0:T(8,128)S(1)} %bitcast.30), channel_id=1, replica_groups=mesh['z'=8,'x'=4,'y'=8,'c'=2] {'x'}, dimensions={0} | all-to-all | bytes 655360 | tf_op jit(solution)/shard_map/all_to_all | solution.py:295
  73.7 0.1 all_to_all.17
  73.8 28.3 %all_to_all.26 = f32[64,1,320]{2,1,0:T(1,128)S(1)} all-to-all(f32[64,1,320]{2,1,0:T(1,128)S(1)} %all_to_all.17), channel_id=1, replica_groups=mesh['z'=8,'x'=4,'y'=8,'c'=2] {'z','y'}, dimensions={0} | all-to-all | bytes 163840 | tf_op jit(solution)/shard_map/all_to_all | solution.py:296
  102.1 0.1 reduce_sum.19
  102.2 0.1 broadcast_in_dim.20
  102.3 15.1 %all_to_all.27 = f32[64,1,320]{2,1,0:T(1,128)S(1)} all-to-all(f32[64,1,320]{2,1,0:T(1,128)S(1)} %broadcast_in_dim.20), channel_id=1, replica_groups=mesh['z'=8,'x'=4,'y'=8,'c'=2] {'z','y'}, dimensions={0} | all-to-all | bytes 163840 | tf_op jit(solution)/shard_map/all_to_all | solution.py:298
  117.4 0.2 reduce.1
  117.6 0.1 broadcast_in_dim.21
  117.8 8.3 %all_to_all.28 = f32[4,160,128]{2,1,0:T(8,128)S(1)} all-to-all(f32[4,160,128]{2,1,0:T(8,128)S(1)} %broadcast_in_dim.22), channel_id=1, replica_groups=mesh['z'=8,'x'=4,'y'=8,'c'=2] {'x'}, dimensions={0} | all-to-all | bytes 655360 | tf_op jit(solution)/shard_map/all_to_all | solution.py:300
  126.0 7.3 %collective-permute-start.13 = (f32[640,128]{1,0:T(8,128)S(1)}, f32[640,128]{1,0:T(8,128)S(1)}, u32[]{:S(2)}, u32[]{:S(2)}) collective-permute-start(f32[640,128]{1,0:T(8,128)S(1)} %bitcast.25), channel_id=1, source_target_pairs={{0,1},{1,0},{2,3},{3,2},{4,5},{5,4},{6,7},{7,6},{8,9},{9,8},{10,11... | collective-permute-start | bytes 983048 | tf_op jit(solution)/shard_map/ppermute | solution.py:261
  133.3 1.1 collective-permute-done.13.other_ref
  134.4 17.3 %finish.1 = (bf16[384,512]{1,0:T(8,128)(2,1)}, f32[4,128]{1,0:T(4,128)}) custom-call(f32[640,128]{1,0:T(8,128)S(1)} %bitcast.26, f32[640,128]{1,0:T(8,128)S(1)} %collective-permute-done.13.other_ref, f32[384,512]{1,0:T(8,128)S(1)} %get-tuple-element.13.f_ref, s32[1]{0:T(128)} %bitcast.8.core_ref), custom_call_target="tpu_custom_call" | custom-call | flops 1207959552 | bytes 2097152 | tf_op jit(solution)/shard_map/finish/pallas_call | solution.py:305
  (3 shorter events, 0.1 us)
Async XLA Ops:
  0.6 17.0 %collective-permute-start.3 = (bf16[384,512]{1,0:T(8,128)(2,1)}, bf16[384,512]{1,0:T(8,128)(2,1)S(1)}, u32[]{:S(2)}, u32[]{:S(2)}) collective-permute-start(bf16[384,512]{1,0:T(8,128)(2,1)} %bitcast.19), channel_id=1, source_target_pairs={{16,32},{32,16},{48,64},{64,48},{80,96},{96,80},{112,128},{128,112... | collective-permute-start | bytes 1179656 | tf_op jit(solution)/shard_map/ppermute | solution.py:248
  1.3 16.3 %collective-permute-start.2 = (bf16[384,512]{1,0:T(8,128)(2,1)}, bf16[384,512]{1,0:T(8,128)(2,1)S(1)}, u32[]{:S(2)}, u32[]{:S(2)}) collective-permute-start(bf16[384,512]{1,0:T(8,128)(2,1)} %bitcast.20), channel_id=1, source_target_pairs={{0,16},{16,0},{32,48},{48,32},{64,80},{80,64},{96,112},{112,96},{1... | collective-permute-start | bytes 1179656 | tf_op jit(solution)/shard_map/ppermute | solution.py:248
  7.7 10.0 %collective-permute-start.1 = (bf16[384,512]{1,0:T(8,128)(2,1)}, bf16[384,512]{1,0:T(8,128)(2,1)S(1)}, u32[]{:S(2)}, u32[]{:S(2)}) collective-permute-start(bf16[384,512]{1,0:T(8,128)(2,1)} %bitcast.21), channel_id=1, source_target_pairs={{1,2},{2,1},{3,4},{4,3},{5,6},{6,5},{7,8},{8,7},{9,10},{10,9},{11,... | collective-permute-start | bytes 1179656 | tf_op jit(solution)/shard_map/ppermute | solution.py:248
  12.1 5.7 %collective-permute-start = (bf16[384,512]{1,0:T(8,128)(2,1)}, bf16[384,512]{1,0:T(8,128)(2,1)S(1)}, u32[]{:S(2)}, u32[]{:S(2)}) collective-permute-start(bf16[384,512]{1,0:T(8,128)(2,1)} %bitcast.22), channel_id=1, source_target_pairs={{0,1},{1,0},{2,3},{3,2},{4,5},{5,4},{6,7},{7,6},{8,9},{9,8},{10,11... | collective-permute-start | bytes 1179656 | tf_op jit(solution)/shard_map/ppermute | solution.py:248
  14.8 2.9 %copy-start.3 = (s32[1,1,4]{2,1,0:T(1,128)S(1)}, s32[1,1,4]{2,1,0:T(1,128)}, u32[]{:S(2)}) copy-start(s32[1,1,4]{2,1,0:T(1,128)} %param.7) | copy-start | bytes 52
  14.8 1.4 copy-start
  16.2 1.0 copy-start.2
  17.2 1.4 copy-start.1
  20.1 13.2 %collective-permute-start.7 = (bf16[384,512]{1,0:T(8,128)(2,1)S(1)}, bf16[384,512]{1,0:T(8,128)(2,1)S(1)}, u32[]{:S(2)}, u32[]{:S(2)}) collective-permute-start(bf16[384,512]{1,0:T(8,128)(2,1)S(1)} %get-tuple-element.9.v_ref), channel_id=1, source_target_pairs={{16,32},{32,16},{48,64},{64,48},{80,96},{96,80},{112,128},{128,112... | collective-permute-start | bytes 1179656 | tf_op jit(solution)/shard_map/ppermute | solution.py:248
  20.8 14.8 %collective-permute-start.6 = (bf16[384,512]{1,0:T(8,128)(2,1)S(1)}, bf16[384,512]{1,0:T(8,128)(2,1)S(1)}, u32[]{:S(2)}, u32[]{:S(2)}) collective-permute-start(bf16[384,512]{1,0:T(8,128)(2,1)S(1)} %get-tuple-element.9.v_ref), channel_id=1, source_target_pairs={{0,16},{16,0},{32,48},{48,32},{64,80},{80,64},{96,112},{112,96},{1... | collective-permute-start | bytes 1179656 | tf_op jit(solution)/shard_map/ppermute | solution.py:248
  26.9 9.7 %collective-permute-start.5 = (bf16[384,512]{1,0:T(8,128)(2,1)S(1)}, bf16[384,512]{1,0:T(8,128)(2,1)S(1)}, u32[]{:S(2)}, u32[]{:S(2)}) collective-permute-start(bf16[384,512]{1,0:T(8,128)(2,1)S(1)} %get-tuple-element.9.v_ref), channel_id=1, source_target_pairs={{1,2},{2,1},{3,4},{4,3},{5,6},{6,5},{7,8},{8,7},{9,10},{10,9},{11,... | collective-permute-start | bytes 1179656 | tf_op jit(solution)/shard_map/ppermute | solution.py:248
  31.0 5.5 %collective-permute-start.4 = (bf16[384,512]{1,0:T(8,128)(2,1)S(1)}, bf16[384,512]{1,0:T(8,128)(2,1)S(1)}, u32[]{:S(2)}, u32[]{:S(2)}) collective-permute-start(bf16[384,512]{1,0:T(8,128)(2,1)S(1)} %get-tuple-element.9.v_ref), channel_id=1, source_target_pairs={{0,1},{1,0},{2,3},{3,2},{4,5},{5,4},{6,7},{7,6},{8,9},{9,8},{10,11... | collective-permute-start | bytes 1179656 | tf_op jit(solution)/shard_map/ppermute | solution.py:248
  38.1 12.7 %collective-permute-start.11 = (bf16[384,512]{1,0:T(8,128)(2,1)S(1)}, bf16[384,512]{1,0:T(8,128)(2,1)S(1)}, u32[]{:S(2)}, u32[]{:S(2)}) collective-permute-start(bf16[384,512]{1,0:T(8,128)(2,1)S(1)} %middle.1.v_ref), channel_id=1, source_target_pairs={{16,32},{32,16},{48,64},{64,48},{80,96},{96,80},{112,128},{128,112... | collective-permute-start | bytes 1179656 | tf_op jit(solution)/shard_map/ppermute | solution.py:248
  38.8 14.4 %collective-permute-start.10 = (bf16[384,512]{1,0:T(8,128)(2,1)S(1)}, bf16[384,512]{1,0:T(8,128)(2,1)S(1)}, u32[]{:S(2)}, u32[]{:S(2)}) collective-permute-start(bf16[384,512]{1,0:T(8,128)(2,1)S(1)} %middle.1.v_ref), channel_id=1, source_target_pairs={{0,16},{16,0},{32,48},{48,32},{64,80},{80,64},{96,112},{112,96},{1... | collective-permute-start | bytes 1179656 | tf_op jit(solution)/shard_map/ppermute | solution.py:248
  44.4 9.7 %collective-permute-start.9 = (bf16[384,512]{1,0:T(8,128)(2,1)S(1)}, bf16[384,512]{1,0:T(8,128)(2,1)S(1)}, u32[]{:S(2)}, u32[]{:S(2)}) collective-permute-start(bf16[384,512]{1,0:T(8,128)(2,1)S(1)} %middle.1.v_ref), channel_id=1, source_target_pairs={{1,2},{2,1},{3,4},{4,3},{5,6},{6,5},{7,8},{8,7},{9,10},{10,9},{11,... | collective-permute-start | bytes 1179656 | tf_op jit(solution)/shard_map/ppermute | solution.py:248
  48.5 5.5 %collective-permute-start.8 = (bf16[384,512]{1,0:T(8,128)(2,1)S(1)}, bf16[384,512]{1,0:T(8,128)(2,1)S(1)}, u32[]{:S(2)}, u32[]{:S(2)}) collective-permute-start(bf16[384,512]{1,0:T(8,128)(2,1)S(1)} %middle.1.v_ref), channel_id=1, source_target_pairs={{0,1},{1,0},{2,3},{3,2},{4,5},{5,4},{6,7},{7,6},{8,9},{9,8},{10,11... | collective-permute-start | bytes 1179656 | tf_op jit(solution)/shard_map/ppermute | solution.py:248
  58.7 3.5 %collective-permute-start.12 = (f32[640,128]{1,0:T(8,128)S(1)}, f32[640,128]{1,0:T(8,128)S(1)}, u32[]{:S(2)}, u32[]{:S(2)}) collective-permute-start(f32[640,128]{1,0:T(8,128)S(1)} %get-tuple-element.12), channel_id=1, source_target_pairs={{0,1},{1,0},{2,3},{3,2},{4,5},{5,4},{6,7},{7,6},{8,9},{9,8},{10,11... | collective-permute-start | bytes 983048 | tf_op jit(solution)/shard_map/ppermute | solution.py:261
  126.0 8.4 %collective-permute-start.13 = (f32[640,128]{1,0:T(8,128)S(1)}, f32[640,128]{1,0:T(8,128)S(1)}, u32[]{:S(2)}, u32[]{:S(2)}) collective-permute-start(f32[640,128]{1,0:T(8,128)S(1)} %bitcast.25), channel_id=1, source_target_pairs={{0,1},{1,0},{2,3},{3,2},{4,5},{5,4},{6,7},{7,6},{8,9},{9,8},{10,11... | collective-permute-start | bytes 983048 | tf_op jit(solution)/shard_map/ppermute | solution.py:261

commit v4 on v3

--- a/solution.py
+++ b/solution.py
@@ -12,7 +12,6 @@
 CENTER = 1.25
 SCALE = 0.5
 NB = 128
-HIGHEST = lax.Precision.HIGHEST
 F32 = jnp.float32
 VMEM = pl.BlockSpec(memory_space=pltpu.VMEM)
 SMEM = pl.BlockSpec(memory_space=pltpu.SMEM)
@@ -22,14 +21,18 @@
 LIMIT = 12 * 2**20
 
 
-def dot(a, b, dims, precision=None):
-    return lax.dot_general(
-        a, b, (dims, ((), ())), precision=precision, preferred_element_type=F32
-    )
-
-
-def halo_product(c_ref, l_ref, index, h_ref):
-    return l_ref[index - 1].astype(F32) * dot(c_ref[index], h_ref[...], ((1,), (0,)))
+def dot(a, b, dims):
+    return lax.dot_general(a, b, (dims, ((), ())), preferred_element_type=F32)
+
+
+def halo_sum(c_ref, l_ref, i_ref, halos):
+    none = jnp.zeros(c_ref.shape[1:], c_ref.dtype)
+    left = []
+    for k in range(4):
+        index = i_ref[k]
+        left.append(jnp.where(l_ref[index - 1] != 0, c_ref[index], none))
+    right = jnp.concatenate([h[...] for h in halos], 0)
+    return dot(jnp.concatenate(left, 1), right, ((1,), (0,)))
 
 
 def own_kernel(v_ref, c_ref, w_ref, o_ref):
@@ -37,22 +40,15 @@
     o_ref[...] = (w_ref[...] - CENTER) * v.astype(F32) + dot(c_ref[0], v, ((1,), (0,)))
 
 
-def halo_sum(part_ref, c_ref, l_ref, i_ref, halos):
-    total = part_ref[...]
-    for d, h in enumerate(halos):
-        total = total + halo_product(c_ref, l_ref, i_ref[d], h)
-    return total
-
-
 def first_kernel(part_ref, c_ref, l_ref, i_ref, h0, h1, h2, h3, o_ref, r_ref):
-    out = SCALE * halo_sum(part_ref, c_ref, l_ref, i_ref, (h0, h1, h2, h3))
+    out = SCALE * (part_ref[...] + halo_sum(c_ref, l_ref, i_ref, (h0, h1, h2, h3)))
     o_ref[...] = out
     r_ref[...] = out.astype(jnp.bfloat16)
 
 
 def middle_kernel(part_ref, c_ref, l_ref, i_ref, h0, h1, h2, h3, p_ref, r_ref):
-    out = 2.0 * SCALE * halo_sum(part_ref, c_ref, l_ref, i_ref, (h0, h1, h2, h3)) - p_ref[...].astype(F32)
-    r_ref[...] = out.astype(jnp.bfloat16)
+    total = part_ref[...] + halo_sum(c_ref, l_ref, i_ref, (h0, h1, h2, h3))
+    r_ref[...] = (2.0 * SCALE * total - p_ref[...].astype(F32)).astype(jnp.bfloat16)
 
 
 def split(v):
@@ -62,39 +58,37 @@
     return high, middle, rest - middle
 
 
-def pieces(v):
-    return [p.astype(jnp.bfloat16) for p in split(v)]
-
-
-def product(a, b, dims):
-    total = dot(a[1], b[1], dims)
-    for i, k in ((0, 2), (2, 0), (0, 1), (1, 0), (0, 0)):
-        total = total + dot(a[i], b[k], dims)
-    return total
-
-
-def last_kernel(part_ref, c_ref, l_ref, i_ref, h0, h1, h2, h3, p_ref, core_ref, o_ref, keep_ref, send_ref):
-    out = 2.0 * SCALE * halo_sum(part_ref, c_ref, l_ref, i_ref, (h0, h1, h2, h3)) - p_ref[...]
+def stack(parts, axis):
+    return jnp.concatenate(parts, axis).astype(jnp.bfloat16)
+
+
+def left_stack(v, axis):
+    high, middle, low = split(v)
+    return stack([low, high, middle, middle, high, high], axis)
+
+
+def right_stack(v, axis):
+    high, middle, low = split(v)
+    return stack([high, low, middle, high, middle, high], axis)
+
+
+def last_kernel(part_ref, c_ref, l_ref, i_ref, h0, h1, h2, h3, p_ref, core_ref, *outs):
+    o_ref, keep_ref, send_ref, g_ref = outs
+    total = part_ref[...] + halo_sum(c_ref, l_ref, i_ref, (h0, h1, h2, h3))
+    out = 2.0 * SCALE * total - p_ref[...]
     o_ref[...] = out
-    right = pieces(out)
-    n = 0
-    for i in range(4):
-        left = pieces(out[:, i * NB : (i + 1) * NB].T)
-        g = product(left, [p[:, : (i + 1) * NB] for p in right], ((1,), (0,)))
-        for l in range(i + 1):
-            block = g[:, l * NB : (l + 1) * NB]
-            rows = slice((n % 5) * NB, (n % 5 + 1) * NB)
-            mine = core_ref[0] == n // 5
-
-            @pl.when(mine)
-            def _():
-                keep_ref[rows, :] = block
-
-            @pl.when(jnp.logical_not(mine))
-            def _():
-                send_ref[rows, :] = block
-
-            n += 1
+    left, right = left_stack(out, 0), right_stack(out, 0)
+    for i in (0, 2):
+        g = dot(left[:, i * NB : (i + 2) * NB], right[:, : (i + 2) * NB], ((0,), (0,)))
+        for r in range(i, i + 2):
+            for l in range(r + 1):
+                n = r * (r + 1) // 2 + l
+                block = g[(r - i) * NB : (r - i + 1) * NB, l * NB : (l + 1) * NB]
+                g_ref[n * NB : (n + 1) * NB, :] = block
+    count = 5 * NB
+    core = core_ref[0]
+    keep_ref[...] = g_ref[pl.ds(pl.multiple_of(core * count, NB), count), :]
+    send_ref[...] = g_ref[pl.ds(pl.multiple_of((1 - core) * count, NB), count), :]
 
 
 def shape(*dims, dtype=F32):
@@ -125,7 +119,7 @@
     return jnp.broadcast_to(ref[i : i + 1, :], (8, NB))
 
 
-def leaf(a, z_ref, d_ref, col_buf, a_buf, z_buf, right_buf, left_buf, hook):
+def leaf(a, z_ref, d_ref, col_buf, next_buf, a_buf, z_buf, right_buf, left_buf, hook):
     lane = lax.broadcasted_iota(jnp.int32, (8, NB), 1)
     sub = lax.broadcasted_iota(jnp.int32, (8, NB), 0)
     z = [(lane == sub + 8 * r).astype(F32) for r in range(16)]
@@ -133,14 +127,18 @@
     for m in range(16):
         k0, p = 8 * m, m % 2
         near = range(m + 1, min(m + 1 + NEAR, 16))
+        if m == 0:
+            cols = [lanes(a[0], j) for j in range(8)]
         for j in range(8):
-            col_buf[p, j] = lanes(a[m], k0 + j)
+            col_buf[p, j] = cols[j]
         a_buf[p] = a[m]
         z_buf[p] = z[m]
         s = {(i, j): row(col_buf.at[p, j], i) for i in range(8) for j in range(i, 8)}
         rb = [row(a_buf.at[p], j) for j in range(8)]
         zb = [row(z_buf.at[p], j) for j in range(8)]
         cr = {r: [lanes(a[r], k0 + j) for j in range(8)] for r in near}
+        if m < 15:
+            cols = [lanes(a[m + 1], k0 + 8 + j) for j in range(8)]
         for j in range(8):
             inv = 1.0 / s[j, j]
             for jj in range(j + 1, 8):
@@ -151,6 +149,10 @@
                 zb[jj] = zb[jj] - f * zb[j]
             for r in near:
                 low = cr[r][j] * inv
+                if r == m + 1:
+                    next_buf[p, j] = cr[r][j]
+                    for jj in range(8):
+                        cols[jj] = cols[jj] - low * row(next_buf.at[p, j], jj)
                 for jj in range(j + 1, 8):
                     cr[r][jj] = cr[r][jj] - low * s[j, jj]
                 a[r] = a[r] - low * rb[j]
@@ -163,14 +165,16 @@
             z_ref[k0 + j : k0 + j + 1, :] = (zb[j] * rs)[0:1]
             diag = jnp.where(lane == k0 + j, s[j, j] * rs, diag)
         if m + 1 + NEAR < 16:
-            lh, lm, ll = split(left_buf[p])
-            rh, rm, rl = split(right_buf[p])
-            left = jnp.concatenate([lh, lh, lm, lm, lh, ll], 0).astype(jnp.bfloat16)
-            right = jnp.concatenate([rh, rm, rh, rm, rl, rh], 0).astype(jnp.bfloat16)
-            change = dot(left, right, ((0,), (0,)))
+            lo = 8 * (m + 1 + NEAR) // 16 * 16
+            across = lax.broadcasted_iota(jnp.int32, (NB - lo, NB), 1)
+            down = lax.broadcasted_iota(jnp.int32, (NB - lo, NB), 0)
+            unit = (across == down + lo).astype(F32).astype(jnp.bfloat16)
+            left = dot(unit, left_stack(left_buf[p], 0), ((1,), (1,))).astype(jnp.bfloat16)
+            change = dot(left, right_stack(right_buf[p], 0), ((1,), (0,)))
             for r in range(m + 1 + NEAR, 16):
-                a[r] = a[r] - change[8 * r : 8 * r + 8, :NB]
-                z[r] = z[r] - change[8 * r : 8 * r + 8, NB:]
+                at = slice(8 * r - lo, 8 * r - lo + 8)
+                a[r] = a[r] - change[at, :NB]
+                z[r] = z[r] - change[at, NB:]
         hook(m)
     d_ref[...] = diag[0:1]
 
@@ -200,15 +204,17 @@
         w_ref[l, rows(i), :] = v
         stored.add((i, l))
 
+    def product(a, b):
+        return dot(left_stack(a, 1), right_stack(b, 1), ((1,), (1,)))
+
     def panel(i, j):
-        v = dot(get(i, j), z_ref[j], ((1,), (1,)), HIGHEST)
+        v = product(get(i, j), z_ref[j])
         put(i, j, v)
         if i >= 4:
             o_ref[rows(i - 4), rows(j)] = (v * root).astype(jnp.bfloat16)
 
     def update(i, l, j):
-        change = dot(w_ref[j, rows(i), :], w_ref[j, rows(l), :], ((1,), (1,)), HIGHEST)
-        put(i, l, get(i, l) - change)
+        put(i, l, get(i, l) - product(w_ref[j, rows(i), :], w_ref[j, rows(l), :]))
 
     queue = []
 
@@ -277,16 +283,22 @@
 
     own = call(own_kernel, full, [VMEM] * 3, "own_block", flops)
 
+    specs = [VMEM] * 2 + [SMEM] * 2 + [VMEM] * 4
+
     def operands(v):
         halos = neighbours(v)
         return (own(v, blocks, weights), blocks, present, index, *halos)
 
-    specs = [VMEM, VMEM, SMEM, SMEM] + [VMEM] * 4
     x1, r1 = call(first_kernel, (full, half), specs, "first", 4 * flops)(*operands(v0))
     r2 = call(middle_kernel, half, specs + [VMEM], "middle", 4 * flops)(*operands(r1), v0)
     piece = shape(5 * NB, NB)
     filtered, keep, send = call(
-        last_kernel, (full, piece, piece), specs + [VMEM, SMEM], "last_and_correlation", 8 * flops
+        last_kernel,
+        (full, piece, piece),
+        specs + [VMEM, SMEM],
+        "last_and_correlation",
+        8 * flops,
+        (pltpu.VMEM((10 * NB, NB), F32),),
     )(*operands(r2), x1, core)
 
     summed = keep + swap(send)
@@ -313,6 +325,7 @@
             pltpu.VMEM((4, NB, NB), F32),
             pltpu.VMEM((1, NB), F32),
             pltpu.VMEM((2, 8, 8, NB), F32),
+            pltpu.VMEM((2, 8, 8, NB), F32),
             pltpu.VMEM((2, 8, NB), F32),
             pltpu.VMEM((2, 8, NB), F32),
             pltpu.VMEM((2, 8, 2 * NB), F32),

time: 152 us -> 147 us (0.967)
  Pallas kernels: 26.2 us -> 20.4 us
    pallas_call x1, Pallas kernels: 17.3 us -> 14.3 us  [local(): call(functools.partial(finish_kernel, root), (half, shape(4, NB)), [VMEM]...]
    pallas_call x1, Pallas kernels: 4.67 us -> 2.44 us  [local(): call(last_kernel, (full, piece, piece), specs + [VMEM, SMEM], 'last_and_c...]
where the time goes in v4:
time: 147 us; the launch traced here: 146 us
  blocking collectives  63.1 us (43%)
  starting transfers between devices  48.1 us (33%)
  Pallas kernels  20.4 us (14%)
  waiting for transfers between devices  8.74 us (6%)
  local copies, waits for them, and re-layouts  4.35 us (3%)
    ppermute x12, starting transfers between devices, exchange(): return lax.ppermute(v, axes, pairs)  38.4 us
    all_to_all x1, blocking collectives, local(): part = lax.all_to_all(part.reshape(64, share), PLANE, 0, 0, tiled=True)  28.3 us
    all_to_all x1, blocking collectives, local(): lax.all_to_all(jnp.broadcast_to(total[None], (64, share)), PLANE, 0, 0, t...  15.1 us
    pallas_call x1, Pallas kernels, local(): call(functools.partial(finish_kernel, root), (half, shape(4, NB)), [VMEM]...  14.3 us
    all_to_all x1, blocking collectives, local(): part = lax.all_to_all(summed.reshape(4, quarter, NB), 'x', 0, 0).sum(0)  11.4 us
    ppermute x2, starting transfers between devices, swap(): return lax.ppermute(v, 'c', [(0, 1), (1, 0)])  9.62 us
    all_to_all x1, blocking collectives, local(): mine = lax.all_to_all(jnp.broadcast_to(part, (4, quarter, NB)), 'x', 0, 0)  8.25 us
    ppermute x12, waiting for transfers between devices, exchange(): return lax.ppermute(v, axes, pairs)  6.45 us
  transfers between devices with their start and end apart: 14, of which 6 were waited for; matrix products, arithmetic and copies ran while one was open for 1% of the time, Pallas kernels for 1%

profile of v4, /device:TPU:1, one launch (start us, length us, event | category | flops | bytes accessed | tf_op | source)
XLA Modules:
  0.0 146.0 jit_solution(11948510874423125005)
XLA Ops:
  0.6 0.7 collective-permute-start.3
  1.3 6.4 %collective-permute-start.2 = (bf16[384,512]{1,0:T(8,128)(2,1)}, bf16[384,512]{1,0:T(8,128)(2,1)S(1)}, u32[]{:S(2)}, u32[]{:S(2)}) collective-permute-start(bf16[384,512]{1,0:T(8,128)(2,1)} %bitcast.20), channel_id=1, source_target_pairs={{0,16},{16,0},{32,48},{48,32},{64,80},{80,64},{96,112},{112,96},{1... | collective-permute-start | bytes 1179656 | tf_op jit(solution)/shard_map/ppermute | solution.py:254
  7.7 4.3 %collective-permute-start.1 = (bf16[384,512]{1,0:T(8,128)(2,1)}, bf16[384,512]{1,0:T(8,128)(2,1)S(1)}, u32[]{:S(2)}, u32[]{:S(2)}) collective-permute-start(bf16[384,512]{1,0:T(8,128)(2,1)} %bitcast.21), channel_id=1, source_target_pairs={{1,2},{2,1},{3,4},{4,3},{5,6},{6,5},{7,8},{8,7},{9,10},{10,9},{11,... | collective-permute-start | bytes 1179656 | tf_op jit(solution)/shard_map/ppermute | solution.py:254
  12.1 1.9 %collective-permute-start = (bf16[384,512]{1,0:T(8,128)(2,1)}, bf16[384,512]{1,0:T(8,128)(2,1)S(1)}, u32[]{:S(2)}, u32[]{:S(2)}) collective-permute-start(bf16[384,512]{1,0:T(8,128)(2,1)} %bitcast.22), channel_id=1, source_target_pairs={{0,1},{1,0},{2,3},{3,2},{4,5},{5,4},{6,7},{7,6},{8,9},{9,8},{10,11... | collective-permute-start | bytes 1179656 | tf_op jit(solution)/shard_map/ppermute | solution.py:254
  14.0 0.8 copy.9.w_ref
  14.8 0.0 copy-start.3
  14.8 0.0 copy-start
  14.8 1.4 copy-done
  16.2 0.0 copy-start.2
  16.2 1.0 copy-done.2
  17.2 0.0 copy-start.1
  17.2 0.4 own_block.3.part_ref
  17.6 0.1 pad_add_fusion.i_ref
  17.7 0.0 collective-permute-done.3.h3
  17.7 0.0 collective-permute-done.2.h2
  17.7 0.0 collective-permute-done.1.h1
  17.7 0.0 collective-permute-done.h0
  17.7 0.0 copy-done.3
  17.7 0.9 copy-done.1
  18.6 1.3 first.1
  19.9 0.7 collective-permute-start.7
  20.6 6.1 %collective-permute-start.6 = (bf16[384,512]{1,0:T(8,128)(2,1)S(1)}, bf16[384,512]{1,0:T(8,128)(2,1)S(1)}, u32[]{:S(2)}, u32[]{:S(2)}) collective-permute-start(bf16[384,512]{1,0:T(8,128)(2,1)S(1)} %get-tuple-element.9.v_ref), channel_id=1, source_target_pairs={{0,16},{16,0},{32,48},{48,32},{64,80},{80,64},{96,112},{112,96},{1... | collective-permute-start | bytes 1179656 | tf_op jit(solution)/shard_map/ppermute | solution.py:254
  26.7 4.1 %collective-permute-start.5 = (bf16[384,512]{1,0:T(8,128)(2,1)S(1)}, bf16[384,512]{1,0:T(8,128)(2,1)S(1)}, u32[]{:S(2)}, u32[]{:S(2)}) collective-permute-start(bf16[384,512]{1,0:T(8,128)(2,1)S(1)} %get-tuple-element.9.v_ref), channel_id=1, source_target_pairs={{1,2},{2,1},{3,4},{4,3},{5,6},{6,5},{7,8},{8,7},{9,10},{10,9},{11,... | collective-permute-start | bytes 1179656 | tf_op jit(solution)/shard_map/ppermute | solution.py:254
  30.8 1.9 %collective-permute-start.4 = (bf16[384,512]{1,0:T(8,128)(2,1)S(1)}, bf16[384,512]{1,0:T(8,128)(2,1)S(1)}, u32[]{:S(2)}, u32[]{:S(2)}) collective-permute-start(bf16[384,512]{1,0:T(8,128)(2,1)S(1)} %get-tuple-element.9.v_ref), channel_id=1, source_target_pairs={{0,1},{1,0},{2,3},{3,2},{4,5},{5,4},{6,7},{7,6},{8,9},{9,8},{10,11... | collective-permute-start | bytes 1179656 | tf_op jit(solution)/shard_map/ppermute | solution.py:254
  32.7 0.4 own_block.4.part_ref
  33.1 0.0 collective-permute-done.7.h3
  33.1 2.2 %collective-permute-done.6.h2 = bf16[384,512]{1,0:T(8,128)(2,1)S(1)} collective-permute-done((bf16[384,512]{1,0:T(8,128)(2,1)S(1)}, bf16[384,512]{1,0:T(8,128)(2,1)S(1)}, u32[]{:S(2)}, u32[]{:S(2)}) %collective-permute-start.6) | collective-permute-done | bytes 393248 | tf_op jit(solution)/shard_map/ppermute | solution.py:254
  35.4 0.9 collective-permute-done.5.h1
  36.3 0.0 collective-permute-done.4.h0
  36.3 1.3 middle.1.v_ref
  37.6 0.7 collective-permute-start.11
  38.3 5.5 %collective-permute-start.10 = (bf16[384,512]{1,0:T(8,128)(2,1)S(1)}, bf16[384,512]{1,0:T(8,128)(2,1)S(1)}, u32[]{:S(2)}, u32[]{:S(2)}) collective-permute-start(bf16[384,512]{1,0:T(8,128)(2,1)S(1)} %middle.1.v_ref), channel_id=1, source_target_pairs={{0,16},{16,0},{32,48},{48,32},{64,80},{80,64},{96,112},{112,96},{1... | collective-permute-start | bytes 1179656 | tf_op jit(solution)/shard_map/ppermute | solution.py:254
  43.9 4.1 %collective-permute-start.9 = (bf16[384,512]{1,0:T(8,128)(2,1)S(1)}, bf16[384,512]{1,0:T(8,128)(2,1)S(1)}, u32[]{:S(2)}, u32[]{:S(2)}) collective-permute-start(bf16[384,512]{1,0:T(8,128)(2,1)S(1)} %middle.1.v_ref), channel_id=1, source_target_pairs={{1,2},{2,1},{3,4},{4,3},{5,6},{6,5},{7,8},{8,7},{9,10},{10,9},{11,... | collective-permute-start | bytes 1179656 | tf_op jit(solution)/shard_map/ppermute | solution.py:254
  48.0 1.9 %collective-permute-start.8 = (bf16[384,512]{1,0:T(8,128)(2,1)S(1)}, bf16[384,512]{1,0:T(8,128)(2,1)S(1)}, u32[]{:S(2)}, u32[]{:S(2)}) collective-permute-start(bf16[384,512]{1,0:T(8,128)(2,1)S(1)} %middle.1.v_ref), channel_id=1, source_target_pairs={{0,1},{1,0},{2,3},{3,2},{4,5},{5,4},{6,7},{7,6},{8,9},{9,8},{10,11... | collective-permute-start | bytes 1179656 | tf_op jit(solution)/shard_map/ppermute | solution.py:254
  50.0 0.4 own_block.5.part_ref
  50.3 0.0 collective-permute-done.11.h3
  50.4 2.4 %collective-permute-done.10.h2 = bf16[384,512]{1,0:T(8,128)(2,1)S(1)} collective-permute-done((bf16[384,512]{1,0:T(8,128)(2,1)S(1)}, bf16[384,512]{1,0:T(8,128)(2,1)S(1)}, u32[]{:S(2)}, u32[]{:S(2)}) %collective-permute-start.10) | collective-permute-done | bytes 393248 | tf_op jit(solution)/shard_map/ppermute | solution.py:254
  52.7 0.8 collective-permute-done.9.h1
  53.6 0.0 collective-permute-done.8.h0
  53.6 2.4 %last_and_correlation.1 = (f32[384,512]{1,0:T(8,128)S(1)}, f32[640,128]{1,0:T(8,128)S(1)}, f32[640,128]{1,0:T(8,128)S(1)}) custom-call(f32[384,512]{1,0:T(8,128)S(1)} %own_block.5.part_ref, bf16[5,384,384]{2,1,0:T(8,128)(2,1)S(1)} %bitcast.18, s32[4]{0:T(128)S(1)} %bitcast.29, s32[4]{0:T(128)S(1)} %pad_add_fusion.i_ref, ...), custom_call_target="tpu_custom_call" | custom-call | flops 1207959552 | bytes 2097152 | tf_op jit(solution)/shard_map/last_and_correlation/pallas_call | solution.py:295
  56.0 2.3 %collective-permute-start.12 = (f32[640,128]{1,0:T(8,128)S(1)}, f32[640,128]{1,0:T(8,128)S(1)}, u32[]{:S(2)}, u32[]{:S(2)}) collective-permute-start(f32[640,128]{1,0:T(8,128)S(1)} %get-tuple-element.12), channel_id=1, source_target_pairs={{0,1},{1,0},{2,3},{3,2},{4,5},{5,4},{6,7},{7,6},{8,9},{9,8},{10,11... | collective-permute-start | bytes 983048 | tf_op jit(solution)/shard_map/ppermute | solution.py:267
  58.3 1.2 collective-permute-done.12
  59.6 11.4 %all_to_all.25 = f32[4,160,128]{2,1,0:T(8,128)S(1)} all-to-all(f32[4,160,128]{2,1,0:T(8,128)S(1)} %bitcast.30), channel_id=1, replica_groups=mesh['z'=8,'x'=4,'y'=8,'c'=2] {'x'}, dimensions={0} | all-to-all | bytes 655360 | tf_op jit(solution)/shard_map/all_to_all | solution.py:307
  71.0 0.1 all_to_all.17
  71.1 28.3 %all_to_all.26 = f32[64,1,320]{2,1,0:T(1,128)S(1)} all-to-all(f32[64,1,320]{2,1,0:T(1,128)S(1)} %all_to_all.17), channel_id=1, replica_groups=mesh['z'=8,'x'=4,'y'=8,'c'=2] {'z','y'}, dimensions={0} | all-to-all | bytes 163840 | tf_op jit(solution)/shard_map/all_to_all | solution.py:308
  99.4 0.1 reduce_sum.19
  99.6 0.1 broadcast_in_dim.20
  99.6 15.1 %all_to_all.27 = f32[64,1,320]{2,1,0:T(1,128)S(1)} all-to-all(f32[64,1,320]{2,1,0:T(1,128)S(1)} %broadcast_in_dim.20), channel_id=1, replica_groups=mesh['z'=8,'x'=4,'y'=8,'c'=2] {'z','y'}, dimensions={0} | all-to-all | bytes 163840 | tf_op jit(solution)/shard_map/all_to_all | solution.py:310
  114.7 0.2 reduce.1
  115.0 0.1 broadcast_in_dim.21
  115.1 8.3 %all_to_all.28 = f32[4,160,128]{2,1,0:T(8,128)S(1)} all-to-all(f32[4,160,128]{2,1,0:T(8,128)S(1)} %broadcast_in_dim.22), channel_id=1, replica_groups=mesh['z'=8,'x'=4,'y'=8,'c'=2] {'x'}, dimensions={0} | all-to-all | bytes 655360 | tf_op jit(solution)/shard_map/all_to_all | solution.py:312
  123.3 7.3 %collective-permute-start.13 = (f32[640,128]{1,0:T(8,128)S(1)}, f32[640,128]{1,0:T(8,128)S(1)}, u32[]{:S(2)}, u32[]{:S(2)}) collective-permute-start(f32[640,128]{1,0:T(8,128)S(1)} %bitcast.25), channel_id=1, source_target_pairs={{0,1},{1,0},{2,3},{3,2},{4,5},{5,4},{6,7},{7,6},{8,9},{9,8},{10,11... | collective-permute-start | bytes 983048 | tf_op jit(solution)/shard_map/ppermute | solution.py:267
  130.7 1.1 collective-permute-done.13.other_ref
  131.7 14.3 %finish.1 = (bf16[384,512]{1,0:T(8,128)(2,1)}, f32[4,128]{1,0:T(4,128)}) custom-call(f32[640,128]{1,0:T(8,128)S(1)} %bitcast.26, f32[640,128]{1,0:T(8,128)S(1)} %collective-permute-done.13.other_ref, f32[384,512]{1,0:T(8,128)S(1)} %get-tuple-element.13.f_ref, s32[1]{0:T(128)} %bitcast.8.core_ref), custom_call_target="tpu_custom_call" | custom-call | flops 1207959552 | bytes 2097152 | tf_op jit(solution)/shard_map/finish/pallas_call | solution.py:317
  (3 shorter events, 0.1 us)
Async XLA Ops:
  0.6 17.0 %collective-permute-start.3 = (bf16[384,512]{1,0:T(8,128)(2,1)}, bf16[384,512]{1,0:T(8,128)(2,1)S(1)}, u32[]{:S(2)}, u32[]{:S(2)}) collective-permute-start(bf16[384,512]{1,0:T(8,128)(2,1)} %bitcast.19), channel_id=1, source_target_pairs={{16,32},{32,16},{48,64},{64,48},{80,96},{96,80},{112,128},{128,112... | collective-permute-start | bytes 1179656 | tf_op jit(solution)/shard_map/ppermute | solution.py:254
  1.3 16.3 %collective-permute-start.2 = (bf16[384,512]{1,0:T(8,128)(2,1)}, bf16[384,512]{1,0:T(8,128)(2,1)S(1)}, u32[]{:S(2)}, u32[]{:S(2)}) collective-permute-start(bf16[384,512]{1,0:T(8,128)(2,1)} %bitcast.20), channel_id=1, source_target_pairs={{0,16},{16,0},{32,48},{48,32},{64,80},{80,64},{96,112},{112,96},{1... | collective-permute-start | bytes 1179656 | tf_op jit(solution)/shard_map/ppermute | solution.py:254
  7.7 10.0 %collective-permute-start.1 = (bf16[384,512]{1,0:T(8,128)(2,1)}, bf16[384,512]{1,0:T(8,128)(2,1)S(1)}, u32[]{:S(2)}, u32[]{:S(2)}) collective-permute-start(bf16[384,512]{1,0:T(8,128)(2,1)} %bitcast.21), channel_id=1, source_target_pairs={{1,2},{2,1},{3,4},{4,3},{5,6},{6,5},{7,8},{8,7},{9,10},{10,9},{11,... | collective-permute-start | bytes 1179656 | tf_op jit(solution)/shard_map/ppermute | solution.py:254
  12.1 5.7 %collective-permute-start = (bf16[384,512]{1,0:T(8,128)(2,1)}, bf16[384,512]{1,0:T(8,128)(2,1)S(1)}, u32[]{:S(2)}, u32[]{:S(2)}) collective-permute-start(bf16[384,512]{1,0:T(8,128)(2,1)} %bitcast.22), channel_id=1, source_target_pairs={{0,1},{1,0},{2,3},{3,2},{4,5},{5,4},{6,7},{7,6},{8,9},{9,8},{10,11... | collective-permute-start | bytes 1179656 | tf_op jit(solution)/shard_map/ppermute | solution.py:254
  14.8 2.9 %copy-start.3 = (s32[1,1,4]{2,1,0:T(1,128)S(1)}, s32[1,1,4]{2,1,0:T(1,128)}, u32[]{:S(2)}) copy-start(s32[1,1,4]{2,1,0:T(1,128)} %param.7) | copy-start | bytes 52
  14.8 1.4 copy-start
  16.2 1.0 copy-start.2
  17.2 1.4 copy-start.1
  19.9 13.2 %collective-permute-start.7 = (bf16[384,512]{1,0:T(8,128)(2,1)S(1)}, bf16[384,512]{1,0:T(8,128)(2,1)S(1)}, u32[]{:S(2)}, u32[]{:S(2)}) collective-permute-start(bf16[384,512]{1,0:T(8,128)(2,1)S(1)} %get-tuple-element.9.v_ref), channel_id=1, source_target_pairs={{16,32},{32,16},{48,64},{64,48},{80,96},{96,80},{112,128},{128,112... | collective-permute-start | bytes 1179656 | tf_op jit(solution)/shard_map/ppermute | solution.py:254
  20.6 14.8 %collective-permute-start.6 = (bf16[384,512]{1,0:T(8,128)(2,1)S(1)}, bf16[384,512]{1,0:T(8,128)(2,1)S(1)}, u32[]{:S(2)}, u32[]{:S(2)}) collective-permute-start(bf16[384,512]{1,0:T(8,128)(2,1)S(1)} %get-tuple-element.9.v_ref), channel_id=1, source_target_pairs={{0,16},{16,0},{32,48},{48,32},{64,80},{80,64},{96,112},{112,96},{1... | collective-permute-start | bytes 1179656 | tf_op jit(solution)/shard_map/ppermute | solution.py:254
  26.7 9.7 %collective-permute-start.5 = (bf16[384,512]{1,0:T(8,128)(2,1)S(1)}, bf16[384,512]{1,0:T(8,128)(2,1)S(1)}, u32[]{:S(2)}, u32[]{:S(2)}) collective-permute-start(bf16[384,512]{1,0:T(8,128)(2,1)S(1)} %get-tuple-element.9.v_ref), channel_id=1, source_target_pairs={{1,2},{2,1},{3,4},{4,3},{5,6},{6,5},{7,8},{8,7},{9,10},{10,9},{11,... | collective-permute-start | bytes 1179656 | tf_op jit(solution)/shard_map/ppermute | solution.py:254
  30.8 5.5 %collective-permute-start.4 = (bf16[384,512]{1,0:T(8,128)(2,1)S(1)}, bf16[384,512]{1,0:T(8,128)(2,1)S(1)}, u32[]{:S(2)}, u32[]{:S(2)}) collective-permute-start(bf16[384,512]{1,0:T(8,128)(2,1)S(1)} %get-tuple-element.9.v_ref), channel_id=1, source_target_pairs={{0,1},{1,0},{2,3},{3,2},{4,5},{5,4},{6,7},{7,6},{8,9},{9,8},{10,11... | collective-permute-start | bytes 1179656 | tf_op jit(solution)/shard_map/ppermute | solution.py:254
  37.6 12.7 %collective-permute-start.11 = (bf16[384,512]{1,0:T(8,128)(2,1)S(1)}, bf16[384,512]{1,0:T(8,128)(2,1)S(1)}, u32[]{:S(2)}, u32[]{:S(2)}) collective-permute-start(bf16[384,512]{1,0:T(8,128)(2,1)S(1)} %middle.1.v_ref), channel_id=1, source_target_pairs={{16,32},{32,16},{48,64},{64,48},{80,96},{96,80},{112,128},{128,112... | collective-permute-start | bytes 1179656 | tf_op jit(solution)/shard_map/ppermute | solution.py:254
  38.3 14.4 %collective-permute-start.10 = (bf16[384,512]{1,0:T(8,128)(2,1)S(1)}, bf16[384,512]{1,0:T(8,128)(2,1)S(1)}, u32[]{:S(2)}, u32[]{:S(2)}) collective-permute-start(bf16[384,512]{1,0:T(8,128)(2,1)S(1)} %middle.1.v_ref), channel_id=1, source_target_pairs={{0,16},{16,0},{32,48},{48,32},{64,80},{80,64},{96,112},{112,96},{1... | collective-permute-start | bytes 1179656 | tf_op jit(solution)/shard_map/ppermute | solution.py:254
  43.9 9.7 %collective-permute-start.9 = (bf16[384,512]{1,0:T(8,128)(2,1)S(1)}, bf16[384,512]{1,0:T(8,128)(2,1)S(1)}, u32[]{:S(2)}, u32[]{:S(2)}) collective-permute-start(bf16[384,512]{1,0:T(8,128)(2,1)S(1)} %middle.1.v_ref), channel_id=1, source_target_pairs={{1,2},{2,1},{3,4},{4,3},{5,6},{6,5},{7,8},{8,7},{9,10},{10,9},{11,... | collective-permute-start | bytes 1179656 | tf_op jit(solution)/shard_map/ppermute | solution.py:254
  48.0 5.5 %collective-permute-start.8 = (bf16[384,512]{1,0:T(8,128)(2,1)S(1)}, bf16[384,512]{1,0:T(8,128)(2,1)S(1)}, u32[]{:S(2)}, u32[]{:S(2)}) collective-permute-start(bf16[384,512]{1,0:T(8,128)(2,1)S(1)} %middle.1.v_ref), channel_id=1, source_target_pairs={{0,1},{1,0},{2,3},{3,2},{4,5},{5,4},{6,7},{7,6},{8,9},{9,8},{10,11... | collective-permute-start | bytes 1179656 | tf_op jit(solution)/shard_map/ppermute | solution.py:254
  56.0 3.6 %collective-permute-start.12 = (f32[640,128]{1,0:T(8,128)S(1)}, f32[640,128]{1,0:T(8,128)S(1)}, u32[]{:S(2)}, u32[]{:S(2)}) collective-permute-start(f32[640,128]{1,0:T(8,128)S(1)} %get-tuple-element.12), channel_id=1, source_target_pairs={{0,1},{1,0},{2,3},{3,2},{4,5},{5,4},{6,7},{7,6},{8,9},{9,8},{10,11... | collective-permute-start | bytes 983048 | tf_op jit(solution)/shard_map/ppermute | solution.py:267
  123.3 8.4 %collective-permute-start.13 = (f32[640,128]{1,0:T(8,128)S(1)}, f32[640,128]{1,0:T(8,128)S(1)}, u32[]{:S(2)}, u32[]{:S(2)}) collective-permute-start(f32[640,128]{1,0:T(8,128)S(1)} %bitcast.25), channel_id=1, source_target_pairs={{0,1},{1,0},{2,3},{3,2},{4,5},{5,4},{6,7},{7,6},{8,9},{9,8},{10,11... | collective-permute-start | bytes 983048 | tf_op jit(solution)/shard_map/ppermute | solution.py:267

commit v5 on v4

--- a/solution.py
+++ b/solution.py
@@ -17,7 +17,6 @@
 SMEM = pl.BlockSpec(memory_space=pltpu.SMEM)
 GX = ("z", "x")
 GY = ("y", "c")
-PLANE = ("z", "y")
 LIMIT = 12 * 2**20
 
 
@@ -302,14 +301,12 @@
     )(*operands(r2), x1, core)
 
     summed = keep + swap(send)
-    quarter = 5 * NB // 4
-    share = quarter * NB // 64
-    part = lax.all_to_all(summed.reshape(4, quarter, NB), "x", 0, 0).sum(0)
-    part = lax.all_to_all(part.reshape(64, share), PLANE, 0, 0, tiled=True)
-    total = part.reshape(64, share).sum(0)
-    part = lax.all_to_all(jnp.broadcast_to(total[None], (64, share)), PLANE, 0, 0, tiled=True)
-    part = part.reshape(1, quarter, NB)
-    mine = lax.all_to_all(jnp.broadcast_to(part, (4, quarter, NB)), "x", 0, 0)
+    share = 5 * NB * NB // 32
+    part = lax.all_to_all(summed.reshape(32, share), GX, 0, 0, tiled=True)
+    part = part.reshape(32, share).sum(0).reshape(1, share // NB, NB)
+    part = lax.all_to_all(jnp.broadcast_to(part, (8, share // NB, NB)), "y", 0, 0)
+    total = part.sum(0).reshape(1, share)
+    mine = lax.all_to_all(jnp.broadcast_to(total, (32, share)), GX, 0, 0, tiled=True)
     mine = mine.reshape(5 * NB, NB)
     other = swap(mine)
 

time: 147 us -> 139 us (0.946)
  blocking collectives: 63.1 us -> 56.8 us
    all_to_all x4 -> x3, blocking collectives: 63.1 us -> 56.8 us  [the longest x1 25 us: local(): part = lax.all_to_all(summed.reshape(32, share), GX, 0, 0, tiled=True)]
where the time goes in v5:
time: 139 us
  blocking collectives  56.8 us (41%)
  starting transfers between devices  47.2 us (34%)
  Pallas kernels  20.4 us (15%)
  waiting for transfers between devices  8.74 us (6%)
  local copies, waits for them, and re-layouts  4.23 us (3%)
    ppermute x12, starting transfers between devices, exchange(): return lax.ppermute(v, axes, pairs)  38.4 us
    all_to_all x1, blocking collectives, local(): part = lax.all_to_all(summed.reshape(32, share), GX, 0, 0, tiled=True)  25 us
    all_to_all x1, blocking collectives, local(): lax.all_to_all(jnp.broadcast_to(part, (8, share // NB, NB)), 'y', 0, 0)  16.3 us
    all_to_all x1, blocking collectives, local(): lax.all_to_all(jnp.broadcast_to(total, (32, share)), GX, 0, 0, tiled=True)  15.5 us
    pallas_call x1, Pallas kernels, local(): call(functools.partial(finish_kernel, root), (half, shape(4, NB)), [VMEM]...  14.3 us
    ppermute x2, starting transfers between devices, swap(): return lax.ppermute(v, 'c', [(0, 1), (1, 0)])  8.81 us
    ppermute x12, waiting for transfers between devices, exchange(): return lax.ppermute(v, axes, pairs)  6.45 us
    unnamed x8, local copies, waits for them, and re-layouts  3.24 us
  transfers between devices with their start and end apart: 14, of which 6 were waited for; matrix products, arithmetic and copies ran while one was open for 1% of the time, Pallas kernels for 1%

profile of v5, /device:TPU:1, one launch (start us, length us, event | category | flops | bytes accessed | tf_op | source)
XLA Modules:
  0.0 138.6 jit_solution(2155075246534537185)
XLA Ops:
  0.6 0.7 collective-permute-start.3
  1.3 6.4 %collective-permute-start.2 = (bf16[384,512]{1,0:T(8,128)(2,1)}, bf16[384,512]{1,0:T(8,128)(2,1)S(1)}, u32[]{:S(2)}, u32[]{:S(2)}) collective-permute-start(bf16[384,512]{1,0:T(8,128)(2,1)} %bitcast.22), channel_id=1, source_target_pairs={{0,16},{16,0},{32,48},{48,32},{64,80},{80,64},{96,112},{112,96},{1... | collective-permute-start | bytes 1179656 | tf_op jit(solution)/shard_map/ppermute | solution.py:253
  7.7 4.3 %collective-permute-start.1 = (bf16[384,512]{1,0:T(8,128)(2,1)}, bf16[384,512]{1,0:T(8,128)(2,1)S(1)}, u32[]{:S(2)}, u32[]{:S(2)}) collective-permute-start(bf16[384,512]{1,0:T(8,128)(2,1)} %bitcast.23), channel_id=1, source_target_pairs={{1,2},{2,1},{3,4},{4,3},{5,6},{6,5},{7,8},{8,7},{9,10},{10,9},{11,... | collective-permute-start | bytes 1179656 | tf_op jit(solution)/shard_map/ppermute | solution.py:253
  12.1 1.9 %collective-permute-start = (bf16[384,512]{1,0:T(8,128)(2,1)}, bf16[384,512]{1,0:T(8,128)(2,1)S(1)}, u32[]{:S(2)}, u32[]{:S(2)}) collective-permute-start(bf16[384,512]{1,0:T(8,128)(2,1)} %bitcast.24), channel_id=1, source_target_pairs={{0,1},{1,0},{2,3},{3,2},{4,5},{5,4},{6,7},{7,6},{8,9},{9,8},{10,11... | collective-permute-start | bytes 1179656 | tf_op jit(solution)/shard_map/ppermute | solution.py:253
  14.0 0.8 copy.17.w_ref
  14.8 0.0 copy-start.3
  14.8 0.0 copy-start
  14.8 1.4 copy-done
  16.2 0.0 copy-start.2
  16.2 1.0 copy-done.2
  17.2 0.0 copy-start.1
  17.2 0.4 own_block.3.part_ref
  17.6 0.1 pad_add_fusion.i_ref
  17.7 0.0 collective-permute-done.3.h3
  17.7 0.0 collective-permute-done.2.h2
  17.7 0.0 collective-permute-done.1.h1
  17.7 0.0 collective-permute-done.h0
  17.7 0.0 copy-done.3
  17.7 0.9 copy-done.1
  18.6 1.3 first.1
  19.9 0.7 collective-permute-start.7
  20.6 6.1 %collective-permute-start.6 = (bf16[384,512]{1,0:T(8,128)(2,1)S(1)}, bf16[384,512]{1,0:T(8,128)(2,1)S(1)}, u32[]{:S(2)}, u32[]{:S(2)}) collective-permute-start(bf16[384,512]{1,0:T(8,128)(2,1)S(1)} %get-tuple-element.9.v_ref), channel_id=1, source_target_pairs={{0,16},{16,0},{32,48},{48,32},{64,80},{80,64},{96,112},{112,96},{1... | collective-permute-start | bytes 1179656 | tf_op jit(solution)/shard_map/ppermute | solution.py:253
  26.7 4.1 %collective-permute-start.5 = (bf16[384,512]{1,0:T(8,128)(2,1)S(1)}, bf16[384,512]{1,0:T(8,128)(2,1)S(1)}, u32[]{:S(2)}, u32[]{:S(2)}) collective-permute-start(bf16[384,512]{1,0:T(8,128)(2,1)S(1)} %get-tuple-element.9.v_ref), channel_id=1, source_target_pairs={{1,2},{2,1},{3,4},{4,3},{5,6},{6,5},{7,8},{8,7},{9,10},{10,9},{11,... | collective-permute-start | bytes 1179656 | tf_op jit(solution)/shard_map/ppermute | solution.py:253
  30.8 1.9 %collective-permute-start.4 = (bf16[384,512]{1,0:T(8,128)(2,1)S(1)}, bf16[384,512]{1,0:T(8,128)(2,1)S(1)}, u32[]{:S(2)}, u32[]{:S(2)}) collective-permute-start(bf16[384,512]{1,0:T(8,128)(2,1)S(1)} %get-tuple-element.9.v_ref), channel_id=1, source_target_pairs={{0,1},{1,0},{2,3},{3,2},{4,5},{5,4},{6,7},{7,6},{8,9},{9,8},{10,11... | collective-permute-start | bytes 1179656 | tf_op jit(solution)/shard_map/ppermute | solution.py:253
  32.7 0.4 own_block.4.part_ref
  33.1 0.0 collective-permute-done.7.h3
  33.1 2.2 %collective-permute-done.6.h2 = bf16[384,512]{1,0:T(8,128)(2,1)S(1)} collective-permute-done((bf16[384,512]{1,0:T(8,128)(2,1)S(1)}, bf16[384,512]{1,0:T(8,128)(2,1)S(1)}, u32[]{:S(2)}, u32[]{:S(2)}) %collective-permute-start.6) | collective-permute-done | bytes 393248 | tf_op jit(solution)/shard_map/ppermute | solution.py:253
  35.4 0.9 collective-permute-done.5.h1
  36.3 0.0 collective-permute-done.4.h0
  36.3 1.3 middle.1.v_ref
  37.6 0.7 collective-permute-start.11
  38.3 5.5 %collective-permute-start.10 = (bf16[384,512]{1,0:T(8,128)(2,1)S(1)}, bf16[384,512]{1,0:T(8,128)(2,1)S(1)}, u32[]{:S(2)}, u32[]{:S(2)}) collective-permute-start(bf16[384,512]{1,0:T(8,128)(2,1)S(1)} %middle.1.v_ref), channel_id=1, source_target_pairs={{0,16},{16,0},{32,48},{48,32},{64,80},{80,64},{96,112},{112,96},{1... | collective-permute-start | bytes 1179656 | tf_op jit(solution)/shard_map/ppermute | solution.py:253
  43.9 4.1 %collective-permute-start.9 = (bf16[384,512]{1,0:T(8,128)(2,1)S(1)}, bf16[384,512]{1,0:T(8,128)(2,1)S(1)}, u32[]{:S(2)}, u32[]{:S(2)}) collective-permute-start(bf16[384,512]{1,0:T(8,128)(2,1)S(1)} %middle.1.v_ref), channel_id=1, source_target_pairs={{1,2},{2,1},{3,4},{4,3},{5,6},{6,5},{7,8},{8,7},{9,10},{10,9},{11,... | collective-permute-start | bytes 1179656 | tf_op jit(solution)/shard_map/ppermute | solution.py:253
  48.0 1.9 %collective-permute-start.8 = (bf16[384,512]{1,0:T(8,128)(2,1)S(1)}, bf16[384,512]{1,0:T(8,128)(2,1)S(1)}, u32[]{:S(2)}, u32[]{:S(2)}) collective-permute-start(bf16[384,512]{1,0:T(8,128)(2,1)S(1)} %middle.1.v_ref), channel_id=1, source_target_pairs={{0,1},{1,0},{2,3},{3,2},{4,5},{5,4},{6,7},{7,6},{8,9},{9,8},{10,11... | collective-permute-start | bytes 1179656 | tf_op jit(solution)/shard_map/ppermute | solution.py:253
  50.0 0.4 own_block.5.part_ref
  50.3 0.0 collective-permute-done.11.h3
  50.4 2.4 %collective-permute-done.10.h2 = bf16[384,512]{1,0:T(8,128)(2,1)S(1)} collective-permute-done((bf16[384,512]{1,0:T(8,128)(2,1)S(1)}, bf16[384,512]{1,0:T(8,128)(2,1)S(1)}, u32[]{:S(2)}, u32[]{:S(2)}) %collective-permute-start.10) | collective-permute-done | bytes 393248 | tf_op jit(solution)/shard_map/ppermute | solution.py:253
  52.7 0.8 collective-permute-done.9.h1
  53.6 0.0 collective-permute-done.8.h0
  53.6 2.4 %last_and_correlation.1 = (f32[384,512]{1,0:T(8,128)S(1)}, f32[640,128]{1,0:T(8,128)S(1)}, f32[640,128]{1,0:T(8,128)S(1)}) custom-call(f32[384,512]{1,0:T(8,128)S(1)} %own_block.5.part_ref, bf16[5,384,384]{2,1,0:T(8,128)(2,1)S(1)} %bitcast.20, s32[4]{0:T(128)S(1)} %bitcast.31, s32[4]{0:T(128)S(1)} %pad_add_fusion.i_ref, ...), custom_call_target="tpu_custom_call" | custom-call | flops 1207959552 | bytes 2097152 | tf_op jit(solution)/shard_map/last_and_correlation/pallas_call | solution.py:294
  56.0 2.3 %collective-permute-start.12 = (f32[640,128]{1,0:T(8,128)S(1)}, f32[640,128]{1,0:T(8,128)S(1)}, u32[]{:S(2)}, u32[]{:S(2)}) collective-permute-start(f32[640,128]{1,0:T(8,128)S(1)} %get-tuple-element.12), channel_id=1, source_target_pairs={{0,1},{1,0},{2,3},{3,2},{4,5},{5,4},{6,7},{7,6},{8,9},{9,8},{10,11... | collective-permute-start | bytes 983048 | tf_op jit(solution)/shard_map/ppermute | solution.py:266
  58.3 1.2 collective-permute-done.12
  59.6 25.0 %all_to_all.20 = f32[32,1,2560]{2,1,0:T(1,128)S(1)} all-to-all(f32[32,1,2560]{2,1,0:T(1,128)S(1)} %bitcast.32), channel_id=1, replica_groups=mesh['z'=8,'x'=4,'y'=8,'c'=2] {'z','x'}, dimensions={0} | all-to-all | bytes 655360 | tf_op jit(solution)/shard_map/all_to_all | solution.py:305
  84.6 0.2 reduce_sum.18
  84.8 16.3 %all_to_all.21 = f32[8,20,128]{2,1,0:T(8,128)S(1)} all-to-all(f32[8,20,128]{2,1,0:T(8,128)S(1)} %broadcast_in_dim.22), channel_id=1, replica_groups=mesh['z'=8,'x'=4,'y'=8,'c'=2] {'y'}, dimensions={0} | all-to-all | bytes 163840 | tf_op jit(solution)/shard_map/all_to_all | solution.py:307
  101.1 0.2 broadcast_in_dim.24
  101.3 15.5 %all_to_all.22 = f32[32,1,2560]{2,1,0:T(1,128)S(1)} all-to-all(f32[32,1,2560]{2,1,0:T(1,128)S(1)} %broadcast_in_dim.24), channel_id=1, replica_groups=mesh['z'=8,'x'=4,'y'=8,'c'=2] {'z','x'}, dimensions={0} | all-to-all | bytes 655360 | tf_op jit(solution)/shard_map/all_to_all | solution.py:309
  116.8 6.5 %collective-permute-start.13 = (f32[640,128]{1,0:T(8,128)S(1)}, f32[640,128]{1,0:T(8,128)S(1)}, u32[]{:S(2)}, u32[]{:S(2)}) collective-permute-start(f32[640,128]{1,0:T(8,128)S(1)} %bitcast.27), channel_id=1, source_target_pairs={{0,1},{1,0},{2,3},{3,2},{4,5},{5,4},{6,7},{7,6},{8,9},{9,8},{10,11... | collective-permute-start | bytes 983048 | tf_op jit(solution)/shard_map/ppermute | solution.py:266
  123.3 1.1 collective-permute-done.13.other_ref
  124.3 14.3 %finish.1 = (bf16[384,512]{1,0:T(8,128)(2,1)}, f32[4,128]{1,0:T(4,128)}) custom-call(f32[640,128]{1,0:T(8,128)S(1)} %bitcast.28, f32[640,128]{1,0:T(8,128)S(1)} %collective-permute-done.13.other_ref, f32[384,512]{1,0:T(8,128)S(1)} %get-tuple-element.13.f_ref, s32[1]{0:T(128)} %bitcast.8.core_ref), custom_call_target="tpu_custom_call" | custom-call | flops 1207959552 | bytes 2097152 | tf_op jit(solution)/shard_map/finish/pallas_call | solution.py:314
  (3 shorter events, 0.1 us)
Async XLA Ops:
  0.6 17.0 %collective-permute-start.3 = (bf16[384,512]{1,0:T(8,128)(2,1)}, bf16[384,512]{1,0:T(8,128)(2,1)S(1)}, u32[]{:S(2)}, u32[]{:S(2)}) collective-permute-start(bf16[384,512]{1,0:T(8,128)(2,1)} %bitcast.21), channel_id=1, source_target_pairs={{16,32},{32,16},{48,64},{64,48},{80,96},{96,80},{112,128},{128,112... | collective-permute-start | bytes 1179656 | tf_op jit(solution)/shard_map/ppermute | solution.py:253
  1.3 16.3 %collective-permute-start.2 = (bf16[384,512]{1,0:T(8,128)(2,1)}, bf16[384,512]{1,0:T(8,128)(2,1)S(1)}, u32[]{:S(2)}, u32[]{:S(2)}) collective-permute-start(bf16[384,512]{1,0:T(8,128)(2,1)} %bitcast.22), channel_id=1, source_target_pairs={{0,16},{16,0},{32,48},{48,32},{64,80},{80,64},{96,112},{112,96},{1... | collective-permute-start | bytes 1179656 | tf_op jit(solution)/shard_map/ppermute | solution.py:253
  7.7 10.0 %collective-permute-start.1 = (bf16[384,512]{1,0:T(8,128)(2,1)}, bf16[384,512]{1,0:T(8,128)(2,1)S(1)}, u32[]{:S(2)}, u32[]{:S(2)}) collective-permute-start(bf16[384,512]{1,0:T(8,128)(2,1)} %bitcast.23), channel_id=1, source_target_pairs={{1,2},{2,1},{3,4},{4,3},{5,6},{6,5},{7,8},{8,7},{9,10},{10,9},{11,... | collective-permute-start | bytes 1179656 | tf_op jit(solution)/shard_map/ppermute | solution.py:253
  12.1 5.7 %collective-permute-start = (bf16[384,512]{1,0:T(8,128)(2,1)}, bf16[384,512]{1,0:T(8,128)(2,1)S(1)}, u32[]{:S(2)}, u32[]{:S(2)}) collective-permute-start(bf16[384,512]{1,0:T(8,128)(2,1)} %bitcast.24), channel_id=1, source_target_pairs={{0,1},{1,0},{2,3},{3,2},{4,5},{5,4},{6,7},{7,6},{8,9},{9,8},{10,11... | collective-permute-start | bytes 1179656 | tf_op jit(solution)/shard_map/ppermute | solution.py:253
  14.8 2.9 %copy-start.3 = (s32[1,1,4]{2,1,0:T(1,128)S(1)}, s32[1,1,4]{2,1,0:T(1,128)}, u32[]{:S(2)}) copy-start(s32[1,1,4]{2,1,0:T(1,128)} %param.7) | copy-start | bytes 52
  14.8 1.4 copy-start
  16.2 1.0 copy-start.2
  17.2 1.4 copy-start.1
  19.9 13.2 %collective-permute-start.7 = (bf16[384,512]{1,0:T(8,128)(2,1)S(1)}, bf16[384,512]{1,0:T(8,128)(2,1)S(1)}, u32[]{:S(2)}, u32[]{:S(2)}) collective-permute-start(bf16[384,512]{1,0:T(8,128)(2,1)S(1)} %get-tuple-element.9.v_ref), channel_id=1, source_target_pairs={{16,32},{32,16},{48,64},{64,48},{80,96},{96,80},{112,128},{128,112... | collective-permute-start | bytes 1179656 | tf_op jit(solution)/shard_map/ppermute | solution.py:253
  20.6 14.8 %collective-permute-start.6 = (bf16[384,512]{1,0:T(8,128)(2,1)S(1)}, bf16[384,512]{1,0:T(8,128)(2,1)S(1)}, u32[]{:S(2)}, u32[]{:S(2)}) collective-permute-start(bf16[384,512]{1,0:T(8,128)(2,1)S(1)} %get-tuple-element.9.v_ref), channel_id=1, source_target_pairs={{0,16},{16,0},{32,48},{48,32},{64,80},{80,64},{96,112},{112,96},{1... | collective-permute-start | bytes 1179656 | tf_op jit(solution)/shard_map/ppermute | solution.py:253
  26.7 9.7 %collective-permute-start.5 = (bf16[384,512]{1,0:T(8,128)(2,1)S(1)}, bf16[384,512]{1,0:T(8,128)(2,1)S(1)}, u32[]{:S(2)}, u32[]{:S(2)}) collective-permute-start(bf16[384,512]{1,0:T(8,128)(2,1)S(1)} %get-tuple-element.9.v_ref), channel_id=1, source_target_pairs={{1,2},{2,1},{3,4},{4,3},{5,6},{6,5},{7,8},{8,7},{9,10},{10,9},{11,... | collective-permute-start | bytes 1179656 | tf_op jit(solution)/shard_map/ppermute | solution.py:253
  30.8 5.5 %collective-permute-start.4 = (bf16[384,512]{1,0:T(8,128)(2,1)S(1)}, bf16[384,512]{1,0:T(8,128)(2,1)S(1)}, u32[]{:S(2)}, u32[]{:S(2)}) collective-permute-start(bf16[384,512]{1,0:T(8,128)(2,1)S(1)} %get-tuple-element.9.v_ref), channel_id=1, source_target_pairs={{0,1},{1,0},{2,3},{3,2},{4,5},{5,4},{6,7},{7,6},{8,9},{9,8},{10,11... | collective-permute-start | bytes 1179656 | tf_op jit(solution)/shard_map/ppermute | solution.py:253
  37.6 12.7 %collective-permute-start.11 = (bf16[384,512]{1,0:T(8,128)(2,1)S(1)}, bf16[384,512]{1,0:T(8,128)(2,1)S(1)}, u32[]{:S(2)}, u32[]{:S(2)}) collective-permute-start(bf16[384,512]{1,0:T(8,128)(2,1)S(1)} %middle.1.v_ref), channel_id=1, source_target_pairs={{16,32},{32,16},{48,64},{64,48},{80,96},{96,80},{112,128},{128,112... | collective-permute-start | bytes 1179656 | tf_op jit(solution)/shard_map/ppermute | solution.py:253
  38.3 14.4 %collective-permute-start.10 = (bf16[384,512]{1,0:T(8,128)(2,1)S(1)}, bf16[384,512]{1,0:T(8,128)(2,1)S(1)}, u32[]{:S(2)}, u32[]{:S(2)}) collective-permute-start(bf16[384,512]{1,0:T(8,128)(2,1)S(1)} %middle.1.v_ref), channel_id=1, source_target_pairs={{0,16},{16,0},{32,48},{48,32},{64,80},{80,64},{96,112},{112,96},{1... | collective-permute-start | bytes 1179656 | tf_op jit(solution)/shard_map/ppermute | solution.py:253
  43.9 9.7 %collective-permute-start.9 = (bf16[384,512]{1,0:T(8,128)(2,1)S(1)}, bf16[384,512]{1,0:T(8,128)(2,1)S(1)}, u32[]{:S(2)}, u32[]{:S(2)}) collective-permute-start(bf16[384,512]{1,0:T(8,128)(2,1)S(1)} %middle.1.v_ref), channel_id=1, source_target_pairs={{1,2},{2,1},{3,4},{4,3},{5,6},{6,5},{7,8},{8,7},{9,10},{10,9},{11,... | collective-permute-start | bytes 1179656 | tf_op jit(solution)/shard_map/ppermute | solution.py:253
  48.0 5.5 %collective-permute-start.8 = (bf16[384,512]{1,0:T(8,128)(2,1)S(1)}, bf16[384,512]{1,0:T(8,128)(2,1)S(1)}, u32[]{:S(2)}, u32[]{:S(2)}) collective-permute-start(bf16[384,512]{1,0:T(8,128)(2,1)S(1)} %middle.1.v_ref), channel_id=1, source_target_pairs={{0,1},{1,0},{2,3},{3,2},{4,5},{5,4},{6,7},{7,6},{8,9},{9,8},{10,11... | collective-permute-start | bytes 1179656 | tf_op jit(solution)/shard_map/ppermute | solution.py:253
  56.0 3.5 %collective-permute-start.12 = (f32[640,128]{1,0:T(8,128)S(1)}, f32[640,128]{1,0:T(8,128)S(1)}, u32[]{:S(2)}, u32[]{:S(2)}) collective-permute-start(f32[640,128]{1,0:T(8,128)S(1)} %get-tuple-element.12), channel_id=1, source_target_pairs={{0,1},{1,0},{2,3},{3,2},{4,5},{5,4},{6,7},{7,6},{8,9},{9,8},{10,11... | collective-permute-start | bytes 983048 | tf_op jit(solution)/shard_map/ppermute | solution.py:266
  116.8 7.6 %collective-permute-start.13 = (f32[640,128]{1,0:T(8,128)S(1)}, f32[640,128]{1,0:T(8,128)S(1)}, u32[]{:S(2)}, u32[]{:S(2)}) collective-permute-start(f32[640,128]{1,0:T(8,128)S(1)} %bitcast.27), channel_id=1, source_target_pairs={{0,1},{1,0},{2,3},{3,2},{4,5},{5,4},{6,7},{7,6},{8,9},{9,8},{10,11... | collective-permute-start | bytes 983048 | tf_op jit(solution)/shard_map/ppermute | solution.py:266

commit v6 on v5

--- a/solution.py
+++ b/solution.py
@@ -18,6 +18,12 @@
 GX = ("z", "x")
 GY = ("y", "c")
 LIMIT = 12 * 2**20
+PART = 4 * NB + 32
+PLACES = {(1, 0): (0, 1), (2, 0): (0, 2), (3, 0): (0, 3), (2, 1): (1, 1), (3, 1): (1, 2), (3, 2): (1, 3)}
+
+
+def iotas():
+    return [lax.broadcasted_iota(jnp.int32, (NB, NB), d) for d in (0, 1)]
 
 
 def dot(a, b, dims):
@@ -77,17 +83,25 @@
     out = 2.0 * SCALE * total - p_ref[...]
     o_ref[...] = out
     left, right = left_stack(out, 0), right_stack(out, 0)
+    down, across = iotas()
     for i in (0, 2):
         g = dot(left[:, i * NB : (i + 2) * NB], right[:, : (i + 2) * NB], ((0,), (0,)))
-        for r in range(i, i + 2):
-            for l in range(r + 1):
-                n = r * (r + 1) // 2 + l
-                block = g[(r - i) * NB : (r - i + 1) * NB, l * NB : (l + 1) * NB]
-                g_ref[n * NB : (n + 1) * NB, :] = block
-    count = 5 * NB
+
+        def block(r, l):
+            return g[(r - i) * NB : (r - i + 1) * NB, l * NB : (l + 1) * NB]
+
+        start = i // 2 * PART
+        second = block(i + 1, i + 1)
+        g_ref[start : start + NB, :] = jnp.where(down >= across, block(i, i), second)
+        tail = jnp.sum(jnp.where(down == across, second, 0.0), 0, keepdims=True)
+        g_ref[start + 4 * NB : start + PART, :] = jnp.broadcast_to(tail, (PART - 4 * NB, NB))
+        for (r, l), (part, n) in PLACES.items():
+            if r in (i, i + 1):
+                at = part * PART + n * NB
+                g_ref[at : at + NB, :] = block(r, l)
     core = core_ref[0]
-    keep_ref[...] = g_ref[pl.ds(pl.multiple_of(core * count, NB), count), :]
-    send_ref[...] = g_ref[pl.ds(pl.multiple_of((1 - core) * count, NB), count), :]
+    keep_ref[...] = g_ref[pl.ds(pl.multiple_of(core * PART, 8), PART), :]
+    send_ref[...] = g_ref[pl.ds(pl.multiple_of((1 - core) * PART, 8), PART), :]
 
 
 def shape(*dims, dtype=F32):
@@ -181,10 +195,6 @@
 def finish_kernel(
     root, mine_ref, other_ref, f_ref, core_ref, o_ref, d_ref, w_ref, z_ref, e_ref, *bufs
 ):
-    order = {}
-    for i in range(4):
-        for l in range(i + 1):
-            order[i, l] = len(order)
     stored = set()
 
     def rows(i):
@@ -195,9 +205,19 @@
             return w_ref[l, rows(i), :]
         if i >= 4:
             return f_ref[rows(i - 4), rows(l)]
-        n = order[i, l]
-        here, there = mine_ref[rows(n % 5), :], other_ref[rows(n % 5), :]
-        return jnp.where(core_ref[0] == n // 5, here, there)
+        if i != l:
+            part, n = PLACES[i, l]
+            return given(part, slice(n * NB, (n + 1) * NB))
+        both = given(i // 2, slice(0, NB))
+        if i % 2 == 0:
+            return jnp.where(down >= across, both, both.T)
+        tail = given(i // 2, slice(4 * NB, 4 * NB + 8))[0:1]
+        return jnp.where(down == across, tail, jnp.where(down < across, both, both.T))
+
+    def given(part, at):
+        return jnp.where(core_ref[0] == part, mine_ref[at, :], other_ref[at, :])
+
+    down, across = iotas()
 
     def put(i, l, v):
         w_ref[l, rows(i), :] = v
@@ -290,24 +310,24 @@
 
     x1, r1 = call(first_kernel, (full, half), specs, "first", 4 * flops)(*operands(v0))
     r2 = call(middle_kernel, half, specs + [VMEM], "middle", 4 * flops)(*operands(r1), v0)
-    piece = shape(5 * NB, NB)
+    piece = shape(PART, NB)
     filtered, keep, send = call(
         last_kernel,
         (full, piece, piece),
         specs + [VMEM, SMEM],
         "last_and_correlation",
         8 * flops,
-        (pltpu.VMEM((10 * NB, NB), F32),),
+        (pltpu.VMEM((2 * PART, NB), F32),),
     )(*operands(r2), x1, core)
 
     summed = keep + swap(send)
-    share = 5 * NB * NB // 32
+    share = PART * NB // 32
     part = lax.all_to_all(summed.reshape(32, share), GX, 0, 0, tiled=True)
     part = part.reshape(32, share).sum(0).reshape(1, share // NB, NB)
     part = lax.all_to_all(jnp.broadcast_to(part, (8, share // NB, NB)), "y", 0, 0)
     total = part.sum(0).reshape(1, share)
     mine = lax.all_to_all(jnp.broadcast_to(total, (32, share)), GX, 0, 0, tiled=True)
-    mine = mine.reshape(5 * NB, NB)
+    mine = mine.reshape(PART, NB)
     other = swap(mine)
 
     root = math.sqrt(rows * 512)

time: 139 us -> 138 us (level)
  no operation moved by 1% of the time
where the time goes in v6:
time: 138 us; the launch traced here: 137 us
  blocking collectives  55.5 us (40%)
  starting transfers between devices  46.9 us (34%)
  Pallas kernels  20.5 us (15%)
  waiting for transfers between devices  8.59 us (6%)
  local copies, waits for them, and re-layouts  4.2 us (3%)
    ppermute x12, starting transfers between devices, exchange(): return lax.ppermute(v, axes, pairs)  38.4 us
    all_to_all x1, blocking collectives, local(): part = lax.all_to_all(summed.reshape(32, share), GX, 0, 0, tiled=True)  24.1 us
    all_to_all x1, blocking collectives, local(): lax.all_to_all(jnp.broadcast_to(part, (8, share // NB, NB)), 'y', 0, 0)  16.4 us
    all_to_all x1, blocking collectives, local(): lax.all_to_all(jnp.broadcast_to(total, (32, share)), GX, 0, 0, tiled=True)  15 us
    pallas_call x1, Pallas kernels, local(): call(functools.partial(finish_kernel, root), (half, shape(4, NB)), [VMEM]...  14.3 us
    ppermute x2, starting transfers between devices, swap(): return lax.ppermute(v, 'c', [(0, 1), (1, 0)])  8.5 us
    ppermute x12, waiting for transfers between devices, exchange(): return lax.ppermute(v, axes, pairs)  6.44 us
    unnamed x8, local copies, waits for them, and re-layouts  3.24 us
  transfers between devices with their start and end apart: 14, of which 6 were waited for; matrix products, arithmetic and copies ran while one was open for 1% of the time, Pallas kernels for 1%

profile of v6, /device:TPU:1, one launch (start us, length us, event | category | flops | bytes accessed | tf_op | source)
XLA Modules:
  0.0 136.9 jit_solution(9919825134688981800)
XLA Ops:
  0.6 0.7 collective-permute-start.3
  1.3 6.4 %collective-permute-start.2 = (bf16[384,512]{1,0:T(8,128)(2,1)}, bf16[384,512]{1,0:T(8,128)(2,1)S(1)}, u32[]{:S(2)}, u32[]{:S(2)}) collective-permute-start(bf16[384,512]{1,0:T(8,128)(2,1)} %bitcast.22), channel_id=1, source_target_pairs={{0,16},{16,0},{32,48},{48,32},{64,80},{80,64},{96,112},{112,96},{1... | collective-permute-start | bytes 1179656 | tf_op jit(solution)/shard_map/ppermute | solution.py:273
  7.7 4.3 %collective-permute-start.1 = (bf16[384,512]{1,0:T(8,128)(2,1)}, bf16[384,512]{1,0:T(8,128)(2,1)S(1)}, u32[]{:S(2)}, u32[]{:S(2)}) collective-permute-start(bf16[384,512]{1,0:T(8,128)(2,1)} %bitcast.23), channel_id=1, source_target_pairs={{1,2},{2,1},{3,4},{4,3},{5,6},{6,5},{7,8},{8,7},{9,10},{10,9},{11,... | collective-permute-start | bytes 1179656 | tf_op jit(solution)/shard_map/ppermute | solution.py:273
  12.1 1.9 %collective-permute-start = (bf16[384,512]{1,0:T(8,128)(2,1)}, bf16[384,512]{1,0:T(8,128)(2,1)S(1)}, u32[]{:S(2)}, u32[]{:S(2)}) collective-permute-start(bf16[384,512]{1,0:T(8,128)(2,1)} %bitcast.24), channel_id=1, source_target_pairs={{0,1},{1,0},{2,3},{3,2},{4,5},{5,4},{6,7},{7,6},{8,9},{9,8},{10,11... | collective-permute-start | bytes 1179656 | tf_op jit(solution)/shard_map/ppermute | solution.py:273
  14.0 0.8 copy.17.w_ref
  14.8 0.0 copy-start.3
  14.8 0.0 copy-start
  14.8 1.4 %copy-done = bf16[1,1,5,384,384]{4,3,2,1,0:T(8,128)(2,1)S(1)} copy-done((bf16[1,1,5,384,384]{4,3,2,1,0:T(8,128)(2,1)S(1)}, bf16[1,1,5,384,384]{4,3,2,1,0:T(8,128)(2,1)}, u32[]{:S(2)}) %copy-start) | copy-done | bytes 1474584
  16.2 0.0 copy-start.2
  16.2 1.0 copy-done.2
  17.2 0.0 copy-start.1
  17.2 0.4 own_block.3.part_ref
  17.6 0.1 pad_add_fusion.i_ref
  17.7 0.0 collective-permute-done.3.h3
  17.7 0.0 collective-permute-done.2.h2
  17.7 0.0 collective-permute-done.1.h1
  17.7 0.0 collective-permute-done.h0
  17.7 0.0 copy-done.3
  17.7 0.9 copy-done.1
  18.6 1.3 first.1
  19.9 0.7 collective-permute-start.7
  20.6 6.1 %collective-permute-start.6 = (bf16[384,512]{1,0:T(8,128)(2,1)S(1)}, bf16[384,512]{1,0:T(8,128)(2,1)S(1)}, u32[]{:S(2)}, u32[]{:S(2)}) collective-permute-start(bf16[384,512]{1,0:T(8,128)(2,1)S(1)} %get-tuple-element.9.v_ref), channel_id=1, source_target_pairs={{0,16},{16,0},{32,48},{48,32},{64,80},{80,64},{96,112},{112,96},{1... | collective-permute-start | bytes 1179656 | tf_op jit(solution)/shard_map/ppermute | solution.py:273
  26.7 4.1 %collective-permute-start.5 = (bf16[384,512]{1,0:T(8,128)(2,1)S(1)}, bf16[384,512]{1,0:T(8,128)(2,1)S(1)}, u32[]{:S(2)}, u32[]{:S(2)}) collective-permute-start(bf16[384,512]{1,0:T(8,128)(2,1)S(1)} %get-tuple-element.9.v_ref), channel_id=1, source_target_pairs={{1,2},{2,1},{3,4},{4,3},{5,6},{6,5},{7,8},{8,7},{9,10},{10,9},{11,... | collective-permute-start | bytes 1179656 | tf_op jit(solution)/shard_map/ppermute | solution.py:273
  30.8 1.9 %collective-permute-start.4 = (bf16[384,512]{1,0:T(8,128)(2,1)S(1)}, bf16[384,512]{1,0:T(8,128)(2,1)S(1)}, u32[]{:S(2)}, u32[]{:S(2)}) collective-permute-start(bf16[384,512]{1,0:T(8,128)(2,1)S(1)} %get-tuple-element.9.v_ref), channel_id=1, source_target_pairs={{0,1},{1,0},{2,3},{3,2},{4,5},{5,4},{6,7},{7,6},{8,9},{9,8},{10,11... | collective-permute-start | bytes 1179656 | tf_op jit(solution)/shard_map/ppermute | solution.py:273
  32.7 0.4 own_block.4.part_ref
  33.1 0.0 collective-permute-done.7.h3
  33.1 2.2 %collective-permute-done.6.h2 = bf16[384,512]{1,0:T(8,128)(2,1)S(1)} collective-permute-done((bf16[384,512]{1,0:T(8,128)(2,1)S(1)}, bf16[384,512]{1,0:T(8,128)(2,1)S(1)}, u32[]{:S(2)}, u32[]{:S(2)}) %collective-permute-start.6) | collective-permute-done | bytes 393248 | tf_op jit(solution)/shard_map/ppermute | solution.py:273
  35.4 1.0 collective-permute-done.5.h1
  36.3 0.0 collective-permute-done.4.h0
  36.3 1.3 middle.1.v_ref
  37.6 0.7 collective-permute-start.11
  38.3 5.5 %collective-permute-start.10 = (bf16[384,512]{1,0:T(8,128)(2,1)S(1)}, bf16[384,512]{1,0:T(8,128)(2,1)S(1)}, u32[]{:S(2)}, u32[]{:S(2)}) collective-permute-start(bf16[384,512]{1,0:T(8,128)(2,1)S(1)} %middle.1.v_ref), channel_id=1, source_target_pairs={{0,16},{16,0},{32,48},{48,32},{64,80},{80,64},{96,112},{112,96},{1... | collective-permute-start | bytes 1179656 | tf_op jit(solution)/shard_map/ppermute | solution.py:273
  43.9 4.1 %collective-permute-start.9 = (bf16[384,512]{1,0:T(8,128)(2,1)S(1)}, bf16[384,512]{1,0:T(8,128)(2,1)S(1)}, u32[]{:S(2)}, u32[]{:S(2)}) collective-permute-start(bf16[384,512]{1,0:T(8,128)(2,1)S(1)} %middle.1.v_ref), channel_id=1, source_target_pairs={{1,2},{2,1},{3,4},{4,3},{5,6},{6,5},{7,8},{8,7},{9,10},{10,9},{11,... | collective-permute-start | bytes 1179656 | tf_op jit(solution)/shard_map/ppermute | solution.py:273
  48.0 1.9 %collective-permute-start.8 = (bf16[384,512]{1,0:T(8,128)(2,1)S(1)}, bf16[384,512]{1,0:T(8,128)(2,1)S(1)}, u32[]{:S(2)}, u32[]{:S(2)}) collective-permute-start(bf16[384,512]{1,0:T(8,128)(2,1)S(1)} %middle.1.v_ref), channel_id=1, source_target_pairs={{0,1},{1,0},{2,3},{3,2},{4,5},{5,4},{6,7},{7,6},{8,9},{9,8},{10,11... | collective-permute-start | bytes 1179656 | tf_op jit(solution)/shard_map/ppermute | solution.py:273
  50.0 0.4 own_block.5.part_ref
  50.4 0.0 collective-permute-done.11.h3
  50.4 2.4 %collective-permute-done.10.h2 = bf16[384,512]{1,0:T(8,128)(2,1)S(1)} collective-permute-done((bf16[384,512]{1,0:T(8,128)(2,1)S(1)}, bf16[384,512]{1,0:T(8,128)(2,1)S(1)}, u32[]{:S(2)}, u32[]{:S(2)}) %collective-permute-start.10) | collective-permute-done | bytes 393248 | tf_op jit(solution)/shard_map/ppermute | solution.py:273
  52.7 0.8 collective-permute-done.9.h1
  53.6 0.0 collective-permute-done.8.h0
  53.6 2.4 %last_and_correlation.1 = (f32[384,512]{1,0:T(8,128)S(1)}, f32[544,128]{1,0:T(8,128)S(1)}, f32[544,128]{1,0:T(8,128)S(1)}) custom-call(f32[384,512]{1,0:T(8,128)S(1)} %own_block.5.part_ref, bf16[5,384,384]{2,1,0:T(8,128)(2,1)S(1)} %bitcast.20, s32[4]{0:T(128)S(1)} %bitcast.31, s32[4]{0:T(128)S(1)} %pad_add_fusion.i_ref, ...), custom_call_target="tpu_custom_call" | custom-call | flops 1207959552 | bytes 2097152 | tf_op jit(solution)/shard_map/last_and_correlation/pallas_call | solution.py:314
  56.0 2.3 %collective-permute-start.12 = (f32[544,128]{1,0:T(8,128)S(1)}, f32[544,128]{1,0:T(8,128)S(1)}, u32[]{:S(2)}, u32[]{:S(2)}) collective-permute-start(f32[544,128]{1,0:T(8,128)S(1)} %get-tuple-element.12), channel_id=1, source_target_pairs={{0,1},{1,0},{2,3},{3,2},{4,5},{5,4},{6,7},{7,6},{8,9},{9,8},{10,11... | collective-permute-start | bytes 835592 | tf_op jit(solution)/shard_map/ppermute | solution.py:286
  58.3 1.2 collective-permute-done.12
  59.5 24.1 %all_to_all.20 = f32[32,1,2176]{2,1,0:T(1,128)S(1)} all-to-all(f32[32,1,2176]{2,1,0:T(1,128)S(1)} %bitcast.32), channel_id=1, replica_groups=mesh['z'=8,'x'=4,'y'=8,'c'=2] {'z','x'}, dimensions={0} | all-to-all | bytes 557056 | tf_op jit(solution)/shard_map/all_to_all | solution.py:325
  83.6 0.2 reduce_sum.18
  83.8 16.4 %all_to_all.21 = f32[8,17,128]{2,1,0:T(8,128)S(1)} all-to-all(f32[8,17,128]{2,1,0:T(8,128)S(1)} %broadcast_in_dim.22), channel_id=1, replica_groups=mesh['z'=8,'x'=4,'y'=8,'c'=2] {'y'}, dimensions={0} | all-to-all | bytes 139264 | tf_op jit(solution)/shard_map/all_to_all | solution.py:327
  100.3 0.1 broadcast_in_dim.24
  100.4 15.0 %all_to_all.22 = f32[32,1,2176]{2,1,0:T(1,128)S(1)} all-to-all(f32[32,1,2176]{2,1,0:T(1,128)S(1)} %broadcast_in_dim.24), channel_id=1, replica_groups=mesh['z'=8,'x'=4,'y'=8,'c'=2] {'z','x'}, dimensions={0} | all-to-all | bytes 557056 | tf_op jit(solution)/shard_map/all_to_all | solution.py:329
  115.4 6.2 %collective-permute-start.13 = (f32[544,128]{1,0:T(8,128)S(1)}, f32[544,128]{1,0:T(8,128)S(1)}, u32[]{:S(2)}, u32[]{:S(2)}) collective-permute-start(f32[544,128]{1,0:T(8,128)S(1)} %bitcast.27), channel_id=1, source_target_pairs={{0,1},{1,0},{2,3},{3,2},{4,5},{5,4},{6,7},{7,6},{8,9},{9,8},{10,11... | collective-permute-start | bytes 835592 | tf_op jit(solution)/shard_map/ppermute | solution.py:286
  121.6 1.0 collective-permute-done.13.other_ref
  122.6 14.3 %finish.1 = (bf16[384,512]{1,0:T(8,128)(2,1)}, f32[4,128]{1,0:T(4,128)}) custom-call(f32[544,128]{1,0:T(8,128)S(1)} %bitcast.28, f32[544,128]{1,0:T(8,128)S(1)} %collective-permute-done.13.other_ref, f32[384,512]{1,0:T(8,128)S(1)} %get-tuple-element.13.f_ref, s32[1]{0:T(128)} %bitcast.8.core_ref), custom_call_target="tpu_custom_call" | custom-call | flops 1207959552 | bytes 2097152 | tf_op jit(solution)/shard_map/finish/pallas_call | solution.py:334
  (3 shorter events, 0.1 us)
Async XLA Ops:
  0.6 17.0 %collective-permute-start.3 = (bf16[384,512]{1,0:T(8,128)(2,1)}, bf16[384,512]{1,0:T(8,128)(2,1)S(1)}, u32[]{:S(2)}, u32[]{:S(2)}) collective-permute-start(bf16[384,512]{1,0:T(8,128)(2,1)} %bitcast.21), channel_id=1, source_target_pairs={{16,32},{32,16},{48,64},{64,48},{80,96},{96,80},{112,128},{128,112... | collective-permute-start | bytes 1179656 | tf_op jit(solution)/shard_map/ppermute | solution.py:273
  1.3 16.3 %collective-permute-start.2 = (bf16[384,512]{1,0:T(8,128)(2,1)}, bf16[384,512]{1,0:T(8,128)(2,1)S(1)}, u32[]{:S(2)}, u32[]{:S(2)}) collective-permute-start(bf16[384,512]{1,0:T(8,128)(2,1)} %bitcast.22), channel_id=1, source_target_pairs={{0,16},{16,0},{32,48},{48,32},{64,80},{80,64},{96,112},{112,96},{1... | collective-permute-start | bytes 1179656 | tf_op jit(solution)/shard_map/ppermute | solution.py:273
  7.7 10.0 %collective-permute-start.1 = (bf16[384,512]{1,0:T(8,128)(2,1)}, bf16[384,512]{1,0:T(8,128)(2,1)S(1)}, u32[]{:S(2)}, u32[]{:S(2)}) collective-permute-start(bf16[384,512]{1,0:T(8,128)(2,1)} %bitcast.23), channel_id=1, source_target_pairs={{1,2},{2,1},{3,4},{4,3},{5,6},{6,5},{7,8},{8,7},{9,10},{10,9},{11,... | collective-permute-start | bytes 1179656 | tf_op jit(solution)/shard_map/ppermute | solution.py:273
  12.1 5.7 %collective-permute-start = (bf16[384,512]{1,0:T(8,128)(2,1)}, bf16[384,512]{1,0:T(8,128)(2,1)S(1)}, u32[]{:S(2)}, u32[]{:S(2)}) collective-permute-start(bf16[384,512]{1,0:T(8,128)(2,1)} %bitcast.24), channel_id=1, source_target_pairs={{0,1},{1,0},{2,3},{3,2},{4,5},{5,4},{6,7},{7,6},{8,9},{9,8},{10,11... | collective-permute-start | bytes 1179656 | tf_op jit(solution)/shard_map/ppermute | solution.py:273
  14.8 2.9 %copy-start.3 = (s32[1,1,4]{2,1,0:T(1,128)S(1)}, s32[1,1,4]{2,1,0:T(1,128)}, u32[]{:S(2)}) copy-start(s32[1,1,4]{2,1,0:T(1,128)} %param.7) | copy-start | bytes 52
  14.8 1.4 %copy-start = (bf16[1,1,5,384,384]{4,3,2,1,0:T(8,128)(2,1)S(1)}, bf16[1,1,5,384,384]{4,3,2,1,0:T(8,128)(2,1)}, u32[]{:S(2)}) copy-start(bf16[1,1,5,384,384]{4,3,2,1,0:T(8,128)(2,1)} %param.5) | copy-start | bytes 4423684
  16.2 1.0 copy-start.2
  17.2 1.4 %copy-start.1 = (bf16[1,1,5,384,384]{4,3,2,1,0:T(8,128)(2,1)S(1)}, bf16[1,1,5,384,384]{4,3,2,1,0:T(8,128)(2,1)}, u32[]{:S(2)}) copy-start(bf16[1,1,5,384,384]{4,3,2,1,0:T(8,128)(2,1)} %param.5) | copy-start | bytes 4423684
  19.9 13.2 %collective-permute-start.7 = (bf16[384,512]{1,0:T(8,128)(2,1)S(1)}, bf16[384,512]{1,0:T(8,128)(2,1)S(1)}, u32[]{:S(2)}, u32[]{:S(2)}) collective-permute-start(bf16[384,512]{1,0:T(8,128)(2,1)S(1)} %get-tuple-element.9.v_ref), channel_id=1, source_target_pairs={{16,32},{32,16},{48,64},{64,48},{80,96},{96,80},{112,128},{128,112... | collective-permute-start | bytes 1179656 | tf_op jit(solution)/shard_map/ppermute | solution.py:273
  20.6 14.8 %collective-permute-start.6 = (bf16[384,512]{1,0:T(8,128)(2,1)S(1)}, bf16[384,512]{1,0:T(8,128)(2,1)S(1)}, u32[]{:S(2)}, u32[]{:S(2)}) collective-permute-start(bf16[384,512]{1,0:T(8,128)(2,1)S(1)} %get-tuple-element.9.v_ref), channel_id=1, source_target_pairs={{0,16},{16,0},{32,48},{48,32},{64,80},{80,64},{96,112},{112,96},{1... | collective-permute-start | bytes 1179656 | tf_op jit(solution)/shard_map/ppermute | solution.py:273
  26.7 9.7 %collective-permute-start.5 = (bf16[384,512]{1,0:T(8,128)(2,1)S(1)}, bf16[384,512]{1,0:T(8,128)(2,1)S(1)}, u32[]{:S(2)}, u32[]{:S(2)}) collective-permute-start(bf16[384,512]{1,0:T(8,128)(2,1)S(1)} %get-tuple-element.9.v_ref), channel_id=1, source_target_pairs={{1,2},{2,1},{3,4},{4,3},{5,6},{6,5},{7,8},{8,7},{9,10},{10,9},{11,... | collective-permute-start | bytes 1179656 | tf_op jit(solution)/shard_map/ppermute | solution.py:273
  30.8 5.5 %collective-permute-start.4 = (bf16[384,512]{1,0:T(8,128)(2,1)S(1)}, bf16[384,512]{1,0:T(8,128)(2,1)S(1)}, u32[]{:S(2)}, u32[]{:S(2)}) collective-permute-start(bf16[384,512]{1,0:T(8,128)(2,1)S(1)} %get-tuple-element.9.v_ref), channel_id=1, source_target_pairs={{0,1},{1,0},{2,3},{3,2},{4,5},{5,4},{6,7},{7,6},{8,9},{9,8},{10,11... | collective-permute-start | bytes 1179656 | tf_op jit(solution)/shard_map/ppermute | solution.py:273
  37.6 12.7 %collective-permute-start.11 = (bf16[384,512]{1,0:T(8,128)(2,1)S(1)}, bf16[384,512]{1,0:T(8,128)(2,1)S(1)}, u32[]{:S(2)}, u32[]{:S(2)}) collective-permute-start(bf16[384,512]{1,0:T(8,128)(2,1)S(1)} %middle.1.v_ref), channel_id=1, source_target_pairs={{16,32},{32,16},{48,64},{64,48},{80,96},{96,80},{112,128},{128,112... | collective-permute-start | bytes 1179656 | tf_op jit(solution)/shard_map/ppermute | solution.py:273
  38.3 14.4 %collective-permute-start.10 = (bf16[384,512]{1,0:T(8,128)(2,1)S(1)}, bf16[384,512]{1,0:T(8,128)(2,1)S(1)}, u32[]{:S(2)}, u32[]{:S(2)}) collective-permute-start(bf16[384,512]{1,0:T(8,128)(2,1)S(1)} %middle.1.v_ref), channel_id=1, source_target_pairs={{0,16},{16,0},{32,48},{48,32},{64,80},{80,64},{96,112},{112,96},{1... | collective-permute-start | bytes 1179656 | tf_op jit(solution)/shard_map/ppermute | solution.py:273
  43.9 9.7 %collective-permute-start.9 = (bf16[384,512]{1,0:T(8,128)(2,1)S(1)}, bf16[384,512]{1,0:T(8,128)(2,1)S(1)}, u32[]{:S(2)}, u32[]{:S(2)}) collective-permute-start(bf16[384,512]{1,0:T(8,128)(2,1)S(1)} %middle.1.v_ref), channel_id=1, source_target_pairs={{1,2},{2,1},{3,4},{4,3},{5,6},{6,5},{7,8},{8,7},{9,10},{10,9},{11,... | collective-permute-start | bytes 1179656 | tf_op jit(solution)/shard_map/ppermute | solution.py:273
  48.0 5.5 %collective-permute-start.8 = (bf16[384,512]{1,0:T(8,128)(2,1)S(1)}, bf16[384,512]{1,0:T(8,128)(2,1)S(1)}, u32[]{:S(2)}, u32[]{:S(2)}) collective-permute-start(bf16[384,512]{1,0:T(8,128)(2,1)S(1)} %middle.1.v_ref), channel_id=1, source_target_pairs={{0,1},{1,0},{2,3},{3,2},{4,5},{5,4},{6,7},{7,6},{8,9},{9,8},{10,11... | collective-permute-start | bytes 1179656 | tf_op jit(solution)/shard_map/ppermute | solution.py:273
  56.0 3.5 %collective-permute-start.12 = (f32[544,128]{1,0:T(8,128)S(1)}, f32[544,128]{1,0:T(8,128)S(1)}, u32[]{:S(2)}, u32[]{:S(2)}) collective-permute-start(f32[544,128]{1,0:T(8,128)S(1)} %get-tuple-element.12), channel_id=1, source_target_pairs={{0,1},{1,0},{2,3},{3,2},{4,5},{5,4},{6,7},{7,6},{8,9},{9,8},{10,11... | collective-permute-start | bytes 835592 | tf_op jit(solution)/shard_map/ppermute | solution.py:286
  115.4 7.2 %collective-permute-start.13 = (f32[544,128]{1,0:T(8,128)S(1)}, f32[544,128]{1,0:T(8,128)S(1)}, u32[]{:S(2)}, u32[]{:S(2)}) collective-permute-start(f32[544,128]{1,0:T(8,128)S(1)} %bitcast.27), channel_id=1, source_target_pairs={{0,1},{1,0},{2,3},{3,2},{4,5},{5,4},{6,7},{7,6},{8,9},{9,8},{10,11... | collective-permute-start | bytes 835592 | tf_op jit(solution)/shard_map/ppermute | solution.py:286

commit v7 on v6

--- a/solution.py
+++ b/solution.py
@@ -30,14 +30,17 @@
     return lax.dot_general(a, b, (dims, ((), ())), preferred_element_type=F32)
 
 
-def halo_sum(c_ref, l_ref, i_ref, halos):
+def wide_kernel(c_ref, l_ref, i_ref, x_ref, y_ref):
     none = jnp.zeros(c_ref.shape[1:], c_ref.dtype)
-    left = []
     for k in range(4):
         index = i_ref[k]
-        left.append(jnp.where(l_ref[index - 1] != 0, c_ref[index], none))
-    right = jnp.concatenate([h[...] for h in halos], 0)
-    return dot(jnp.concatenate(left, 1), right, ((1,), (0,)))
+        at = slice(k % 2 * none.shape[1], (k % 2 + 1) * none.shape[1])
+        (x_ref if k < 2 else y_ref)[:, at] = jnp.where(l_ref[index - 1] != 0, c_ref[index], none)
+
+
+def halo_sum(part_ref, wide_ref, h0, h1):
+    halos = jnp.concatenate([h0[...], h1[...]], 0)
+    return part_ref[...] + dot(wide_ref[...], halos, ((1,), (0,)))
 
 
 def own_kernel(v_ref, c_ref, w_ref, o_ref):
@@ -45,14 +48,18 @@
     o_ref[...] = (w_ref[...] - CENTER) * v.astype(F32) + dot(c_ref[0], v, ((1,), (0,)))
 
 
-def first_kernel(part_ref, c_ref, l_ref, i_ref, h0, h1, h2, h3, o_ref, r_ref):
-    out = SCALE * (part_ref[...] + halo_sum(c_ref, l_ref, i_ref, (h0, h1, h2, h3)))
+def x_kernel(part_ref, wide_ref, h0, h1, o_ref):
+    o_ref[...] = halo_sum(part_ref, wide_ref, h0, h1)
+
+
+def first_kernel(part_ref, wide_ref, h0, h1, o_ref, r_ref):
+    out = SCALE * halo_sum(part_ref, wide_ref, h0, h1)
     o_ref[...] = out
     r_ref[...] = out.astype(jnp.bfloat16)
 
 
-def middle_kernel(part_ref, c_ref, l_ref, i_ref, h0, h1, h2, h3, p_ref, r_ref):
-    total = part_ref[...] + halo_sum(c_ref, l_ref, i_ref, (h0, h1, h2, h3))
+def middle_kernel(part_ref, wide_ref, h0, h1, p_ref, r_ref):
+    total = halo_sum(part_ref, wide_ref, h0, h1)
     r_ref[...] = (2.0 * SCALE * total - p_ref[...].astype(F32)).astype(jnp.bfloat16)
 
 
@@ -77,10 +84,8 @@
     return stack([high, low, middle, high, middle, high], axis)
 
 
-def last_kernel(part_ref, c_ref, l_ref, i_ref, h0, h1, h2, h3, p_ref, core_ref, *outs):
-    o_ref, keep_ref, send_ref, g_ref = outs
-    total = part_ref[...] + halo_sum(c_ref, l_ref, i_ref, (h0, h1, h2, h3))
-    out = 2.0 * SCALE * total - p_ref[...]
+def last_kernel(part_ref, wide_ref, h0, h1, p_ref, core_ref, o_ref, keep_ref, send_ref, g_ref):
+    out = 2.0 * SCALE * halo_sum(part_ref, wide_ref, h0, h1) - p_ref[...]
     o_ref[...] = out
     left, right = left_stack(out, 0), right_stack(out, 0)
     down, across = iotas()
@@ -274,12 +279,9 @@
 
 
 def neighbours(v):
-    return (
-        exchange(v, GY, 16, 0),
-        exchange(v, GY, 16, 1),
-        exchange(v, GX, 32, 0),
-        exchange(v, GX, 32, 1),
-    )
+    along_x = exchange(v, GX, 32, 1), exchange(v, GX, 32, 0)
+    along_y = exchange(v, GY, 16, 1), exchange(v, GY, 16, 0)
+    return along_x, along_y
 
 
 def swap(v):
@@ -294,7 +296,7 @@
     present = linked[0, 0]
     core = lax.axis_index("c").astype(jnp.int32)
     odd = lax.rem(lax.axis_index("x"), 2).astype(jnp.int32)
-    index = jnp.stack([4 - core, 3 + core, 2 - odd, 1 + odd])
+    index = jnp.stack([1 + odd, 2 - odd, 3 + core, 4 - core])
     core = core[None]
     full = shape(rows, width)
     half = shape(rows, width, dtype=jnp.bfloat16)
@@ -302,14 +304,19 @@
 
     own = call(own_kernel, full, [VMEM] * 3, "own_block", flops)
 
-    specs = [VMEM] * 2 + [SMEM] * 2 + [VMEM] * 4
+    pair = shape(rows, 2 * rows, dtype=jnp.bfloat16)
+    wide = call(wide_kernel, (pair, pair), [VMEM, SMEM, SMEM], "wide", 1)
+    wide_x, wide_y = wide(blocks, present, index)
+    specs = [VMEM] * 4
+    along_x = call(x_kernel, full, specs, "along_x", 2 * flops)
 
     def operands(v):
-        halos = neighbours(v)
-        return (own(v, blocks, weights), blocks, present, index, *halos)
-
-    x1, r1 = call(first_kernel, (full, half), specs, "first", 4 * flops)(*operands(v0))
-    r2 = call(middle_kernel, half, specs + [VMEM], "middle", 4 * flops)(*operands(r1), v0)
+        x_halos, y_halos = neighbours(v)
+        part = along_x(own(v, blocks, weights), wide_x, *x_halos)
+        return (part, wide_y, *y_halos)
+
+    x1, r1 = call(first_kernel, (full, half), specs, "first", 2 * flops)(*operands(v0))
+    r2 = call(middle_kernel, half, specs + [VMEM], "middle", 2 * flops)(*operands(r1), v0)
     piece = shape(PART, NB)
     filtered, keep, send = call(
         last_kernel,

time: 138 us -> 137 us (level)
  Pallas kernels: 20.5 us -> 22.4 us
  blocking collectives: 55.5 us -> 53.9 us
    pallas_call x5 -> x9, Pallas kernels: 3.73 us -> 6.25 us  [the longest x6 3.62 us: operands(): part = along_x(own(v, blocks, weights), wide_x, *x_halos)]
    all_to_all x1, blocking collectives: 16.4 us -> 14.7 us  [local(): lax.all_to_all(jnp.broadcast_to(part, (8, share // NB, NB)), 'y', 0, 0)]
    unnamed x8 -> x10, local copies, waits for them, and re-layouts: 3.24 us -> 3.55 us
  transfers between devices with their start and end apart: 14 -> 14, of which waited for: 6 -> 6; matrix products, arithmetic and copies ran while one was open for 1% -> 0% of each run, Pallas kernels for 1% -> 3%
where the time goes in v7:
time: 137 us; the launch traced here: 136 us
  blocking collectives  53.9 us (39%)
  starting transfers between devices  47.5 us (35%)
  Pallas kernels  22.4 us (16%)
  waiting for transfers between devices  7.54 us (6%)
  local copies, waits for them, and re-layouts  3.84 us (3%)
    ppermute x12, starting transfers between devices, exchange(): return lax.ppermute(v, axes, pairs)  38.8 us
    all_to_all x1, blocking collectives, local(): part = lax.all_to_all(summed.reshape(32, share), GX, 0, 0, tiled=True)  24.2 us
    all_to_all x1, blocking collectives, local(): lax.all_to_all(jnp.broadcast_to(total, (32, share)), GX, 0, 0, tiled=True)  15 us
    all_to_all x1, blocking collectives, local(): lax.all_to_all(jnp.broadcast_to(part, (8, share // NB, NB)), 'y', 0, 0)  14.7 us
    pallas_call x1, Pallas kernels, local(): call(functools.partial(finish_kernel, root), (half, shape(4, NB)), [VMEM]...  14.3 us
    ppermute x2, starting transfers between devices, swap(): return lax.ppermute(v, 'c', [(0, 1), (1, 0)])  8.66 us
    ppermute x12, waiting for transfers between devices, exchange(): return lax.ppermute(v, axes, pairs)  5.39 us
    pallas_call x6, Pallas kernels, operands(): part = along_x(own(v, blocks, weights), wide_x, *x_halos)  3.62 us
  transfers between devices with their start and end apart: 14, of which 6 were waited for; matrix products, arithmetic and copies ran while one was open for 0% of the time, Pallas kernels for 3%

profile of v7, /device:TPU:1, one launch (start us, length us, event | category | flops | bytes accessed | tf_op | source)
XLA Modules:
  0.0 136.4 jit_solution(885501153232088438)
XLA Ops:
  0.6 0.0 copy-start.4
  0.6 1.4 %collective-permute-start = (bf16[384,512]{1,0:T(8,128)(2,1)}, bf16[384,512]{1,0:T(8,128)(2,1)}, u32[]{:S(2)}, u32[]{:S(2)}) collective-permute-start(bf16[384,512]{1,0:T(8,128)(2,1)} %bitcast.19), channel_id=1, source_target_pairs={{16,32},{32,16},{48,64},{64,48},{80,96},{96,80},{112,128},{128,112... | collective-permute-start | bytes 1179656 | tf_op jit(solution)/shard_map/ppermute | solution.py:278
  2.1 5.7 %collective-permute-start.1 = (bf16[384,512]{1,0:T(8,128)(2,1)}, bf16[384,512]{1,0:T(8,128)(2,1)}, u32[]{:S(2)}, u32[]{:S(2)}) collective-permute-start(bf16[384,512]{1,0:T(8,128)(2,1)} %bitcast.20), channel_id=1, source_target_pairs={{0,16},{16,0},{32,48},{48,32},{64,80},{80,64},{96,112},{112,96},{1... | collective-permute-start | bytes 1179656 | tf_op jit(solution)/shard_map/ppermute | solution.py:278
  7.7 4.3 %collective-permute-start.2 = (bf16[384,512]{1,0:T(8,128)(2,1)}, bf16[384,512]{1,0:T(8,128)(2,1)S(1)}, u32[]{:S(2)}, u32[]{:S(2)}) collective-permute-start(bf16[384,512]{1,0:T(8,128)(2,1)} %bitcast.21), channel_id=1, source_target_pairs={{1,2},{2,1},{3,4},{4,3},{5,6},{6,5},{7,8},{8,7},{9,10},{10,9},{11,... | collective-permute-start | bytes 1179656 | tf_op jit(solution)/shard_map/ppermute | solution.py:278
  12.1 1.9 %collective-permute-start.3 = (bf16[384,512]{1,0:T(8,128)(2,1)}, bf16[384,512]{1,0:T(8,128)(2,1)}, u32[]{:S(2)}, u32[]{:S(2)}) collective-permute-start(bf16[384,512]{1,0:T(8,128)(2,1)} %bitcast.22), channel_id=1, source_target_pairs={{0,1},{1,0},{2,3},{3,2},{4,5},{5,4},{6,7},{7,6},{8,9},{9,8},{10,11... | collective-permute-start | bytes 1179656 | tf_op jit(solution)/shard_map/ppermute | solution.py:278
  14.0 0.1 pad_add_fusion.i_ref
  14.1 0.0 copy-start
  14.1 1.4 %copy-done = bf16[1,1,5,384,384]{4,3,2,1,0:T(8,128)(2,1)S(1)} copy-done((bf16[1,1,5,384,384]{4,3,2,1,0:T(8,128)(2,1)S(1)}, bf16[1,1,5,384,384]{4,3,2,1,0:T(8,128)(2,1)}, u32[]{:S(2)}) %copy-start) | copy-done | bytes 1474584
  15.5 0.0 copy-start.3
  15.5 0.7 copy-done.3
  16.1 0.0 copy-start.1
  16.1 0.7 wide.1
  16.8 0.0 copy-done.4
  16.8 0.1 copy.17.w_ref
  17.0 0.5 copy-done.1
  17.5 0.0 copy-start.2
  17.5 1.0 copy-done.2
  18.5 0.4 own_block.3.part_ref
  18.9 0.0 collective-permute-done.h0
  18.9 0.0 collective-permute-done.1.h1
  18.9 1.6 %along_x.3.part_ref = f32[384,512]{1,0:T(8,128)S(1)} custom-call(f32[384,512]{1,0:T(8,128)S(1)} %own_block.3.part_ref, bf16[384,768]{1,0:T(8,128)(2,1)S(1)} %get-tuple-element.11.wide_ref, bf16[384,512]{1,0:T(8,128)(2,1)} %collective-permute-done.h0, bf16[384,512]{1,0:T(8,128)(2,1)} %collective-permute-done.1.h1), custom_call_target="tpu_custom_call" | custom-call | flops 301989888 | bytes 2097152 | tf_op jit(solution)/shard_map/along_x/pallas_call | solution.py:315
  20.5 0.0 collective-permute-done.2.h0
  20.5 0.0 collective-permute-done.3.h1
  20.5 1.5 %first.1 = (f32[384,512]{1,0:T(8,128)S(1)}, bf16[384,512]{1,0:T(8,128)(2,1)S(1)}) custom-call(f32[384,512]{1,0:T(8,128)S(1)} %along_x.3.part_ref, bf16[384,768]{1,0:T(8,128)(2,1)S(1)} %get-tuple-element.12.wide_ref, bf16[384,512]{1,0:T(8,128)(2,1)S(1)} %collective-permute-done.2.h0, bf16[384,512]{1,0:T(8,128)(2,1)} %collective-permute-done.3.h1), custom_call_target="tpu_custom_call" | custom-call | flops 301989888 | bytes 2097152 | tf_op jit(solution)/shard_map/first/pallas_call | solution.py:318
  22.0 0.7 collective-permute-start.4
  22.7 6.1 %collective-permute-start.5 = (bf16[384,512]{1,0:T(8,128)(2,1)S(1)}, bf16[384,512]{1,0:T(8,128)(2,1)S(1)}, u32[]{:S(2)}, u32[]{:S(2)}) collective-permute-start(bf16[384,512]{1,0:T(8,128)(2,1)S(1)} %get-tuple-element.13.v_ref), channel_id=1, source_target_pairs={{0,16},{16,0},{32,48},{48,32},{64,80},{80,64},{96,112},{112,96},{1... | collective-permute-start | bytes 1179656 | tf_op jit(solution)/shard_map/ppermute | solution.py:278
  28.7 4.1 %collective-permute-start.6 = (bf16[384,512]{1,0:T(8,128)(2,1)S(1)}, bf16[384,512]{1,0:T(8,128)(2,1)S(1)}, u32[]{:S(2)}, u32[]{:S(2)}) collective-permute-start(bf16[384,512]{1,0:T(8,128)(2,1)S(1)} %get-tuple-element.13.v_ref), channel_id=1, source_target_pairs={{1,2},{2,1},{3,4},{4,3},{5,6},{6,5},{7,8},{8,7},{9,10},{10,9},{11,... | collective-permute-start | bytes 1179656 | tf_op jit(solution)/shard_map/ppermute | solution.py:278
  32.9 1.9 %collective-permute-start.7 = (bf16[384,512]{1,0:T(8,128)(2,1)S(1)}, bf16[384,512]{1,0:T(8,128)(2,1)S(1)}, u32[]{:S(2)}, u32[]{:S(2)}) collective-permute-start(bf16[384,512]{1,0:T(8,128)(2,1)S(1)} %get-tuple-element.13.v_ref), channel_id=1, source_target_pairs={{0,1},{1,0},{2,3},{3,2},{4,5},{5,4},{6,7},{7,6},{8,9},{9,8},{10,11... | collective-permute-start | bytes 1179656 | tf_op jit(solution)/shard_map/ppermute | solution.py:278
  34.8 0.4 own_block.4.part_ref
  35.2 0.0 collective-permute-done.4.h0
  35.2 2.2 %collective-permute-done.5.h1 = bf16[384,512]{1,0:T(8,128)(2,1)S(1)} collective-permute-done((bf16[384,512]{1,0:T(8,128)(2,1)S(1)}, bf16[384,512]{1,0:T(8,128)(2,1)S(1)}, u32[]{:S(2)}, u32[]{:S(2)}) %collective-permute-start.5) | collective-permute-done | bytes 393248 | tf_op jit(solution)/shard_map/ppermute | solution.py:278
  37.4 0.5 along_x.4.part_ref
  37.9 0.5 collective-permute-done.6.h0
  38.4 0.0 collective-permute-done.7.h1
  38.4 0.5 middle.1.v_ref
  38.9 0.7 collective-permute-start.8
  39.6 5.6 %collective-permute-start.9 = (bf16[384,512]{1,0:T(8,128)(2,1)S(1)}, bf16[384,512]{1,0:T(8,128)(2,1)S(1)}, u32[]{:S(2)}, u32[]{:S(2)}) collective-permute-start(bf16[384,512]{1,0:T(8,128)(2,1)S(1)} %middle.1.v_ref), channel_id=1, source_target_pairs={{0,16},{16,0},{32,48},{48,32},{64,80},{80,64},{96,112},{112,96},{1... | collective-permute-start | bytes 1179656 | tf_op jit(solution)/shard_map/ppermute | solution.py:278
  45.1 4.5 %collective-permute-start.10 = (bf16[384,512]{1,0:T(8,128)(2,1)S(1)}, bf16[384,512]{1,0:T(8,128)(2,1)S(1)}, u32[]{:S(2)}, u32[]{:S(2)}) collective-permute-start(bf16[384,512]{1,0:T(8,128)(2,1)S(1)} %middle.1.v_ref), channel_id=1, source_target_pairs={{1,2},{2,1},{3,4},{4,3},{5,6},{6,5},{7,8},{8,7},{9,10},{10,9},{11,... | collective-permute-start | bytes 1179656 | tf_op jit(solution)/shard_map/ppermute | solution.py:278
  49.7 1.9 %collective-permute-start.11 = (bf16[384,512]{1,0:T(8,128)(2,1)S(1)}, bf16[384,512]{1,0:T(8,128)(2,1)S(1)}, u32[]{:S(2)}, u32[]{:S(2)}) collective-permute-start(bf16[384,512]{1,0:T(8,128)(2,1)S(1)} %middle.1.v_ref), channel_id=1, source_target_pairs={{0,1},{1,0},{2,3},{3,2},{4,5},{5,4},{6,7},{7,6},{8,9},{9,8},{10,11... | collective-permute-start | bytes 1179656 | tf_op jit(solution)/shard_map/ppermute | solution.py:278
  51.6 0.4 own_block.5.part_ref
  52.0 0.0 collective-permute-done.8.h0
  52.0 1.4 %collective-permute-done.9.h1 = bf16[384,512]{1,0:T(8,128)(2,1)S(1)} collective-permute-done((bf16[384,512]{1,0:T(8,128)(2,1)S(1)}, bf16[384,512]{1,0:T(8,128)(2,1)S(1)}, u32[]{:S(2)}, u32[]{:S(2)}) %collective-permute-start.9) | collective-permute-done | bytes 393248 | tf_op jit(solution)/shard_map/ppermute | solution.py:278
  53.4 0.5 along_x.5.part_ref
  53.9 1.3 collective-permute-done.10.h0
  55.1 0.0 collective-permute-done.11.h1
  55.1 1.9 %last_and_correlation.1 = (f32[384,512]{1,0:T(8,128)S(1)}, f32[544,128]{1,0:T(8,128)S(1)}, f32[544,128]{1,0:T(8,128)S(1)}) custom-call(f32[384,512]{1,0:T(8,128)S(1)} %along_x.5.part_ref, bf16[384,768]{1,0:T(8,128)(2,1)S(1)} %get-tuple-element.12.wide_ref, bf16[384,512]{1,0:T(8,128)(2,1)S(1)} %collective-permute-done.10.h0, ...), custom_call_target="tpu_custom_call" | custom-call | flops 1207959552 | bytes 2097152 | tf_op jit(solution)/shard_map/last_and_correlation/pallas_call | solution.py:321
  57.0 2.5 %collective-permute-start.12 = (f32[544,128]{1,0:T(8,128)S(1)}, f32[544,128]{1,0:T(8,128)S(1)}, u32[]{:S(2)}, u32[]{:S(2)}) collective-permute-start(f32[544,128]{1,0:T(8,128)S(1)} %get-tuple-element.16), channel_id=1, source_target_pairs={{0,1},{1,0},{2,3},{3,2},{4,5},{5,4},{6,7},{7,6},{8,9},{9,8},{10,11... | collective-permute-start | bytes 835592 | tf_op jit(solution)/shard_map/ppermute | solution.py:288
  59.5 1.2 collective-permute-done.12
  60.6 24.2 %all_to_all.20 = f32[32,1,2176]{2,1,0:T(1,128)S(1)} all-to-all(f32[32,1,2176]{2,1,0:T(1,128)S(1)} %bitcast.28), channel_id=1, replica_groups=mesh['z'=8,'x'=4,'y'=8,'c'=2] {'z','x'}, dimensions={0} | all-to-all | bytes 557056 | tf_op jit(solution)/shard_map/all_to_all | solution.py:332
  84.8 0.2 reduce_sum.18
  85.0 14.7 %all_to_all.21 = f32[8,17,128]{2,1,0:T(8,128)S(1)} all-to-all(f32[8,17,128]{2,1,0:T(8,128)S(1)} %broadcast_in_dim.22), channel_id=1, replica_groups=mesh['z'=8,'x'=4,'y'=8,'c'=2] {'y'}, dimensions={0} | all-to-all | bytes 139264 | tf_op jit(solution)/shard_map/all_to_all | solution.py:334
  99.8 0.1 broadcast_in_dim.24
  99.9 15.0 %all_to_all.22 = f32[32,1,2176]{2,1,0:T(1,128)S(1)} all-to-all(f32[32,1,2176]{2,1,0:T(1,128)S(1)} %broadcast_in_dim.24), channel_id=1, replica_groups=mesh['z'=8,'x'=4,'y'=8,'c'=2] {'z','x'}, dimensions={0} | all-to-all | bytes 557056 | tf_op jit(solution)/shard_map/all_to_all | solution.py:336
  114.9 6.2 %collective-permute-start.13 = (f32[544,128]{1,0:T(8,128)S(1)}, f32[544,128]{1,0:T(8,128)S(1)}, u32[]{:S(2)}, u32[]{:S(2)}) collective-permute-start(f32[544,128]{1,0:T(8,128)S(1)} %bitcast.25), channel_id=1, source_target_pairs={{0,1},{1,0},{2,3},{3,2},{4,5},{5,4},{6,7},{7,6},{8,9},{9,8},{10,11... | collective-permute-start | bytes 835592 | tf_op jit(solution)/shard_map/ppermute | solution.py:288
  121.1 1.0 collective-permute-done.13.other_ref
  122.1 14.3 %finish.1 = (bf16[384,512]{1,0:T(8,128)(2,1)}, f32[4,128]{1,0:T(4,128)}) custom-call(f32[544,128]{1,0:T(8,128)S(1)} %bitcast.26, f32[544,128]{1,0:T(8,128)S(1)} %collective-permute-done.13.other_ref, f32[384,512]{1,0:T(8,128)S(1)} %get-tuple-element.17.f_ref, s32[1]{0:T(128)} %bitcast.8.core_ref), custom_call_target="tpu_custom_call" | custom-call | flops 1207959552 | bytes 2097152 | tf_op jit(solution)/shard_map/finish/pallas_call | solution.py:341
  (3 shorter events, 0.1 us)
Async XLA Ops:
  0.6 16.2 %copy-start.4 = (f32[1,1,384]{2,1,0:T(1,128)S(1)}, f32[1,1,384]{2,1,0:T(1,128)}, u32[]{:S(2)}) copy-start(f32[1,1,384]{2,1,0:T(1,128)} %param.6) | copy-start | bytes 4612
  0.6 18.2 %collective-permute-start = (bf16[384,512]{1,0:T(8,128)(2,1)}, bf16[384,512]{1,0:T(8,128)(2,1)}, u32[]{:S(2)}, u32[]{:S(2)}) collective-permute-start(bf16[384,512]{1,0:T(8,128)(2,1)} %bitcast.19), channel_id=1, source_target_pairs={{16,32},{32,16},{48,64},{64,48},{80,96},{96,80},{112,128},{128,112... | collective-permute-start | bytes 1179656 | tf_op jit(solution)/shard_map/ppermute | solution.py:278
  2.1 16.8 %collective-permute-start.1 = (bf16[384,512]{1,0:T(8,128)(2,1)}, bf16[384,512]{1,0:T(8,128)(2,1)}, u32[]{:S(2)}, u32[]{:S(2)}) collective-permute-start(bf16[384,512]{1,0:T(8,128)(2,1)} %bitcast.20), channel_id=1, source_target_pairs={{0,16},{16,0},{32,48},{48,32},{64,80},{80,64},{96,112},{112,96},{1... | collective-permute-start | bytes 1179656 | tf_op jit(solution)/shard_map/ppermute | solution.py:278
  7.7 12.7 %collective-permute-start.2 = (bf16[384,512]{1,0:T(8,128)(2,1)}, bf16[384,512]{1,0:T(8,128)(2,1)S(1)}, u32[]{:S(2)}, u32[]{:S(2)}) collective-permute-start(bf16[384,512]{1,0:T(8,128)(2,1)} %bitcast.21), channel_id=1, source_target_pairs={{1,2},{2,1},{3,4},{4,3},{5,6},{6,5},{7,8},{8,7},{9,10},{10,9},{11,... | collective-permute-start | bytes 1179656 | tf_op jit(solution)/shard_map/ppermute | solution.py:278
  12.1 8.4 %collective-permute-start.3 = (bf16[384,512]{1,0:T(8,128)(2,1)}, bf16[384,512]{1,0:T(8,128)(2,1)}, u32[]{:S(2)}, u32[]{:S(2)}) collective-permute-start(bf16[384,512]{1,0:T(8,128)(2,1)} %bitcast.22), channel_id=1, source_target_pairs={{0,1},{1,0},{2,3},{3,2},{4,5},{5,4},{6,7},{7,6},{8,9},{9,8},{10,11... | collective-permute-start | bytes 1179656 | tf_op jit(solution)/shard_map/ppermute | solution.py:278
  14.1 1.4 %copy-start = (bf16[1,1,5,384,384]{4,3,2,1,0:T(8,128)(2,1)S(1)}, bf16[1,1,5,384,384]{4,3,2,1,0:T(8,128)(2,1)}, u32[]{:S(2)}) copy-start(bf16[1,1,5,384,384]{4,3,2,1,0:T(8,128)(2,1)} %param.5) | copy-start | bytes 4423684
  15.5 0.7 copy-start.3
  16.1 1.4 %copy-start.1 = (bf16[1,1,5,384,384]{4,3,2,1,0:T(8,128)(2,1)S(1)}, bf16[1,1,5,384,384]{4,3,2,1,0:T(8,128)(2,1)}, u32[]{:S(2)}) copy-start(bf16[1,1,5,384,384]{4,3,2,1,0:T(8,128)(2,1)} %param.5) | copy-start | bytes 4423684
  17.5 1.0 copy-start.2
  22.0 13.2 %collective-permute-start.4 = (bf16[384,512]{1,0:T(8,128)(2,1)S(1)}, bf16[384,512]{1,0:T(8,128)(2,1)S(1)}, u32[]{:S(2)}, u32[]{:S(2)}) collective-permute-start(bf16[384,512]{1,0:T(8,128)(2,1)S(1)} %get-tuple-element.13.v_ref), channel_id=1, source_target_pairs={{16,32},{32,16},{48,64},{64,48},{80,96},{96,80},{112,128},{128,112... | collective-permute-start | bytes 1179656 | tf_op jit(solution)/shard_map/ppermute | solution.py:278
  22.7 14.8 %collective-permute-start.5 = (bf16[384,512]{1,0:T(8,128)(2,1)S(1)}, bf16[384,512]{1,0:T(8,128)(2,1)S(1)}, u32[]{:S(2)}, u32[]{:S(2)}) collective-permute-start(bf16[384,512]{1,0:T(8,128)(2,1)S(1)} %get-tuple-element.13.v_ref), channel_id=1, source_target_pairs={{0,16},{16,0},{32,48},{48,32},{64,80},{80,64},{96,112},{112,96},{1... | collective-permute-start | bytes 1179656 | tf_op jit(solution)/shard_map/ppermute | solution.py:278
  28.7 9.7 %collective-permute-start.6 = (bf16[384,512]{1,0:T(8,128)(2,1)S(1)}, bf16[384,512]{1,0:T(8,128)(2,1)S(1)}, u32[]{:S(2)}, u32[]{:S(2)}) collective-permute-start(bf16[384,512]{1,0:T(8,128)(2,1)S(1)} %get-tuple-element.13.v_ref), channel_id=1, source_target_pairs={{1,2},{2,1},{3,4},{4,3},{5,6},{6,5},{7,8},{8,7},{9,10},{10,9},{11,... | collective-permute-start | bytes 1179656 | tf_op jit(solution)/shard_map/ppermute | solution.py:278
  32.9 5.5 %collective-permute-start.7 = (bf16[384,512]{1,0:T(8,128)(2,1)S(1)}, bf16[384,512]{1,0:T(8,128)(2,1)S(1)}, u32[]{:S(2)}, u32[]{:S(2)}) collective-permute-start(bf16[384,512]{1,0:T(8,128)(2,1)S(1)} %get-tuple-element.13.v_ref), channel_id=1, source_target_pairs={{0,1},{1,0},{2,3},{3,2},{4,5},{5,4},{6,7},{7,6},{8,9},{9,8},{10,11... | collective-permute-start | bytes 1179656 | tf_op jit(solution)/shard_map/ppermute | solution.py:278
  38.9 13.1 %collective-permute-start.8 = (bf16[384,512]{1,0:T(8,128)(2,1)S(1)}, bf16[384,512]{1,0:T(8,128)(2,1)S(1)}, u32[]{:S(2)}, u32[]{:S(2)}) collective-permute-start(bf16[384,512]{1,0:T(8,128)(2,1)S(1)} %middle.1.v_ref), channel_id=1, source_target_pairs={{16,32},{32,16},{48,64},{64,48},{80,96},{96,80},{112,128},{128,112... | collective-permute-start | bytes 1179656 | tf_op jit(solution)/shard_map/ppermute | solution.py:278
  39.6 13.8 %collective-permute-start.9 = (bf16[384,512]{1,0:T(8,128)(2,1)S(1)}, bf16[384,512]{1,0:T(8,128)(2,1)S(1)}, u32[]{:S(2)}, u32[]{:S(2)}) collective-permute-start(bf16[384,512]{1,0:T(8,128)(2,1)S(1)} %middle.1.v_ref), channel_id=1, source_target_pairs={{0,16},{16,0},{32,48},{48,32},{64,80},{80,64},{96,112},{112,96},{1... | collective-permute-start | bytes 1179656 | tf_op jit(solution)/shard_map/ppermute | solution.py:278
  45.1 10.0 %collective-permute-start.10 = (bf16[384,512]{1,0:T(8,128)(2,1)S(1)}, bf16[384,512]{1,0:T(8,128)(2,1)S(1)}, u32[]{:S(2)}, u32[]{:S(2)}) collective-permute-start(bf16[384,512]{1,0:T(8,128)(2,1)S(1)} %middle.1.v_ref), channel_id=1, source_target_pairs={{1,2},{2,1},{3,4},{4,3},{5,6},{6,5},{7,8},{8,7},{9,10},{10,9},{11,... | collective-permute-start | bytes 1179656 | tf_op jit(solution)/shard_map/ppermute | solution.py:278
  49.7 5.4 %collective-permute-start.11 = (bf16[384,512]{1,0:T(8,128)(2,1)S(1)}, bf16[384,512]{1,0:T(8,128)(2,1)S(1)}, u32[]{:S(2)}, u32[]{:S(2)}) collective-permute-start(bf16[384,512]{1,0:T(8,128)(2,1)S(1)} %middle.1.v_ref), channel_id=1, source_target_pairs={{0,1},{1,0},{2,3},{3,2},{4,5},{5,4},{6,7},{7,6},{8,9},{9,8},{10,11... | collective-permute-start | bytes 1179656 | tf_op jit(solution)/shard_map/ppermute | solution.py:278
  57.0 3.6 %collective-permute-start.12 = (f32[544,128]{1,0:T(8,128)S(1)}, f32[544,128]{1,0:T(8,128)S(1)}, u32[]{:S(2)}, u32[]{:S(2)}) collective-permute-start(f32[544,128]{1,0:T(8,128)S(1)} %get-tuple-element.16), channel_id=1, source_target_pairs={{0,1},{1,0},{2,3},{3,2},{4,5},{5,4},{6,7},{7,6},{8,9},{9,8},{10,11... | collective-permute-start | bytes 835592 | tf_op jit(solution)/shard_map/ppermute | solution.py:288
  114.9 7.2 %collective-permute-start.13 = (f32[544,128]{1,0:T(8,128)S(1)}, f32[544,128]{1,0:T(8,128)S(1)}, u32[]{:S(2)}, u32[]{:S(2)}) collective-permute-start(f32[544,128]{1,0:T(8,128)S(1)} %bitcast.25), channel_id=1, source_target_pairs={{0,1},{1,0},{2,3},{3,2},{4,5},{5,4},{6,7},{7,6},{8,9},{9,8},{10,11... | collective-permute-start | bytes 835592 | tf_op jit(solution)/shard_map/ppermute | solution.py:288

commit v8 on v7

--- a/solution.py
+++ b/solution.py
@@ -30,7 +30,8 @@
     return lax.dot_general(a, b, (dims, ((), ())), preferred_element_type=F32)
 
 
-def wide_kernel(c_ref, l_ref, i_ref, x_ref, y_ref):
+def wide_kernel(c_ref, l_ref, i_ref, own_ref, x_ref, y_ref):
+    own_ref[...] = c_ref[0]
     none = jnp.zeros(c_ref.shape[1:], c_ref.dtype)
     for k in range(4):
         index = i_ref[k]
@@ -45,7 +46,7 @@
 
 def own_kernel(v_ref, c_ref, w_ref, o_ref):
     v = v_ref[...]
-    o_ref[...] = (w_ref[...] - CENTER) * v.astype(F32) + dot(c_ref[0], v, ((1,), (0,)))
+    o_ref[...] = (w_ref[...] - CENTER) * v.astype(F32) + dot(c_ref[...], v, ((1,), (0,)))
 
 
 def x_kernel(part_ref, wide_ref, h0, h1, o_ref):
@@ -305,14 +306,15 @@
     own = call(own_kernel, full, [VMEM] * 3, "own_block", flops)
 
     pair = shape(rows, 2 * rows, dtype=jnp.bfloat16)
-    wide = call(wide_kernel, (pair, pair), [VMEM, SMEM, SMEM], "wide", 1)
-    wide_x, wide_y = wide(blocks, present, index)
+    square = shape(rows, rows, dtype=jnp.bfloat16)
+    wide = call(wide_kernel, (square, pair, pair), [VMEM, SMEM, SMEM], "wide", flops)
+    block, wide_x, wide_y = wide(blocks, present, index)
     specs = [VMEM] * 4
     along_x = call(x_kernel, full, specs, "along_x", 2 * flops)
 
     def operands(v):
         x_halos, y_halos = neighbours(v)
-        part = along_x(own(v, blocks, weights), wide_x, *x_halos)
+        part = along_x(own(v, block, weights), wide_x, *x_halos)
         return (part, wide_y, *y_halos)
 
     x1, r1 = call(first_kernel, (full, half), specs, "first", 2 * flops)(*operands(v0))

time: 137 us -> 135 us (0.985)
  Pallas kernels: 22.4 us -> 20.3 us
    unnamed x10 -> x6, local copies, waits for them, and re-layouts: 3.55 us -> 2.03 us
  transfers between devices with their start and end apart: 14 -> 14, of which waited for: 6 -> 6; matrix products, arithmetic and copies ran while one was open for 0% -> 1% of each run, Pallas kernels for 3% -> 2%
where the time goes in v8:
time: 135 us
  blocking collectives  55 us (41%)
  starting transfers between devices  47.6 us (35%)
  Pallas kernels  20.3 us (15%)
  waiting for transfers between devices  7.54 us (6%)
  local copies, waits for them, and re-layouts  3 us (2%)
    ppermute x12, starting transfers between devices, exchange(): return lax.ppermute(v, axes, pairs)  38.9 us
    all_to_all x1, blocking collectives, local(): part = lax.all_to_all(summed.reshape(32, share), GX, 0, 0, tiled=True)  24.5 us
    all_to_all x1, blocking collectives, local(): lax.all_to_all(jnp.broadcast_to(part, (8, share // NB, NB)), 'y', 0, 0)  15.6 us
    all_to_all x1, blocking collectives, local(): lax.all_to_all(jnp.broadcast_to(total, (32, share)), GX, 0, 0, tiled=True)  15 us
    pallas_call x1, Pallas kernels, local(): call(functools.partial(finish_kernel, root), (half, shape(4, NB)), [VMEM]...  14.3 us
    ppermute x2, starting transfers between devices, swap(): return lax.ppermute(v, 'c', [(0, 1), (1, 0)])  8.66 us
    ppermute x12, waiting for transfers between devices, exchange(): return lax.ppermute(v, axes, pairs)  5.39 us
  transfers between devices with their start and end apart: 14, of which 6 were waited for; matrix products, arithmetic and copies ran while one was open for 1% of the time, Pallas kernels for 2%

profile of v8, /device:TPU:1, one launch (start us, length us, event | category | flops | bytes accessed | tf_op | source)
XLA Modules:
  0.0 134.7 jit_solution(12219108582286385173)
XLA Ops:
  0.6 0.0 copy-start
  0.6 0.8 collective-permute-start
  1.5 6.4 %collective-permute-start.1 = (bf16[384,512]{1,0:T(8,128)(2,1)}, bf16[384,512]{1,0:T(8,128)(2,1)S(1)}, u32[]{:S(2)}, u32[]{:S(2)}) collective-permute-start(bf16[384,512]{1,0:T(8,128)(2,1)} %bitcast.16), channel_id=1, source_target_pairs={{0,16},{16,0},{32,48},{48,32},{64,80},{80,64},{96,112},{112,96},{1... | collective-permute-start | bytes 1179656 | tf_op jit(solution)/shard_map/ppermute | solution.py:279
  7.9 4.3 %collective-permute-start.2 = (bf16[384,512]{1,0:T(8,128)(2,1)}, bf16[384,512]{1,0:T(8,128)(2,1)S(1)}, u32[]{:S(2)}, u32[]{:S(2)}) collective-permute-start(bf16[384,512]{1,0:T(8,128)(2,1)} %bitcast.17), channel_id=1, source_target_pairs={{1,2},{2,1},{3,4},{4,3},{5,6},{6,5},{7,8},{8,7},{9,10},{10,9},{11,... | collective-permute-start | bytes 1179656 | tf_op jit(solution)/shard_map/ppermute | solution.py:279
  12.2 1.9 %collective-permute-start.3 = (bf16[384,512]{1,0:T(8,128)(2,1)}, bf16[384,512]{1,0:T(8,128)(2,1)S(1)}, u32[]{:S(2)}, u32[]{:S(2)}) collective-permute-start(bf16[384,512]{1,0:T(8,128)(2,1)} %bitcast.18), channel_id=1, source_target_pairs={{0,1},{1,0},{2,3},{3,2},{4,5},{5,4},{6,7},{7,6},{8,9},{9,8},{10,11... | collective-permute-start | bytes 1179656 | tf_op jit(solution)/shard_map/ppermute | solution.py:279
  14.1 0.8 copy.17.w_ref
  14.9 0.1 pad_add_fusion.i_ref
  15.0 0.0 copy-start.1
  15.0 1.4 %copy-done.1 = bf16[1,1,5,384,384]{4,3,2,1,0:T(8,128)(2,1)S(1)} copy-done((bf16[1,1,5,384,384]{4,3,2,1,0:T(8,128)(2,1)S(1)}, bf16[1,1,5,384,384]{4,3,2,1,0:T(8,128)(2,1)}, u32[]{:S(2)}) %copy-start.1) | copy-done | bytes 1474584
  16.4 0.0 copy-start.2
  16.4 0.7 copy-done.2
  17.1 0.7 wide.1
  17.8 0.0 copy-done
  17.8 0.4 own_block.3.part_ref
  18.2 0.0 collective-permute-done.h0
  18.2 0.0 collective-permute-done.1.h1
  18.2 0.5 along_x.3.part_ref
  18.7 0.0 collective-permute-done.2.h0
  18.7 0.0 collective-permute-done.3.h1
  18.7 0.5 first.1
  19.2 0.7 collective-permute-start.4
  19.9 6.1 %collective-permute-start.5 = (bf16[384,512]{1,0:T(8,128)(2,1)S(1)}, bf16[384,512]{1,0:T(8,128)(2,1)S(1)}, u32[]{:S(2)}, u32[]{:S(2)}) collective-permute-start(bf16[384,512]{1,0:T(8,128)(2,1)S(1)} %get-tuple-element.15.v_ref), channel_id=1, source_target_pairs={{0,16},{16,0},{32,48},{48,32},{64,80},{80,64},{96,112},{112,96},{1... | collective-permute-start | bytes 1179656 | tf_op jit(solution)/shard_map/ppermute | solution.py:279
  25.9 4.1 %collective-permute-start.6 = (bf16[384,512]{1,0:T(8,128)(2,1)S(1)}, bf16[384,512]{1,0:T(8,128)(2,1)S(1)}, u32[]{:S(2)}, u32[]{:S(2)}) collective-permute-start(bf16[384,512]{1,0:T(8,128)(2,1)S(1)} %get-tuple-element.15.v_ref), channel_id=1, source_target_pairs={{1,2},{2,1},{3,4},{4,3},{5,6},{6,5},{7,8},{8,7},{9,10},{10,9},{11,... | collective-permute-start | bytes 1179656 | tf_op jit(solution)/shard_map/ppermute | solution.py:279
  30.1 1.9 %collective-permute-start.7 = (bf16[384,512]{1,0:T(8,128)(2,1)S(1)}, bf16[384,512]{1,0:T(8,128)(2,1)S(1)}, u32[]{:S(2)}, u32[]{:S(2)}) collective-permute-start(bf16[384,512]{1,0:T(8,128)(2,1)S(1)} %get-tuple-element.15.v_ref), channel_id=1, source_target_pairs={{0,1},{1,0},{2,3},{3,2},{4,5},{5,4},{6,7},{7,6},{8,9},{9,8},{10,11... | collective-permute-start | bytes 1179656 | tf_op jit(solution)/shard_map/ppermute | solution.py:279
  32.0 0.4 own_block.4.part_ref
  32.4 0.0 collective-permute-done.4.h0
  32.4 2.2 %collective-permute-done.5.h1 = bf16[384,512]{1,0:T(8,128)(2,1)S(1)} collective-permute-done((bf16[384,512]{1,0:T(8,128)(2,1)S(1)}, bf16[384,512]{1,0:T(8,128)(2,1)S(1)}, u32[]{:S(2)}, u32[]{:S(2)}) %collective-permute-start.5) | collective-permute-done | bytes 393248 | tf_op jit(solution)/shard_map/ppermute | solution.py:279
  34.6 0.5 along_x.4.part_ref
  35.1 0.5 collective-permute-done.6.h0
  35.6 0.0 collective-permute-done.7.h1
  35.6 0.5 middle.1.v_ref
  36.1 0.7 collective-permute-start.8
  36.7 5.6 %collective-permute-start.9 = (bf16[384,512]{1,0:T(8,128)(2,1)S(1)}, bf16[384,512]{1,0:T(8,128)(2,1)S(1)}, u32[]{:S(2)}, u32[]{:S(2)}) collective-permute-start(bf16[384,512]{1,0:T(8,128)(2,1)S(1)} %middle.1.v_ref), channel_id=1, source_target_pairs={{0,16},{16,0},{32,48},{48,32},{64,80},{80,64},{96,112},{112,96},{1... | collective-permute-start | bytes 1179656 | tf_op jit(solution)/shard_map/ppermute | solution.py:279
  42.3 4.5 %collective-permute-start.10 = (bf16[384,512]{1,0:T(8,128)(2,1)S(1)}, bf16[384,512]{1,0:T(8,128)(2,1)S(1)}, u32[]{:S(2)}, u32[]{:S(2)}) collective-permute-start(bf16[384,512]{1,0:T(8,128)(2,1)S(1)} %middle.1.v_ref), channel_id=1, source_target_pairs={{1,2},{2,1},{3,4},{4,3},{5,6},{6,5},{7,8},{8,7},{9,10},{10,9},{11,... | collective-permute-start | bytes 1179656 | tf_op jit(solution)/shard_map/ppermute | solution.py:279
  46.9 1.9 %collective-permute-start.11 = (bf16[384,512]{1,0:T(8,128)(2,1)S(1)}, bf16[384,512]{1,0:T(8,128)(2,1)S(1)}, u32[]{:S(2)}, u32[]{:S(2)}) collective-permute-start(bf16[384,512]{1,0:T(8,128)(2,1)S(1)} %middle.1.v_ref), channel_id=1, source_target_pairs={{0,1},{1,0},{2,3},{3,2},{4,5},{5,4},{6,7},{7,6},{8,9},{9,8},{10,11... | collective-permute-start | bytes 1179656 | tf_op jit(solution)/shard_map/ppermute | solution.py:279
  48.8 0.4 own_block.5.part_ref
  49.2 0.0 collective-permute-done.8.h0
  49.2 1.4 %collective-permute-done.9.h1 = bf16[384,512]{1,0:T(8,128)(2,1)S(1)} collective-permute-done((bf16[384,512]{1,0:T(8,128)(2,1)S(1)}, bf16[384,512]{1,0:T(8,128)(2,1)S(1)}, u32[]{:S(2)}, u32[]{:S(2)}) %collective-permute-start.9) | collective-permute-done | bytes 393248 | tf_op jit(solution)/shard_map/ppermute | solution.py:279
  50.6 0.5 along_x.5.part_ref
  51.0 1.3 collective-permute-done.10.h0
  52.3 0.0 collective-permute-done.11.h1
  52.3 1.8 %last_and_correlation.1 = (f32[384,512]{1,0:T(8,128)S(1)}, f32[544,128]{1,0:T(8,128)S(1)}, f32[544,128]{1,0:T(8,128)S(1)}) custom-call(f32[384,512]{1,0:T(8,128)S(1)} %along_x.5.part_ref, bf16[384,768]{1,0:T(8,128)(2,1)S(1)} %get-tuple-element.14.wide_ref, bf16[384,512]{1,0:T(8,128)(2,1)S(1)} %collective-permute-done.10.h0, ...), custom_call_target="tpu_custom_call" | custom-call | flops 1207959552 | bytes 2097152 | tf_op jit(solution)/shard_map/last_and_correlation/pallas_call | solution.py:323
  54.2 2.5 %collective-permute-start.12 = (f32[544,128]{1,0:T(8,128)S(1)}, f32[544,128]{1,0:T(8,128)S(1)}, u32[]{:S(2)}, u32[]{:S(2)}) collective-permute-start(f32[544,128]{1,0:T(8,128)S(1)} %get-tuple-element.18), channel_id=1, source_target_pairs={{0,1},{1,0},{2,3},{3,2},{4,5},{5,4},{6,7},{7,6},{8,9},{9,8},{10,11... | collective-permute-start | bytes 835592 | tf_op jit(solution)/shard_map/ppermute | solution.py:289
  56.6 1.2 collective-permute-done.12
  57.8 24.5 %all_to_all.20 = f32[32,1,2176]{2,1,0:T(1,128)S(1)} all-to-all(f32[32,1,2176]{2,1,0:T(1,128)S(1)} %bitcast.25), channel_id=1, replica_groups=mesh['z'=8,'x'=4,'y'=8,'c'=2] {'z','x'}, dimensions={0} | all-to-all | bytes 557056 | tf_op jit(solution)/shard_map/all_to_all | solution.py:334
  82.3 0.2 reduce_sum.18
  82.5 15.6 %all_to_all.21 = f32[8,17,128]{2,1,0:T(8,128)S(1)} all-to-all(f32[8,17,128]{2,1,0:T(8,128)S(1)} %broadcast_in_dim.22), channel_id=1, replica_groups=mesh['z'=8,'x'=4,'y'=8,'c'=2] {'y'}, dimensions={0} | all-to-all | bytes 139264 | tf_op jit(solution)/shard_map/all_to_all | solution.py:336
  98.1 0.1 broadcast_in_dim.24
  98.2 15.0 %all_to_all.22 = f32[32,1,2176]{2,1,0:T(1,128)S(1)} all-to-all(f32[32,1,2176]{2,1,0:T(1,128)S(1)} %broadcast_in_dim.24), channel_id=1, replica_groups=mesh['z'=8,'x'=4,'y'=8,'c'=2] {'z','x'}, dimensions={0} | all-to-all | bytes 557056 | tf_op jit(solution)/shard_map/all_to_all | solution.py:338
  113.2 6.2 %collective-permute-start.13 = (f32[544,128]{1,0:T(8,128)S(1)}, f32[544,128]{1,0:T(8,128)S(1)}, u32[]{:S(2)}, u32[]{:S(2)}) collective-permute-start(f32[544,128]{1,0:T(8,128)S(1)} %bitcast.22), channel_id=1, source_target_pairs={{0,1},{1,0},{2,3},{3,2},{4,5},{5,4},{6,7},{7,6},{8,9},{9,8},{10,11... | collective-permute-start | bytes 835592 | tf_op jit(solution)/shard_map/ppermute | solution.py:289
  119.4 1.0 collective-permute-done.13.other_ref
  120.4 14.3 %finish.1 = (bf16[384,512]{1,0:T(8,128)(2,1)}, f32[4,128]{1,0:T(4,128)}) custom-call(f32[544,128]{1,0:T(8,128)S(1)} %bitcast.23, f32[544,128]{1,0:T(8,128)S(1)} %collective-permute-done.13.other_ref, f32[384,512]{1,0:T(8,128)S(1)} %get-tuple-element.19.f_ref, s32[1]{0:T(128)} %bitcast.8.core_ref), custom_call_target="tpu_custom_call" | custom-call | flops 1207959552 | bytes 2097152 | tf_op jit(solution)/shard_map/finish/pallas_call | solution.py:343
  (3 shorter events, 0.1 us)
Async XLA Ops:
  0.6 17.1 %copy-start = (bf16[1,1,384,512]{3,2,1,0:T(8,128)(2,1)S(1)}, bf16[1,1,384,512]{3,2,1,0:T(8,128)(2,1)}, u32[]{:S(2)}) copy-start(bf16[1,1,384,512]{3,2,1,0:T(8,128)(2,1)} %param.4) | copy-start | bytes 1179652
  0.6 17.5 %collective-permute-start = (bf16[384,512]{1,0:T(8,128)(2,1)}, bf16[384,512]{1,0:T(8,128)(2,1)S(1)}, u32[]{:S(2)}, u32[]{:S(2)}) collective-permute-start(bf16[384,512]{1,0:T(8,128)(2,1)} %bitcast.15), channel_id=1, source_target_pairs={{16,32},{32,16},{48,64},{64,48},{80,96},{96,80},{112,128},{128,112... | collective-permute-start | bytes 1179656 | tf_op jit(solution)/shard_map/ppermute | solution.py:279
  1.5 16.7 %collective-permute-start.1 = (bf16[384,512]{1,0:T(8,128)(2,1)}, bf16[384,512]{1,0:T(8,128)(2,1)S(1)}, u32[]{:S(2)}, u32[]{:S(2)}) collective-permute-start(bf16[384,512]{1,0:T(8,128)(2,1)} %bitcast.16), channel_id=1, source_target_pairs={{0,16},{16,0},{32,48},{48,32},{64,80},{80,64},{96,112},{112,96},{1... | collective-permute-start | bytes 1179656 | tf_op jit(solution)/shard_map/ppermute | solution.py:279
  7.9 10.8 %collective-permute-start.2 = (bf16[384,512]{1,0:T(8,128)(2,1)}, bf16[384,512]{1,0:T(8,128)(2,1)S(1)}, u32[]{:S(2)}, u32[]{:S(2)}) collective-permute-start(bf16[384,512]{1,0:T(8,128)(2,1)} %bitcast.17), channel_id=1, source_target_pairs={{1,2},{2,1},{3,4},{4,3},{5,6},{6,5},{7,8},{8,7},{9,10},{10,9},{11,... | collective-permute-start | bytes 1179656 | tf_op jit(solution)/shard_map/ppermute | solution.py:279
  12.2 6.5 %collective-permute-start.3 = (bf16[384,512]{1,0:T(8,128)(2,1)}, bf16[384,512]{1,0:T(8,128)(2,1)S(1)}, u32[]{:S(2)}, u32[]{:S(2)}) collective-permute-start(bf16[384,512]{1,0:T(8,128)(2,1)} %bitcast.18), channel_id=1, source_target_pairs={{0,1},{1,0},{2,3},{3,2},{4,5},{5,4},{6,7},{7,6},{8,9},{9,8},{10,11... | collective-permute-start | bytes 1179656 | tf_op jit(solution)/shard_map/ppermute | solution.py:279
  15.0 1.4 %copy-start.1 = (bf16[1,1,5,384,384]{4,3,2,1,0:T(8,128)(2,1)S(1)}, bf16[1,1,5,384,384]{4,3,2,1,0:T(8,128)(2,1)}, u32[]{:S(2)}) copy-start(bf16[1,1,5,384,384]{4,3,2,1,0:T(8,128)(2,1)} %param.5) | copy-start | bytes 4423684
  16.4 0.7 copy-start.2
  19.2 13.2 %collective-permute-start.4 = (bf16[384,512]{1,0:T(8,128)(2,1)S(1)}, bf16[384,512]{1,0:T(8,128)(2,1)S(1)}, u32[]{:S(2)}, u32[]{:S(2)}) collective-permute-start(bf16[384,512]{1,0:T(8,128)(2,1)S(1)} %get-tuple-element.15.v_ref), channel_id=1, source_target_pairs={{16,32},{32,16},{48,64},{64,48},{80,96},{96,80},{112,128},{128,112... | collective-permute-start | bytes 1179656 | tf_op jit(solution)/shard_map/ppermute | solution.py:279
  19.9 14.8 %collective-permute-start.5 = (bf16[384,512]{1,0:T(8,128)(2,1)S(1)}, bf16[384,512]{1,0:T(8,128)(2,1)S(1)}, u32[]{:S(2)}, u32[]{:S(2)}) collective-permute-start(bf16[384,512]{1,0:T(8,128)(2,1)S(1)} %get-tuple-element.15.v_ref), channel_id=1, source_target_pairs={{0,16},{16,0},{32,48},{48,32},{64,80},{80,64},{96,112},{112,96},{1... | collective-permute-start | bytes 1179656 | tf_op jit(solution)/shard_map/ppermute | solution.py:279
  25.9 9.7 %collective-permute-start.6 = (bf16[384,512]{1,0:T(8,128)(2,1)S(1)}, bf16[384,512]{1,0:T(8,128)(2,1)S(1)}, u32[]{:S(2)}, u32[]{:S(2)}) collective-permute-start(bf16[384,512]{1,0:T(8,128)(2,1)S(1)} %get-tuple-element.15.v_ref), channel_id=1, source_target_pairs={{1,2},{2,1},{3,4},{4,3},{5,6},{6,5},{7,8},{8,7},{9,10},{10,9},{11,... | collective-permute-start | bytes 1179656 | tf_op jit(solution)/shard_map/ppermute | solution.py:279
  30.1 5.5 %collective-permute-start.7 = (bf16[384,512]{1,0:T(8,128)(2,1)S(1)}, bf16[384,512]{1,0:T(8,128)(2,1)S(1)}, u32[]{:S(2)}, u32[]{:S(2)}) collective-permute-start(bf16[384,512]{1,0:T(8,128)(2,1)S(1)} %get-tuple-element.15.v_ref), channel_id=1, source_target_pairs={{0,1},{1,0},{2,3},{3,2},{4,5},{5,4},{6,7},{7,6},{8,9},{9,8},{10,11... | collective-permute-start | bytes 1179656 | tf_op jit(solution)/shard_map/ppermute | solution.py:279
  36.1 13.1 %collective-permute-start.8 = (bf16[384,512]{1,0:T(8,128)(2,1)S(1)}, bf16[384,512]{1,0:T(8,128)(2,1)S(1)}, u32[]{:S(2)}, u32[]{:S(2)}) collective-permute-start(bf16[384,512]{1,0:T(8,128)(2,1)S(1)} %middle.1.v_ref), channel_id=1, source_target_pairs={{16,32},{32,16},{48,64},{64,48},{80,96},{96,80},{112,128},{128,112... | collective-permute-start | bytes 1179656 | tf_op jit(solution)/shard_map/ppermute | solution.py:279
  36.7 13.8 %collective-permute-start.9 = (bf16[384,512]{1,0:T(8,128)(2,1)S(1)}, bf16[384,512]{1,0:T(8,128)(2,1)S(1)}, u32[]{:S(2)}, u32[]{:S(2)}) collective-permute-start(bf16[384,512]{1,0:T(8,128)(2,1)S(1)} %middle.1.v_ref), channel_id=1, source_target_pairs={{0,16},{16,0},{32,48},{48,32},{64,80},{80,64},{96,112},{112,96},{1... | collective-permute-start | bytes 1179656 | tf_op jit(solution)/shard_map/ppermute | solution.py:279
  42.3 10.0 %collective-permute-start.10 = (bf16[384,512]{1,0:T(8,128)(2,1)S(1)}, bf16[384,512]{1,0:T(8,128)(2,1)S(1)}, u32[]{:S(2)}, u32[]{:S(2)}) collective-permute-start(bf16[384,512]{1,0:T(8,128)(2,1)S(1)} %middle.1.v_ref), channel_id=1, source_target_pairs={{1,2},{2,1},{3,4},{4,3},{5,6},{6,5},{7,8},{8,7},{9,10},{10,9},{11,... | collective-permute-start | bytes 1179656 | tf_op jit(solution)/shard_map/ppermute | solution.py:279
  46.9 5.4 %collective-permute-start.11 = (bf16[384,512]{1,0:T(8,128)(2,1)S(1)}, bf16[384,512]{1,0:T(8,128)(2,1)S(1)}, u32[]{:S(2)}, u32[]{:S(2)}) collective-permute-start(bf16[384,512]{1,0:T(8,128)(2,1)S(1)} %middle.1.v_ref), channel_id=1, source_target_pairs={{0,1},{1,0},{2,3},{3,2},{4,5},{5,4},{6,7},{7,6},{8,9},{9,8},{10,11... | collective-permute-start | bytes 1179656 | tf_op jit(solution)/shard_map/ppermute | solution.py:279
  54.2 3.6 %collective-permute-start.12 = (f32[544,128]{1,0:T(8,128)S(1)}, f32[544,128]{1,0:T(8,128)S(1)}, u32[]{:S(2)}, u32[]{:S(2)}) collective-permute-start(f32[544,128]{1,0:T(8,128)S(1)} %get-tuple-element.18), channel_id=1, source_target_pairs={{0,1},{1,0},{2,3},{3,2},{4,5},{5,4},{6,7},{7,6},{8,9},{9,8},{10,11... | collective-permute-start | bytes 835592 | tf_op jit(solution)/shard_map/ppermute | solution.py:289
  113.2 7.2 %collective-permute-start.13 = (f32[544,128]{1,0:T(8,128)S(1)}, f32[544,128]{1,0:T(8,128)S(1)}, u32[]{:S(2)}, u32[]{:S(2)}) collective-permute-start(f32[544,128]{1,0:T(8,128)S(1)} %bitcast.22), channel_id=1, source_target_pairs={{0,1},{1,0},{2,3},{3,2},{4,5},{5,4},{6,7},{7,6},{8,9},{9,8},{10,11... | collective-permute-start | bytes 835592 | tf_op jit(solution)/shard_map/ppermute | solution.py:289

commit v9 on v8

--- a/solution.py
+++ b/solution.py
@@ -332,9 +332,9 @@
     summed = keep + swap(send)
     share = PART * NB // 32
     part = lax.all_to_all(summed.reshape(32, share), GX, 0, 0, tiled=True)
-    part = part.reshape(32, share).sum(0).reshape(1, share // NB, NB)
-    part = lax.all_to_all(jnp.broadcast_to(part, (8, share // NB, NB)), "y", 0, 0)
-    total = part.sum(0).reshape(1, share)
+    part = part.reshape(32, share).sum(0, keepdims=True)
+    part = lax.all_to_all(jnp.broadcast_to(part, (8, share)), "y", 0, 0, tiled=True)
+    total = part.reshape(8, share).sum(0, keepdims=True)
     mine = lax.all_to_all(jnp.broadcast_to(total, (32, share)), GX, 0, 0, tiled=True)
     mine = mine.reshape(PART, NB)
     other = swap(mine)

time: 135 us -> 135 us (level)
  no operation moved by 1% of the time
where the time goes in v9:
time: 135 us; the launch traced here: 134 us
  blocking collectives  54.7 us (41%)
  starting transfers between devices  47.6 us (35%)
  Pallas kernels  20.3 us (15%)
  waiting for transfers between devices  7.54 us (6%)
  local copies, waits for them, and re-layouts  3.03 us (2%)
    ppermute x12, starting transfers between devices, exchange(): return lax.ppermute(v, axes, pairs)  38.9 us
    all_to_all x1, blocking collectives, local(): part = lax.all_to_all(summed.reshape(32, share), GX, 0, 0, tiled=True)  24.5 us
    all_to_all x1, blocking collectives, local(): lax.all_to_all(jnp.broadcast_to(part, (8, share)), 'y', 0, 0, tiled=True)  15.2 us
    all_to_all x1, blocking collectives, local(): lax.all_to_all(jnp.broadcast_to(total, (32, share)), GX, 0, 0, tiled=True)  15 us
    pallas_call x1, Pallas kernels, local(): call(functools.partial(finish_kernel, root), (half, shape(4, NB)), [VMEM]...  14.3 us
    ppermute x2, starting transfers between devices, swap(): return lax.ppermute(v, 'c', [(0, 1), (1, 0)])  8.65 us
    ppermute x12, waiting for transfers between devices, exchange(): return lax.ppermute(v, axes, pairs)  5.39 us
  transfers between devices with their start and end apart: 14, of which 6 were waited for; matrix products, arithmetic and copies ran while one was open for 1% of the time, Pallas kernels for 2%

profile of v9, /device:TPU:1, one launch (start us, length us, event | category | flops | bytes accessed | tf_op | source)
XLA Modules:
  0.0 134.4 jit_solution(8290315906112529751)
XLA Ops:
  0.6 0.0 copy-start
  0.6 0.8 collective-permute-start
  1.5 6.4 %collective-permute-start.1 = (bf16[384,512]{1,0:T(8,128)(2,1)}, bf16[384,512]{1,0:T(8,128)(2,1)S(1)}, u32[]{:S(2)}, u32[]{:S(2)}) collective-permute-start(bf16[384,512]{1,0:T(8,128)(2,1)} %bitcast.14), channel_id=1, source_target_pairs={{0,16},{16,0},{32,48},{48,32},{64,80},{80,64},{96,112},{112,96},{1... | collective-permute-start | bytes 1179656 | tf_op jit(solution)/shard_map/ppermute | solution.py:279
  7.9 4.3 %collective-permute-start.2 = (bf16[384,512]{1,0:T(8,128)(2,1)}, bf16[384,512]{1,0:T(8,128)(2,1)S(1)}, u32[]{:S(2)}, u32[]{:S(2)}) collective-permute-start(bf16[384,512]{1,0:T(8,128)(2,1)} %bitcast.15), channel_id=1, source_target_pairs={{1,2},{2,1},{3,4},{4,3},{5,6},{6,5},{7,8},{8,7},{9,10},{10,9},{11,... | collective-permute-start | bytes 1179656 | tf_op jit(solution)/shard_map/ppermute | solution.py:279
  12.2 1.9 %collective-permute-start.3 = (bf16[384,512]{1,0:T(8,128)(2,1)}, bf16[384,512]{1,0:T(8,128)(2,1)S(1)}, u32[]{:S(2)}, u32[]{:S(2)}) collective-permute-start(bf16[384,512]{1,0:T(8,128)(2,1)} %bitcast.16), channel_id=1, source_target_pairs={{0,1},{1,0},{2,3},{3,2},{4,5},{5,4},{6,7},{7,6},{8,9},{9,8},{10,11... | collective-permute-start | bytes 1179656 | tf_op jit(solution)/shard_map/ppermute | solution.py:279
  14.1 0.8 copy.17.w_ref
  14.9 0.1 pad_add_fusion.i_ref
  15.0 0.0 copy-start.1
  15.0 1.4 %copy-done.1 = bf16[1,1,5,384,384]{4,3,2,1,0:T(8,128)(2,1)S(1)} copy-done((bf16[1,1,5,384,384]{4,3,2,1,0:T(8,128)(2,1)S(1)}, bf16[1,1,5,384,384]{4,3,2,1,0:T(8,128)(2,1)}, u32[]{:S(2)}) %copy-start.1) | copy-done | bytes 1474584
  16.4 0.0 copy-start.2
  16.4 0.7 copy-done.2
  17.1 0.7 wide.1
  17.8 0.0 copy-done
  17.8 0.4 own_block.3.part_ref
  18.2 0.0 collective-permute-done.h0
  18.2 0.0 collective-permute-done.1.h1
  18.2 0.5 along_x.3.part_ref
  18.7 0.0 collective-permute-done.2.h0
  18.7 0.0 collective-permute-done.3.h1
  18.7 0.5 first.1
  19.2 0.7 collective-permute-start.4
  19.9 6.1 %collective-permute-start.5 = (bf16[384,512]{1,0:T(8,128)(2,1)S(1)}, bf16[384,512]{1,0:T(8,128)(2,1)S(1)}, u32[]{:S(2)}, u32[]{:S(2)}) collective-permute-start(bf16[384,512]{1,0:T(8,128)(2,1)S(1)} %get-tuple-element.15.v_ref), channel_id=1, source_target_pairs={{0,16},{16,0},{32,48},{48,32},{64,80},{80,64},{96,112},{112,96},{1... | collective-permute-start | bytes 1179656 | tf_op jit(solution)/shard_map/ppermute | solution.py:279
  25.9 4.1 %collective-permute-start.6 = (bf16[384,512]{1,0:T(8,128)(2,1)S(1)}, bf16[384,512]{1,0:T(8,128)(2,1)S(1)}, u32[]{:S(2)}, u32[]{:S(2)}) collective-permute-start(bf16[384,512]{1,0:T(8,128)(2,1)S(1)} %get-tuple-element.15.v_ref), channel_id=1, source_target_pairs={{1,2},{2,1},{3,4},{4,3},{5,6},{6,5},{7,8},{8,7},{9,10},{10,9},{11,... | collective-permute-start | bytes 1179656 | tf_op jit(solution)/shard_map/ppermute | solution.py:279
  30.1 1.9 %collective-permute-start.7 = (bf16[384,512]{1,0:T(8,128)(2,1)S(1)}, bf16[384,512]{1,0:T(8,128)(2,1)S(1)}, u32[]{:S(2)}, u32[]{:S(2)}) collective-permute-start(bf16[384,512]{1,0:T(8,128)(2,1)S(1)} %get-tuple-element.15.v_ref), channel_id=1, source_target_pairs={{0,1},{1,0},{2,3},{3,2},{4,5},{5,4},{6,7},{7,6},{8,9},{9,8},{10,11... | collective-permute-start | bytes 1179656 | tf_op jit(solution)/shard_map/ppermute | solution.py:279
  32.0 0.4 own_block.4.part_ref
  32.4 0.0 collective-permute-done.4.h0
  32.4 2.2 %collective-permute-done.5.h1 = bf16[384,512]{1,0:T(8,128)(2,1)S(1)} collective-permute-done((bf16[384,512]{1,0:T(8,128)(2,1)S(1)}, bf16[384,512]{1,0:T(8,128)(2,1)S(1)}, u32[]{:S(2)}, u32[]{:S(2)}) %collective-permute-start.5) | collective-permute-done | bytes 393248 | tf_op jit(solution)/shard_map/ppermute | solution.py:279
  34.6 0.5 along_x.4.part_ref
  35.1 0.5 collective-permute-done.6.h0
  35.6 0.0 collective-permute-done.7.h1
  35.6 0.5 middle.1.v_ref
  36.1 0.7 collective-permute-start.8
  36.7 5.6 %collective-permute-start.9 = (bf16[384,512]{1,0:T(8,128)(2,1)S(1)}, bf16[384,512]{1,0:T(8,128)(2,1)S(1)}, u32[]{:S(2)}, u32[]{:S(2)}) collective-permute-start(bf16[384,512]{1,0:T(8,128)(2,1)S(1)} %middle.1.v_ref), channel_id=1, source_target_pairs={{0,16},{16,0},{32,48},{48,32},{64,80},{80,64},{96,112},{112,96},{1... | collective-permute-start | bytes 1179656 | tf_op jit(solution)/shard_map/ppermute | solution.py:279
  42.3 4.5 %collective-permute-start.10 = (bf16[384,512]{1,0:T(8,128)(2,1)S(1)}, bf16[384,512]{1,0:T(8,128)(2,1)S(1)}, u32[]{:S(2)}, u32[]{:S(2)}) collective-permute-start(bf16[384,512]{1,0:T(8,128)(2,1)S(1)} %middle.1.v_ref), channel_id=1, source_target_pairs={{1,2},{2,1},{3,4},{4,3},{5,6},{6,5},{7,8},{8,7},{9,10},{10,9},{11,... | collective-permute-start | bytes 1179656 | tf_op jit(solution)/shard_map/ppermute | solution.py:279
  46.9 1.9 %collective-permute-start.11 = (bf16[384,512]{1,0:T(8,128)(2,1)S(1)}, bf16[384,512]{1,0:T(8,128)(2,1)S(1)}, u32[]{:S(2)}, u32[]{:S(2)}) collective-permute-start(bf16[384,512]{1,0:T(8,128)(2,1)S(1)} %middle.1.v_ref), channel_id=1, source_target_pairs={{0,1},{1,0},{2,3},{3,2},{4,5},{5,4},{6,7},{7,6},{8,9},{9,8},{10,11... | collective-permute-start | bytes 1179656 | tf_op jit(solution)/shard_map/ppermute | solution.py:279
  48.8 0.4 own_block.5.part_ref
  49.2 0.0 collective-permute-done.8.h0
  49.2 1.4 %collective-permute-done.9.h1 = bf16[384,512]{1,0:T(8,128)(2,1)S(1)} collective-permute-done((bf16[384,512]{1,0:T(8,128)(2,1)S(1)}, bf16[384,512]{1,0:T(8,128)(2,1)S(1)}, u32[]{:S(2)}, u32[]{:S(2)}) %collective-permute-start.9) | collective-permute-done | bytes 393248 | tf_op jit(solution)/shard_map/ppermute | solution.py:279
  50.6 0.5 along_x.5.part_ref
  51.0 1.3 collective-permute-done.10.h0
  52.3 0.0 collective-permute-done.11.h1
  52.3 1.8 %last_and_correlation.1 = (f32[384,512]{1,0:T(8,128)S(1)}, f32[544,128]{1,0:T(8,128)S(1)}, f32[544,128]{1,0:T(8,128)S(1)}) custom-call(f32[384,512]{1,0:T(8,128)S(1)} %along_x.5.part_ref, bf16[384,768]{1,0:T(8,128)(2,1)S(1)} %get-tuple-element.14.wide_ref, bf16[384,512]{1,0:T(8,128)(2,1)S(1)} %collective-permute-done.10.h0, ...), custom_call_target="tpu_custom_call" | custom-call | flops 1207959552 | bytes 2097152 | tf_op jit(solution)/shard_map/last_and_correlation/pallas_call | solution.py:323
  54.2 2.5 %collective-permute-start.12 = (f32[544,128]{1,0:T(8,128)S(1)}, f32[544,128]{1,0:T(8,128)S(1)}, u32[]{:S(2)}, u32[]{:S(2)}) collective-permute-start(f32[544,128]{1,0:T(8,128)S(1)} %get-tuple-element.18), channel_id=1, source_target_pairs={{0,1},{1,0},{2,3},{3,2},{4,5},{5,4},{6,7},{7,6},{8,9},{9,8},{10,11... | collective-permute-start | bytes 835592 | tf_op jit(solution)/shard_map/ppermute | solution.py:289
  56.6 1.2 collective-permute-done.12
  57.8 24.5 %all_to_all.21 = f32[32,1,2176]{2,1,0:T(1,128)S(1)} all-to-all(f32[32,1,2176]{2,1,0:T(1,128)S(1)} %bitcast.23), channel_id=1, replica_groups=mesh['z'=8,'x'=4,'y'=8,'c'=2] {'z','x'}, dimensions={0} | all-to-all | bytes 557056 | tf_op jit(solution)/shard_map/all_to_all | solution.py:334
  82.3 0.2 reduce_sum.18
  82.5 15.2 %all_to_all.22 = f32[8,1,2176]{2,1,0:T(1,128)S(1)} all-to-all(f32[8,1,2176]{2,1,0:T(1,128)S(1)} %broadcast_in_dim.9), channel_id=1, replica_groups=mesh['z'=8,'x'=4,'y'=8,'c'=2] {'y'}, dimensions={0} | all-to-all | bytes 139264 | tf_op jit(solution)/shard_map/all_to_all | solution.py:336
  97.8 0.1 reduce_sum.19
  97.8 0.1 broadcast_in_dim.20
  98.0 15.0 %all_to_all.23 = f32[32,1,2176]{2,1,0:T(1,128)S(1)} all-to-all(f32[32,1,2176]{2,1,0:T(1,128)S(1)} %broadcast_in_dim.20), channel_id=1, replica_groups=mesh['z'=8,'x'=4,'y'=8,'c'=2] {'z','x'}, dimensions={0} | all-to-all | bytes 557056 | tf_op jit(solution)/shard_map/all_to_all | solution.py:338
  113.0 6.2 %collective-permute-start.13 = (f32[544,128]{1,0:T(8,128)S(1)}, f32[544,128]{1,0:T(8,128)S(1)}, u32[]{:S(2)}, u32[]{:S(2)}) collective-permute-start(f32[544,128]{1,0:T(8,128)S(1)} %bitcast.20), channel_id=1, source_target_pairs={{0,1},{1,0},{2,3},{3,2},{4,5},{5,4},{6,7},{7,6},{8,9},{9,8},{10,11... | collective-permute-start | bytes 835592 | tf_op jit(solution)/shard_map/ppermute | solution.py:289
  119.1 1.0 collective-permute-done.13.other_ref
  120.1 14.3 %finish.1 = (bf16[384,512]{1,0:T(8,128)(2,1)}, f32[4,128]{1,0:T(4,128)}) custom-call(f32[544,128]{1,0:T(8,128)S(1)} %bitcast.21, f32[544,128]{1,0:T(8,128)S(1)} %collective-permute-done.13.other_ref, f32[384,512]{1,0:T(8,128)S(1)} %get-tuple-element.19.f_ref, s32[1]{0:T(128)} %bitcast.8.core_ref), custom_call_target="tpu_custom_call" | custom-call | flops 1207959552 | bytes 2097152 | tf_op jit(solution)/shard_map/finish/pallas_call | solution.py:343
  (2 shorter events, 0.1 us)
Async XLA Ops:
  0.6 17.1 %copy-start = (bf16[1,1,384,512]{3,2,1,0:T(8,128)(2,1)S(1)}, bf16[1,1,384,512]{3,2,1,0:T(8,128)(2,1)}, u32[]{:S(2)}) copy-start(bf16[1,1,384,512]{3,2,1,0:T(8,128)(2,1)} %param.4) | copy-start | bytes 1179652
  0.6 17.5 %collective-permute-start = (bf16[384,512]{1,0:T(8,128)(2,1)}, bf16[384,512]{1,0:T(8,128)(2,1)S(1)}, u32[]{:S(2)}, u32[]{:S(2)}) collective-permute-start(bf16[384,512]{1,0:T(8,128)(2,1)} %bitcast.13), channel_id=1, source_target_pairs={{16,32},{32,16},{48,64},{64,48},{80,96},{96,80},{112,128},{128,112... | collective-permute-start | bytes 1179656 | tf_op jit(solution)/shard_map/ppermute | solution.py:279
  1.5 16.7 %collective-permute-start.1 = (bf16[384,512]{1,0:T(8,128)(2,1)}, bf16[384,512]{1,0:T(8,128)(2,1)S(1)}, u32[]{:S(2)}, u32[]{:S(2)}) collective-permute-start(bf16[384,512]{1,0:T(8,128)(2,1)} %bitcast.14), channel_id=1, source_target_pairs={{0,16},{16,0},{32,48},{48,32},{64,80},{80,64},{96,112},{112,96},{1... | collective-permute-start | bytes 1179656 | tf_op jit(solution)/shard_map/ppermute | solution.py:279
  7.9 10.8 %collective-permute-start.2 = (bf16[384,512]{1,0:T(8,128)(2,1)}, bf16[384,512]{1,0:T(8,128)(2,1)S(1)}, u32[]{:S(2)}, u32[]{:S(2)}) collective-permute-start(bf16[384,512]{1,0:T(8,128)(2,1)} %bitcast.15), channel_id=1, source_target_pairs={{1,2},{2,1},{3,4},{4,3},{5,6},{6,5},{7,8},{8,7},{9,10},{10,9},{11,... | collective-permute-start | bytes 1179656 | tf_op jit(solution)/shard_map/ppermute | solution.py:279
  12.2 6.5 %collective-permute-start.3 = (bf16[384,512]{1,0:T(8,128)(2,1)}, bf16[384,512]{1,0:T(8,128)(2,1)S(1)}, u32[]{:S(2)}, u32[]{:S(2)}) collective-permute-start(bf16[384,512]{1,0:T(8,128)(2,1)} %bitcast.16), channel_id=1, source_target_pairs={{0,1},{1,0},{2,3},{3,2},{4,5},{5,4},{6,7},{7,6},{8,9},{9,8},{10,11... | collective-permute-start | bytes 1179656 | tf_op jit(solution)/shard_map/ppermute | solution.py:279
  15.0 1.4 %copy-start.1 = (bf16[1,1,5,384,384]{4,3,2,1,0:T(8,128)(2,1)S(1)}, bf16[1,1,5,384,384]{4,3,2,1,0:T(8,128)(2,1)}, u32[]{:S(2)}) copy-start(bf16[1,1,5,384,384]{4,3,2,1,0:T(8,128)(2,1)} %param.5) | copy-start | bytes 4423684
  16.4 0.7 copy-start.2
  19.2 13.2 %collective-permute-start.4 = (bf16[384,512]{1,0:T(8,128)(2,1)S(1)}, bf16[384,512]{1,0:T(8,128)(2,1)S(1)}, u32[]{:S(2)}, u32[]{:S(2)}) collective-permute-start(bf16[384,512]{1,0:T(8,128)(2,1)S(1)} %get-tuple-element.15.v_ref), channel_id=1, source_target_pairs={{16,32},{32,16},{48,64},{64,48},{80,96},{96,80},{112,128},{128,112... | collective-permute-start | bytes 1179656 | tf_op jit(solution)/shard_map/ppermute | solution.py:279
  19.9 14.8 %collective-permute-start.5 = (bf16[384,512]{1,0:T(8,128)(2,1)S(1)}, bf16[384,512]{1,0:T(8,128)(2,1)S(1)}, u32[]{:S(2)}, u32[]{:S(2)}) collective-permute-start(bf16[384,512]{1,0:T(8,128)(2,1)S(1)} %get-tuple-element.15.v_ref), channel_id=1, source_target_pairs={{0,16},{16,0},{32,48},{48,32},{64,80},{80,64},{96,112},{112,96},{1... | collective-permute-start | bytes 1179656 | tf_op jit(solution)/shard_map/ppermute | solution.py:279
  25.9 9.7 %collective-permute-start.6 = (bf16[384,512]{1,0:T(8,128)(2,1)S(1)}, bf16[384,512]{1,0:T(8,128)(2,1)S(1)}, u32[]{:S(2)}, u32[]{:S(2)}) collective-permute-start(bf16[384,512]{1,0:T(8,128)(2,1)S(1)} %get-tuple-element.15.v_ref), channel_id=1, source_target_pairs={{1,2},{2,1},{3,4},{4,3},{5,6},{6,5},{7,8},{8,7},{9,10},{10,9},{11,... | collective-permute-start | bytes 1179656 | tf_op jit(solution)/shard_map/ppermute | solution.py:279
  30.1 5.5 %collective-permute-start.7 = (bf16[384,512]{1,0:T(8,128)(2,1)S(1)}, bf16[384,512]{1,0:T(8,128)(2,1)S(1)}, u32[]{:S(2)}, u32[]{:S(2)}) collective-permute-start(bf16[384,512]{1,0:T(8,128)(2,1)S(1)} %get-tuple-element.15.v_ref), channel_id=1, source_target_pairs={{0,1},{1,0},{2,3},{3,2},{4,5},{5,4},{6,7},{7,6},{8,9},{9,8},{10,11... | collective-permute-start | bytes 1179656 | tf_op jit(solution)/shard_map/ppermute | solution.py:279
  36.1 13.1 %collective-permute-start.8 = (bf16[384,512]{1,0:T(8,128)(2,1)S(1)}, bf16[384,512]{1,0:T(8,128)(2,1)S(1)}, u32[]{:S(2)}, u32[]{:S(2)}) collective-permute-start(bf16[384,512]{1,0:T(8,128)(2,1)S(1)} %middle.1.v_ref), channel_id=1, source_target_pairs={{16,32},{32,16},{48,64},{64,48},{80,96},{96,80},{112,128},{128,112... | collective-permute-start | bytes 1179656 | tf_op jit(solution)/shard_map/ppermute | solution.py:279
  36.7 13.8 %collective-permute-start.9 = (bf16[384,512]{1,0:T(8,128)(2,1)S(1)}, bf16[384,512]{1,0:T(8,128)(2,1)S(1)}, u32[]{:S(2)}, u32[]{:S(2)}) collective-permute-start(bf16[384,512]{1,0:T(8,128)(2,1)S(1)} %middle.1.v_ref), channel_id=1, source_target_pairs={{0,16},{16,0},{32,48},{48,32},{64,80},{80,64},{96,112},{112,96},{1... | collective-permute-start | bytes 1179656 | tf_op jit(solution)/shard_map/ppermute | solution.py:279
  42.3 10.0 %collective-permute-start.10 = (bf16[384,512]{1,0:T(8,128)(2,1)S(1)}, bf16[384,512]{1,0:T(8,128)(2,1)S(1)}, u32[]{:S(2)}, u32[]{:S(2)}) collective-permute-start(bf16[384,512]{1,0:T(8,128)(2,1)S(1)} %middle.1.v_ref), channel_id=1, source_target_pairs={{1,2},{2,1},{3,4},{4,3},{5,6},{6,5},{7,8},{8,7},{9,10},{10,9},{11,... | collective-permute-start | bytes 1179656 | tf_op jit(solution)/shard_map/ppermute | solution.py:279
  46.9 5.4 %collective-permute-start.11 = (bf16[384,512]{1,0:T(8,128)(2,1)S(1)}, bf16[384,512]{1,0:T(8,128)(2,1)S(1)}, u32[]{:S(2)}, u32[]{:S(2)}) collective-permute-start(bf16[384,512]{1,0:T(8,128)(2,1)S(1)} %middle.1.v_ref), channel_id=1, source_target_pairs={{0,1},{1,0},{2,3},{3,2},{4,5},{5,4},{6,7},{7,6},{8,9},{9,8},{10,11... | collective-permute-start | bytes 1179656 | tf_op jit(solution)/shard_map/ppermute | solution.py:279
  54.2 3.6 %collective-permute-start.12 = (f32[544,128]{1,0:T(8,128)S(1)}, f32[544,128]{1,0:T(8,128)S(1)}, u32[]{:S(2)}, u32[]{:S(2)}) collective-permute-start(f32[544,128]{1,0:T(8,128)S(1)} %get-tuple-element.18), channel_id=1, source_target_pairs={{0,1},{1,0},{2,3},{3,2},{4,5},{5,4},{6,7},{7,6},{8,9},{9,8},{10,11... | collective-permute-start | bytes 835592 | tf_op jit(solution)/shard_map/ppermute | solution.py:289
  113.0 7.2 %collective-permute-start.13 = (f32[544,128]{1,0:T(8,128)S(1)}, f32[544,128]{1,0:T(8,128)S(1)}, u32[]{:S(2)}, u32[]{:S(2)}) collective-permute-start(f32[544,128]{1,0:T(8,128)S(1)} %bitcast.20), channel_id=1, source_target_pairs={{0,1},{1,0},{2,3},{3,2},{4,5},{5,4},{6,7},{7,6},{8,9},{9,8},{10,11... | collective-permute-start | bytes 835592 | tf_op jit(solution)/shard_map/ppermute | solution.py:289
